TPU v7x, 512 devices: a whole 4x8x8 slice. The times are simulated.
512 devices in a mesh: occ: 32 (over x, z), vir: 16 (over y, core).
Axes of the slice: x: 4, y: 8, z: 8, core: 2. Of those that a mesh axis runs over, the one named last changes fastest.
Arguments:
- pair_integrals: bfloat16 [25600, 1536], P(('vir', 'occ')), may hold values from -0.4375 to 0.4375
- amplitudes: bfloat16 [1536, 40000], P('vir', 'occ'), may hold values from -6 to 6
- vir_irrep: int32 [2, 80], replicated, may hold values from 0 to 7, never falling along the last dimension, each value on 1 to 20 neighbouring positions
- occ_irrep: int32 [200], replicated, may hold values from 0 to 7, never falling along the last dimension, each value on 1 to 50 neighbouring positions
- pair_irrep: int32 [1536], replicated, may hold values from 0 to 7, never falling along the last dimension, each value on 1 to 768 neighbouring positions
- vir_energy: float32 [160], replicated, may hold values from 0.2 to 2
- occ_energy: float32 [200], replicated, may hold values from -1.5 to -0.3
Outputs:
- update: bfloat16 [25600, 40000], P('vir', 'occ')
Inputs may be any that keep to these rules, and one draw needn't show every extreme that they name: `vir_irrep`: labels never fall along a slab; every label 0 to 7 occurs in each slab. `occ_irrep`: labels never fall; every label 0 to 7 occurs. `pair_irrep`: labels never fall; every label 0 to 7 occurs.
All inputs are finite; a program needn't handle non-finite values.
Results may differ from a plain program's by a relative error of at most 0.005.
Values may be sent and summed in bfloat16 or wider, within the bound.
No kernel may reach another device: no remote copies, remote signals or barrier semaphores. Data moves between devices by JAX's collectives and lax.ppermute only.
A program may use at most 128 MiB of HBM per device.

v0:
```python
import jax
import jax.numpy as jnp
from jax import lax
from jax.sharding import PartitionSpec as P


def lookup(indices, table):
    chosen = indices[:, None] == jnp.arange(table.shape[0], dtype=jnp.int32)[None, :]
    return jnp.sum(jnp.where(chosen, table[None, :], jnp.zeros((), table.dtype)), axis=1)


def on_device(pair_integrals, amplitudes, vir_irrep, occ_irrep, pair_irrep, vir_energy, occ_energy):
    vir_count = vir_energy.shape[0]
    occ_count = occ_energy.shape[0]
    local_vir = vir_count // lax.axis_size("vir")
    pair_local = amplitudes.shape[1]
    first_vir = lax.axis_index("vir") * local_vir
    labels_vir = vir_irrep.reshape(-1)
    own_labels = lax.dynamic_slice_in_dim(labels_vir, first_vir, local_vir)
    own_energy = lax.dynamic_slice_in_dim(vir_energy, first_vir, local_vir)
    label_ab = jnp.bitwise_xor(own_labels[:, None], labels_vir[None, :]).reshape(-1)
    energy_ab = (own_energy[:, None] + vir_energy[None, :]).reshape(-1)
    occ_pair = lax.axis_index("occ") * pair_local + jnp.arange(pair_local, dtype=jnp.int32)
    first_occ = occ_pair // occ_count
    second_occ = occ_pair % occ_count
    label_ij = jnp.bitwise_xor(lookup(first_occ, occ_irrep), lookup(second_occ, occ_irrep))
    energy_ij = lookup(first_occ, occ_energy) + lookup(second_occ, occ_energy)
    integral_rows = lax.all_gather(pair_integrals, "occ", axis=0, tiled=True)
    masked_rows = jnp.where(
        label_ab[:, None] == pair_irrep[None, :], integral_rows, jnp.zeros((), integral_rows.dtype)
    )
    keep_mask = label_ab[:, None] == label_ij[None, :]
    ladder_sums = jnp.dot(
        masked_rows,
        lax.all_gather(amplitudes, "vir", axis=0, tiled=True),
        preferred_element_type=jnp.float32,
    )
    ladder = jnp.where(keep_mask, ladder_sums, jnp.zeros((), jnp.float32)).astype(jnp.bfloat16)
    swapped = lax.all_to_all(
        ladder.reshape(local_vir, vir_count, pair_local),
        "vir",
        split_axis=1,
        concat_axis=0,
        tiled=True,
    )
    partner = swapped.transpose(1, 0, 2).reshape(-1, pair_local)
    denominator = energy_ij[None, :] - energy_ab[:, None]
    update = (ladder.astype(jnp.float32) - partner.astype(jnp.float32)) / denominator
    return update.astype(jnp.bfloat16)


def solution(mesh):
    in_specs = (P(("vir", "occ"), None), P("vir", "occ"), P(), P(), P(), P(), P())
    out_specs = P("vir", "occ")
    return jax.shard_map(
        on_device, mesh=mesh, in_specs=in_specs, out_specs=out_specs, check_vma=False
    )
```

profile of v0, /device:TPU:1, one launch (start us, length us, event | category | flops | bytes accessed | tf_op | source)
XLA Modules:
  0.0 375.1 jit_solution(8655366223599506729)
XLA Ops:
  6.5 0.0 copy-start.3
  6.5 0.0 all-gather.6.cloned.1.call-start
  6.5 0.7 all-gather.6.cloned.1.call-update
  7.3 0.0 all-gather.4.cloned.1.call-start
  7.3 0.7 all-gather.4.cloned.1.call-update
  8.0 0.8 reshape.74
  8.8 0.1 dynamic_slice.6
  8.9 0.1 broadcast_xor_fusion
  8.9 0.1 xor.30
  9.0 1.1 select_reduce_fusion.2
  10.1 96.1 %all-gather.6.cloned.1.call-done = bf16[32,50,1536]{2,1,0:T(8,128)(2,1)} async-done(((bf16[1,50,1536]{2,1,0:T(8,128)(2,1)}), bf16[32,50,1536]{2,1,0:T(8,128)(2,1)}) %all-gather.6.cloned.1.call-update) | async-done | bytes 4915216 | tf_op jit(solution)/shard_map/all_gather | solution.py:28
  106.2 7.6 %reshape.80 = bf16[1600,1536]{1,0:T(8,128)(2,1)} reshape(bf16[32,50,1536]{2,1,0:T(8,128)(2,1)} %all-gather.6.cloned.1.call-done) | data formatting | bytes 9830400
  113.8 38.0 %all-gather.4.cloned.1.call-done = bf16[1536,1250]{1,0:T(8,128)(2,1)} async-done(((bf16[96,1250]{1,0:T(8,128)(2,1)}), bf16[1536,1250]{1,0:T(8,128)(2,1)}) %all-gather.4.cloned.1.call-update) | async-done | bytes 3840016 | tf_op jit(solution)/shard_map/all_gather | solution.py:35
  151.8 0.0 copy-done.3
  151.8 10.0 %fusion.2 = bf16[1600,1250]{1,0:T(8,128)(2,1)S(1)} fusion(bf16[1536,1250]{1,0:T(8,128)(2,1)} %all-gather.4.cloned.1.call-done, bf16[1600,1536]{1,0:T(8,128)(2,1)} %reshape.80, s32[1536]{0:T(1024)S(1)} %copy-done.3, s32[1600]{0:T(1024)S(1)} %xor.30, s32[1250]{0:T(1024)S(1)} %xor.31), kind=kOutput, calls=%fused_computation.5 | convolution fusion | flops 6154914816 | bytes 12772744 | tf_op jit(solution)/shard_map/dot_general | solution.py:33
  161.8 0.0 copy-start
  161.9 2.0 copy-done
  163.8 5.2 %copy.16 = bf16[10,160,1250]{2,0,1:T(8,128)(2,1)} copy(bf16[10,160,1250]{2,1,0:T(8,128)(2,1)S(1)} %bitcast.15) | data formatting | bytes 8000000 | tf_op jit(solution)/shard_map/reshape | solution.py:40
  169.0 0.0 copy-start.1
  169.0 0.0 copy-start.2
  169.0 4.9 %all-to-all-start = ((bf16[10,160,1250]{2,0,1:T(8,128)(2,1)}), bf16[10,160,1250]{2,0,1:T(8,128)(2,1)}, u32[]{:S(2)}, u32[]{:S(2)}) async-start(bf16[10,160,1250]{2,0,1:T(8,128)(2,1)} %copy.16), calls=%async_computation | async-start | bytes 13107200 | tf_op jit(solution)/shard_map/all_to_all | solution.py:39
  173.9 0.0 copy-done.1
  173.9 0.1 dynamic_slice.7
  174.0 0.1 broadcast_add_fusion
  174.1 0.1 add.67
  174.1 0.0 copy-done.2
  174.1 0.4 select_reduce_fusion
  174.6 143.4 %all-to-all-done = bf16[10,160,1250]{2,0,1:T(8,128)(2,1)} async-done(((bf16[10,160,1250]{2,0,1:T(8,128)(2,1)}), bf16[10,160,1250]{2,0,1:T(8,128)(2,1)}, u32[]{:S(2)}, u32[]{:S(2)}) %all-to-all-start) | async-done | bytes 4000032 | tf_op jit(solution)/shard_map/all_to_all | solution.py:39
  318.0 7.3 %copy_convert_fusion = f32[10,160,1250]{2,1,0:T(8,128)} fusion(bf16[10,160,1250]{2,0,1:T(8,128)(2,1)} %all-to-all-done), kind=kLoop, calls=%fused_computation.8 | loop fusion | flops 2000000 | bytes 12000000 | tf_op jit(solution)/shard_map/convert_element_type | solution.py:48
  325.3 10.6 %reshape.78 = f32[10,16,10,1250]{3,2,1,0:T(8,128)} reshape(f32[10,160,1250]{2,1,0:T(8,128)} %copy_convert_fusion) | data formatting | bytes 16000000 | tf_op jit(solution)/shard_map/convert_element_type | solution.py:48
  335.9 14.5 %copy.18 = f32[16,10,10,1250]{3,1,0,2:T(8,128)} copy(f32[16,10,10,1250]{3,2,0,1:T(8,128)} %bitcast.14) | data formatting | bytes 16000000 | tf_op jit(solution)/shard_map/convert_element_type | solution.py:48
  350.4 11.1 %reshape.77 = f32[160,10,1250]{2,0,1:T(8,128)} reshape(f32[16,10,10,1250]{3,1,0,2:T(8,128)} %copy.18) | data formatting | bytes 16000000 | tf_op jit(solution)/shard_map/convert_element_type | solution.py:48
  361.5 6.8 %fusion.1 = bf16[1600,1250]{1,0:T(8,128)(2,1)} fusion(f32[160,10,1250]{2,0,1:T(8,128)} %reshape.77, bf16[1600,1250]{1,0:T(8,128)(2,1)} %copy-done, f32[1600]{0:T(1024)S(1)} %add.67, f32[1250]{0:T(1024)S(1)} %add.63), kind=kLoop, calls=%fused_computation.4 | loop fusion | flops 10000000 | bytes 16011400 | tf_op jit(solution)/shard_map/convert_element_type | solution.py:49
  (3 shorter events, 0.0 us)
Async XLA Ops:
  6.5 145.3 %copy-start.3 = (s32[1536]{0:T(1024)S(1)}, s32[1536]{0:T(1024)}, u32[]{:S(2)}) copy-start(s32[1536]{0:T(1024)} %param.11) | copy-start | bytes 18436
  6.5 99.7 %all-gather.6.cloned.1.call-start = ((), (), s32[]{:S(2)}) async-start(), calls=%async_computation.2 | async-start | bytes 5677056 | tf_op jit(solution)/shard_map/all_gather | solution.py:28
  7.3 144.5 %all-gather.4.cloned.1.call-start = ((), (), s32[]{:S(2)}) async-start(), calls=%async_computation.1 | async-start | bytes 4177920 | tf_op jit(solution)/shard_map/all_gather | solution.py:35
  161.8 2.0 copy-start
  169.0 4.9 %copy-start.1 = (f32[160]{0:T(256)S(1)}, f32[160]{0:T(256)}, u32[]{:S(2)}) copy-start(f32[160]{0:T(256)} %param.12) | copy-start | bytes 1924
  169.0 5.1 %copy-start.2 = (f32[200]{0:T(256)S(1)}, f32[200]{0:T(256)}, u32[]{:S(2)}) copy-start(f32[200]{0:T(256)} %param.13) | copy-start | bytes 2404
  169.0 149.0 %all-to-all-start = ((bf16[10,160,1250]{2,0,1:T(8,128)(2,1)}), bf16[10,160,1250]{2,0,1:T(8,128)(2,1)}, u32[]{:S(2)}, u32[]{:S(2)}) async-start(bf16[10,160,1250]{2,0,1:T(8,128)(2,1)} %copy.16), calls=%async_computation | async-start | bytes 13107200 | tf_op jit(solution)/shard_map/all_to_all | solution.py:39
Sparse Core Ops, SparseCore 0:
  10.5 95.6 all-gather.5
  108.4 43.3 all-gather.3
where the time goes:
time: 376 us; the launch traced here: 375 us
  waiting for transfers between devices  279 us (74%)
  local copies, waits for them, and re-layouts  52 us (14%)
  other arithmetic  15.7 us (4%)
  between operations  13.5 us (4%)
  matrix products  10 us (3%)
  starting transfers between devices  4.92 us (1%)
    all_to_all x1, waiting for transfers between devices, on_device(): lax.all_to_all(ladder.reshape(local_vir, vir_count, pair_local), 'vir', s...  143 us
    all_gather x1, waiting for transfers between devices, on_device(): integral_rows = lax.all_gather(pair_integrals, 'occ', axis=0, tiled=True)  96.1 us
    all_gather x1, waiting for transfers between devices, on_device(): lax.all_gather(amplitudes, 'vir', axis=0, tiled=True)  38 us
    convert_element_type x3, local copies, waits for them, and re-layouts, on_device(): partner.astype(jnp.float32)  36.2 us
    dot_general x1, matrix products, on_device(): jnp.dot(masked_rows, lax.all_gather(amplitudes, 'vir', axis=0, tiled=True...  10 us
    unnamed x9, local copies, waits for them, and re-layouts  9.56 us
  transfers between devices with their start and end apart: 3, of which 3 were waited for; matrix products, arithmetic and copies ran while one was open for 3% of the time, Pallas kernels for 0%

commit v1 on v0

v1 whole, which is shorter than its diff:
```python
import functools

import jax
import jax.numpy as jnp
import numpy as np
from jax import lax
from jax.experimental import pallas as pl
from jax.experimental.pallas import tpu as pltpu
from jax.sharding import PartitionSpec as P

SLAB = 80
NW = 160
NOCC = 200
CD = 1536
PAIRS = 1250
OWN = 10
ROWS = 50
CDS = 48
SLOTS = 384
LANES = 128
F32 = jnp.float32
BF16 = jnp.bfloat16
VMEM = pl.BlockSpec(memory_space=pltpu.VMEM)


def params():
    return pltpu.CompilerParams(vmem_limit_bytes=48 * 1024 * 1024)


def call(kernel, shapes, args):
    specs = jax.tree.map(lambda _: VMEM, shapes)
    return pl.pallas_call(
        kernel, out_shape=shapes, in_specs=[VMEM] * len(args), out_specs=specs, compiler_params=params()
    )(*args)


def dot(left, right, contract=((1,), (0,))):
    return lax.dot_general(left, right, (contract, ((), ())), preferred_element_type=F32)


def lookup(indices, table):
    chosen = indices[:, None] == jnp.arange(table.shape[0], dtype=jnp.int32)[None, :]
    return jnp.sum(jnp.where(chosen, table[None, :], jnp.zeros((), table.dtype)), axis=1)


def pack_columns(amp_ref, label_cd_ref, label_ij_ref, slot_ref, out_ref):
    keep = label_cd_ref[...] == label_ij_ref[...]
    masked = jnp.where(keep, amp_ref[...].astype(F32), 0.0).astype(BF16)
    rows = lax.broadcasted_iota(jnp.int32, (SLOTS, PAIRS), 0)
    place = jnp.where(rows == slot_ref[...], 1.0, 0.0).astype(BF16)
    out_ref[...] = dot(masked, place, ((1,), (1,))).astype(BF16)


def turn_rows(rows_ref, out_ref):
    row = lax.broadcasted_iota(jnp.int32, (ROWS, LANES), 0)
    lane = lax.broadcasted_iota(jnp.int32, (ROWS, LANES), 1)
    low = dot(rows_ref[...], jnp.where(lane == row, 1.0, 0.0).astype(BF16), ((0,), (0,)))
    high = dot(rows_ref[...], jnp.where(lane == row + 64, 1.0, 0.0).astype(BF16), ((0,), (0,)))
    half = CDS // 2
    for dest in range(CD // CDS):
        at = dest * CDS
        out_ref[dest] = (low[at : at + half] + high[at + half : at + CDS]).astype(BF16)


def by_partner(got_ref, out_ref):
    half = CDS // 2
    lane = lax.broadcasted_iota(jnp.int32, (half, LANES), 1)
    inside = [(lane >= OWN * a) & (lane < OWN * (a + 1)) for a in range(OWN)]
    for partner in range(16):
        halves = []
        for h in range(2):
            block = jnp.zeros((half, LANES), F32)
            for a in range(OWN):
                granule = a * 16 + partner
                source, piece = granule // 5, granule % 5
                shift = (OWN * a - 64 * h - OWN * piece) % LANES
                moved = got_ref[source].astype(F32)
                if shift:
                    moved = pltpu.roll(moved, shift, axis=1)
                block = jnp.where(inside[a], moved, block)
            halves.append(block)
        out_ref[partner] = jnp.concatenate(halves, axis=0).astype(BF16)


def difference(own_ref, mirror_ref, swap_ref, label_ab_ref, label_cd_ref, out_ref):
    label_cd = label_cd_ref[...]
    for slab in range(2):
        for odd in range(2):
            packed = jnp.zeros((CDS, LANES), F32)
            for quarter in range(4):
                partner = 8 * slab + 2 * quarter + odd
                mirrored = dot(mirror_ref[partner], swap_ref[...])
                diff = own_ref[partner].astype(F32) - mirrored
                keep = label_ab_ref[partner : partner + 1, :] == label_cd
                packed = jnp.where(keep, diff, packed)
            packed = packed.astype(BF16)
            for copy in range(8):
                out_ref[copy, 2 * slab + odd] = packed


def turn_back(got_ref, place_ref, out_ref):
    total = jnp.zeros((400, 384), F32)
    for part in range(4):
        block = got_ref[:, part].reshape(384, LANES)
        total = total + dot(place_ref[part], block, ((1,), (1,)))
    for a in range(OWN):
        rows = total[40 * a : 40 * a + 40].astype(BF16)
        for copy in range(4):
            out_ref[copy, a] = rows


def finish(packed_ref, amp_ref, spread_ref, label_ab_ref, label_cd_ref, energy_ab_ref, label_ij_ref, energy_ij_ref,
           slot_ref, out_ref, place_ref):
    @pl.when(pl.program_id(0) == 0)
    def _():
        rows = lax.broadcasted_iota(jnp.int32, (SLOTS, PAIRS), 0)
        place_ref[...] = jnp.where(rows == slot_ref[...], 1.0, 0.0).astype(BF16)

    label_ab = label_ab_ref[0]
    total = jnp.zeros((NW, SLOTS), F32)
    for part in range(4):
        at = 384 * part
        spread = dot(spread_ref[...], packed_ref[part, 0])
        keep = label_ab == label_cd_ref[:, at : at + 384]
        masked = jnp.where(keep, spread, 0.0).astype(BF16)
        total = total + dot(masked, amp_ref[at : at + 384, :])
    ladder = dot(total.astype(BF16), place_ref[...])
    update = ladder / (energy_ij_ref[...] - energy_ab_ref[0])
    out_ref[...] = jnp.where(label_ab == label_ij_ref[...], update, 0.0).astype(BF16)


def swap_table():
    table = np.zeros((LANES, LANES), np.float32)
    for a in range(OWN):
        for b in range(OWN):
            table[b * OWN + a, a * OWN + b] = 1.0
    return table


def place_table():
    table = np.zeros((4, 400, LANES), np.float32)
    for a in range(OWN):
        for part in range(4):
            for b in range(OWN):
                table[part, a * 40 + part * OWN + b, a * OWN + b] = 1.0
    return table


def spread_table():
    table = np.zeros((NW, 40), np.float32)
    for b in range(NW):
        slab, within = b // SLAB, b % SLAB
        table[b, slab * 20 + within % 20] = 1.0
    return table


def on_device(pair_integrals, amplitudes, vir_irrep, occ_irrep, pair_irrep, vir_energy, occ_energy):
    occ = lax.axis_index("occ")
    vir = lax.axis_index("vir")
    z_groups = [[8 * x + z for z in range(8)] for x in range(4)]
    x_groups = [[8 * x + z for x in range(4)] for z in range(8)]

    labels_vir = vir_irrep.reshape(-1)
    own_labels = lax.dynamic_slice_in_dim(labels_vir, vir * OWN, OWN)
    own_energy = lax.dynamic_slice_in_dim(vir_energy, vir * OWN, OWN)
    label_ab = jnp.bitwise_xor(own_labels[:, None], labels_vir[None, :])
    energy_ab = own_energy[:, None] + vir_energy[None, :]
    occ_pair = occ * PAIRS + jnp.arange(PAIRS, dtype=jnp.int32)
    first_occ = occ_pair // NOCC
    second_occ = occ_pair % NOCC
    label_ij = jnp.bitwise_xor(lookup(first_occ, occ_irrep), lookup(second_occ, occ_irrep))[None, :]
    energy_ij = (lookup(first_occ, occ_energy) + lookup(second_occ, occ_energy))[None, :]
    slot = ((first_occ - (occ * PAIRS) // NOCC) * 50 + second_occ % 50)[None, :]

    label_rows = lax.dynamic_slice_in_dim(pair_irrep, vir * 96, 96)[:, None]
    packed_amp = call(
        pack_columns, jax.ShapeDtypeStruct((96, SLOTS), BF16), (amplitudes, label_rows, label_ij, slot)
    )
    all_amp = lax.all_gather(packed_amp, "vir", axis=0, tiled=True)

    turned = call(turn_rows, jax.ShapeDtypeStruct((32, CDS // 2, LANES), BF16), (pair_integrals,))
    slices = lax.all_to_all(turned, "occ", split_axis=0, concat_axis=0, tiled=True)
    blocks = call(by_partner, jax.ShapeDtypeStruct((16, CDS, LANES), BF16), (slices,))
    mirror = lax.all_to_all(blocks, "vir", split_axis=0, concat_axis=0, tiled=True)
    block_labels = label_ab.reshape(OWN, 16, OWN).transpose(1, 0, 2).reshape(16, OWN * OWN)
    block_labels = jnp.pad(block_labels, ((0, 0), (0, LANES - OWN * OWN)), constant_values=-1)
    label_cds = lax.dynamic_slice_in_dim(pair_irrep, occ * CDS, CDS)[:, None]
    copies = call(
        difference,
        jax.ShapeDtypeStruct((8, 4, CDS, LANES), BF16),
        (blocks, mirror, jnp.asarray(swap_table(), BF16), block_labels, label_cds),
    )
    line = lax.all_to_all(copies, "occ", split_axis=0, concat_axis=0, tiled=True, axis_index_groups=z_groups)
    rows = call(
        turn_back, jax.ShapeDtypeStruct((4, OWN, 40, 384), BF16), (line, jnp.asarray(place_table(), BF16))
    )
    packed = lax.all_to_all(rows, "occ", split_axis=0, concat_axis=0, tiled=True, axis_index_groups=x_groups)

    whole = lambda *shape: pl.BlockSpec(shape, lambda i: (0,) * len(shape))
    return pl.pallas_call(
        finish,
        grid=(OWN,),
        out_shape=jax.ShapeDtypeStruct((OWN * NW, PAIRS), BF16),
        in_specs=[
            pl.BlockSpec((4, 1, 40, 384), lambda i: (0, i, 0, 0)),
            whole(CD, SLOTS),
            whole(NW, 40),
            pl.BlockSpec((1, NW, 1), lambda i: (i, 0, 0)),
            whole(1, CD),
            pl.BlockSpec((1, NW, 1), lambda i: (i, 0, 0)),
            whole(1, PAIRS),
            whole(1, PAIRS),
            whole(1, PAIRS),
        ],
        out_specs=pl.BlockSpec((NW, PAIRS), lambda i: (i, 0)),
        scratch_shapes=[pltpu.VMEM((SLOTS, PAIRS), BF16)],
        compiler_params=params(),
    )(
        packed,
        all_amp,
        jnp.asarray(spread_table(), BF16),
        label_ab[:, :, None],
        pair_irrep[None, :],
        energy_ab[:, :, None],
        label_ij,
        energy_ij,
        slot,
    )


def solution(mesh):
    in_specs = (P(("vir", "occ"), None), P("vir", "occ"), P(), P(), P(), P(), P())
    out_specs = P("vir", "occ")
    return jax.shard_map(
        on_device, mesh=mesh, in_specs=in_specs, out_specs=out_specs, check_vma=False
    )
```

time: 376 us -> 116 us (0.31)
  waiting for transfers between devices: 279 us -> 30.3 us
  local copies, waits for them, and re-layouts: 52 us -> 4.87 us
  starting transfers between devices: 4.92 us -> 27.6 us
  Pallas kernels: 0 us -> 20.2 us
  blocking collectives: 0 us -> 16.5 us
  other arithmetic: 15.7 us -> 1.89 us
  matrix products: 10 us -> 0 us
    all_gather x2 -> x1, waiting for transfers between devices: 134 us -> 0.02 us  [on_device(): all_amp = lax.all_gather(packed_amp, 'vir', axis=0, tiled=True)]
    all_to_all x1 -> x3, waiting for transfers between devices: 143 us -> 30.3 us  [the longest x1 14.4 us: on_device(): lax.all_to_all(rows, 'occ', split_axis=0, concat_axis=0, tiled=True, axis...]
    convert_element_type x3 -> x0, local copies, waits for them, and re-layouts: 36.2 us -> none  [on_device(): partner.astype(jnp.float32)]
    all_to_all x1 -> x3, starting transfers between devices: 4.87 us -> 27.6 us  [the longest x1 13.7 us: on_device(): lax.all_to_all(turned, 'occ', split_axis=0, concat_axis=0, tiled=True)]
    pallas_call x0 -> x6, Pallas kernels: none -> 20.2 us  [the longest x1 14 us: on_device(): pl.pallas_call(finish, grid=(OWN,), out_shape=jax.ShapeDtypeStruct((OWN *...]
    all_to_all x0 -> x1, blocking collectives: none -> 16.5 us  [on_device(): lax.all_to_all(copies, 'occ', split_axis=0, concat_axis=0, tiled=True, ax...]
    convert_element_type x2 -> x0, other arithmetic: 14.1 us -> none  [the longest x1 7.3 us: on_device(): partner.astype(jnp.float32)]
    dot_general x1 -> x0, matrix products: 10 us -> none  [on_device(): jnp.dot(masked_rows, lax.all_gather(amplitudes, 'vir', axis=0, tiled=True...]
  transfers between devices with their start and end apart: 3 -> 4, of which waited for: 3 -> 3; matrix products, arithmetic and copies ran while one was open for 3% -> 3% of each run, Pallas kernels for 0% -> 4%
where the time goes in v1:
time: 116 us; the launch traced here: 115 us
  waiting for transfers between devices  30.3 us (26%)
  starting transfers between devices  27.6 us (24%)
  Pallas kernels  20.2 us (17%)
  blocking collectives  16.5 us (14%)
  between operations  13.6 us (12%)
  local copies, waits for them, and re-layouts  4.87 us (4%)
  other arithmetic  1.89 us (2%)
    all_to_all x1, blocking collectives, on_device(): lax.all_to_all(copies, 'occ', split_axis=0, concat_axis=0, tiled=True, ax...  16.5 us
    all_to_all x1, waiting for transfers between devices, on_device(): lax.all_to_all(rows, 'occ', split_axis=0, concat_axis=0, tiled=True, axis...  14.4 us
    pallas_call x1, Pallas kernels, on_device(): pl.pallas_call(finish, grid=(OWN,), out_shape=jax.ShapeDtypeStruct((OWN *...  14 us
    all_to_all x1, starting transfers between devices, on_device(): lax.all_to_all(turned, 'occ', split_axis=0, concat_axis=0, tiled=True)  13.7 us
    all_to_all x1, waiting for transfers between devices, on_device(): lax.all_to_all(blocks, 'vir', split_axis=0, concat_axis=0, tiled=True)  10.7 us
    all_to_all x1, starting transfers between devices, on_device(): lax.all_to_all(blocks, 'vir', split_axis=0, concat_axis=0, tiled=True)  10.1 us
    pallas_call x5, Pallas kernels, call(): pl.pallas_call(kernel, out_shape=shapes, in_specs=[VMEM] * len(args), out...  6.22 us
    all_to_all x1, waiting for transfers between devices, on_device(): lax.all_to_all(turned, 'occ', split_axis=0, concat_axis=0, tiled=True)  5.15 us
  transfers between devices with their start and end apart: 4, of which 3 were waited for; matrix products, arithmetic and copies ran while one was open for 3% of the time, Pallas kernels for 4%

profile of v1, /device:TPU:1, one launch (start us, length us, event | category | flops | bytes accessed | tf_op | source)
XLA Modules:
  0.0 115.1 jit_solution(16292853683501155994)
XLA Ops:
  6.5 0.0 copy-start.3
  6.5 0.9 copy-done.3
  7.5 0.0 copy-start.7
  7.5 0.0 copy-start.6
  7.5 0.0 copy-start.5
  7.5 1.1 shard_map.100
  8.5 13.7 %all-to-all-start = ((bf16[32,24,128]{2,1,0:T(8,128)(2,1)}), bf16[32,24,128]{2,1,0:T(8,128)(2,1)S(1)}, u32[]{:S(2)}, u32[]{:S(2)}) async-start(bf16[32,24,128]{2,1,0:T(8,128)(2,1)} %shard_map.100), calls=%async_computation | async-start | bytes 393216 | tf_op jit(solution)/shard_map/all_to_all | solution.py:182
  22.3 0.0 all-gather.2.cloned.1.call-start
  22.4 1.1 select_reduce_fusion.2
  23.5 0.8 dynamic-slice_bitcast_fusion
  24.3 0.1 copy.20.label_cd_ref
  24.4 0.1 fusion.5.slot_ref
  24.4 0.0 copy-start.2
  24.5 0.9 copy-done.2
  25.4 1.1 shard_map.104
  26.5 0.0 all-gather.2.cloned.1.call-update
  26.5 5.2 %all-to-all-done.got_ref = bf16[32,24,128]{2,1,0:T(8,128)(2,1)S(1)} async-done(((bf16[32,24,128]{2,1,0:T(8,128)(2,1)}), bf16[32,24,128]{2,1,0:T(8,128)(2,1)S(1)}, u32[]{:S(2)}, u32[]{:S(2)}) %all-to-all-start) | async-done | bytes 196640 | tf_op jit(solution)/shard_map/all_to_all | solution.py:182
  31.7 1.2 %shard_map.101.own_ref = bf16[16,48,128]{2,1,0:T(8,128)(2,1)} custom-call(bf16[32,24,128]{2,1,0:T(8,128)(2,1)S(1)} %all-to-all-done.got_ref), custom_call_target="tpu_custom_call" | custom-call | tf_op jit(solution)/shard_map/pallas_call | solution.py:32
  32.9 0.0 copy-start.1
  32.9 10.1 %all-to-all-start.1 = ((bf16[16,48,128]{2,1,0:T(8,128)(2,1)}), bf16[16,48,128]{2,1,0:T(8,128)(2,1)S(1)}, u32[]{:S(2)}, u32[]{:S(2)}) async-start(bf16[16,48,128]{2,1,0:T(8,128)(2,1)} %shard_map.101.own_ref), calls=%async_computation.1 | async-start | bytes 393216 | tf_op jit(solution)/shard_map/all_to_all | solution.py:184
  43.0 0.0 copy-done.7
  43.0 0.1 reshape.227
  43.1 0.1 xor.53
  43.2 0.1 dynamic_slice.12
  43.2 0.1 xor.50
  43.3 0.1 xor.51
  43.4 0.1 copy.17
  43.5 0.0 copy-done.6
  43.5 0.1 dynamic-slice_bitcast_fusion.1
  43.6 0.1 copy.19.label_cd_ref
  43.7 0.1 copy.18
  43.8 10.7 %all-to-all-done.1.mirror_ref = bf16[16,48,128]{2,1,0:T(8,128)(2,1)S(1)} async-done(((bf16[16,48,128]{2,1,0:T(8,128)(2,1)}), bf16[16,48,128]{2,1,0:T(8,128)(2,1)S(1)}, u32[]{:S(2)}, u32[]{:S(2)}) %all-to-all-start.1) | async-done | bytes 196640 | tf_op jit(solution)/shard_map/all_to_all | solution.py:184
  54.5 0.0 copy-done.5
  54.5 1.2 %shard_map.102 = bf16[8,4,48,128]{3,2,1,0:T(8,128)(2,1)S(1)} custom-call(bf16[16,48,128]{2,1,0:T(8,128)(2,1)} %shard_map.101.own_ref, bf16[16,48,128]{2,1,0:T(8,128)(2,1)S(1)} %all-to-all-done.1.mirror_ref, bf16[128,128]{1,0:T(8,128)(2,1)S(1)} %copy-done.5, s32[16,128]{1,0:T(8,128)S(1)} %pad.4.label_ab_ref, s32[48,1]{1,0:T(8,128)S(1)} %copy.19.label_cd_ref), custom_call_target="tpu_custom_call" | custom-call | tf_op jit(solution)/shard_map/pallas_call | solution.py:32
  55.7 16.5 %all_to_all.20.got_ref = bf16[8,4,48,128]{3,2,1,0:T(8,128)(2,1)S(1)} all-to-all(bf16[8,4,48,128]{3,2,1,0:T(8,128)(2,1)S(1)} %shard_map.102), channel_id=1, replica_groups={{0,16,32,48,64,80,96,112},{128,144,160,176,192,208,224,240},{256,272,28..., dimensions={0} | all-to-all | bytes 786432 | tf_op jit(solution)/shard_map/all_to_all | solution.py:193
  72.3 0.0 copy-done.1
  72.3 1.6 %shard_map.103 = bf16[4,10,40,384]{3,2,1,0:T(8,128)(2,1)} custom-call(bf16[8,4,48,128]{3,2,1,0:T(8,128)(2,1)S(1)} %all_to_all.20.got_ref, bf16[4,400,128]{2,1,0:T(8,128)(2,1)S(1)} %copy-done.1), custom_call_target="tpu_custom_call" | custom-call | tf_op jit(solution)/shard_map/pallas_call | solution.py:32
  73.9 0.0 copy-start.8
  73.9 0.0 copy-start.9
  73.9 3.8 %all-to-all-start.3 = ((bf16[4,10,40,384]{3,2,1,0:T(8,128)(2,1)}), bf16[4,10,40,384]{3,2,1,0:T(8,128)(2,1)S(1)}, u32[]{:S(2)}, u32[]{:S(2)}) async-start(bf16[4,10,40,384]{3,2,1,0:T(8,128)(2,1)} %shard_map.103), calls=%async_computation.3 | async-start | bytes 2457600 | tf_op jit(solution)/shard_map/all_to_all | solution.py:197
  77.7 0.0 copy-start.4
  77.7 0.0 copy-done.8
  77.7 0.1 dynamic_slice.15
  77.8 0.0 copy-done.9
  77.8 0.4 select_reduce_fusion
  78.2 0.1 broadcast_xor_fusion.label_ab_ref
  78.4 0.1 broadcast_add_fusion.energy_ab_ref
  78.5 0.0 all-gather.2.cloned.1.call-done.amp_ref
  78.6 14.4 %all-to-all-done.3.packed_ref = bf16[4,10,40,384]{3,2,1,0:T(8,128)(2,1)S(1)} async-done(((bf16[4,10,40,384]{3,2,1,0:T(8,128)(2,1)}), bf16[4,10,40,384]{3,2,1,0:T(8,128)(2,1)S(1)}, u32[]{:S(2)}, u32[]{:S(2)}) %all-to-all-start.3) | async-done | bytes 1228832 | tf_op jit(solution)/shard_map/all_to_all | solution.py:197
  93.0 0.0 copy-done.4
  93.0 0.0 copy-start
  93.0 1.3 %copy-done = bf16[1536,384]{1,0:T(8,128)(2,1)S(1)} copy-done((bf16[1536,384]{1,0:T(8,128)(2,1)S(1)}, bf16[1536,384]{1,0:T(8,128)(2,1)}, u32[]{:S(2)}) %copy-start) | copy-done | bytes 1179672
  94.3 14.0 %shard_map.105 = bf16[1600,1250]{1,0:T(8,128)(2,1)} custom-call(bf16[4,10,40,384]{3,2,1,0:T(8,128)(2,1)S(1)} %all-to-all-done.3.packed_ref, bf16[1536,384]{1,0:T(8,128)(2,1)S(1)} %copy-done, bf16[160,40]{1,0:T(8,128)(2,1)S(1)} %copy-done.4, s32[10,160,1]{2,1,0:T(8,128)S(1)} %broadcast_xor_fusion.label_ab_ref, s32[1,1536]{1,0:T(1,128)S(1)} %broadcast_in_dim.65.label_cd_ref, ...), custom_call_target="tpu_custom_call" | custom-call | tf_op jit(solution)/shard_map/pallas_call | solution.py:200
  (10 shorter events, 0.1 us)
Async XLA Ops:
  6.5 0.9 copy-start.3
  7.5 35.5 %copy-start.7 = (s32[2,80]{1,0:T(2,128)S(1)}, s32[2,80]{1,0:T(2,128)}, u32[]{:S(2)}) copy-start(s32[2,80]{1,0:T(2,128)} %param.12) | copy-start | bytes 1924
  7.5 36.0 %copy-start.6 = (s32[1536]{0:T(1024)S(1)}, s32[1536]{0:T(1024)}, u32[]{:S(2)}) copy-start(s32[1536]{0:T(1024)} %param.14) | copy-start | bytes 18436
  7.5 47.0 %copy-start.5 = (bf16[128,128]{1,0:T(8,128)(2,1)S(1)}, bf16[128,128]{1,0:T(8,128)(2,1)}, u32[]{:S(2)}) copy-start(bf16[128,128]{1,0:T(8,128)(2,1)} %constant.65.clone.swap_ref) | copy-start | bytes 98308
  8.5 23.1 %all-to-all-start = ((bf16[32,24,128]{2,1,0:T(8,128)(2,1)}), bf16[32,24,128]{2,1,0:T(8,128)(2,1)S(1)}, u32[]{:S(2)}, u32[]{:S(2)}) async-start(bf16[32,24,128]{2,1,0:T(8,128)(2,1)} %shard_map.100), calls=%async_computation | async-start | bytes 393216 | tf_op jit(solution)/shard_map/all_to_all | solution.py:182
  22.3 56.3 %all-gather.2.cloned.1.call-start = ((), (), s32[]{:S(2)}) async-start(), calls=%async_computation.4 | async-start | bytes 1253376 | tf_op jit(solution)/shard_map/all_gather | solution.py:179
  24.4 0.9 copy-start.2
  32.9 39.4 %copy-start.1 = (bf16[4,400,128]{2,1,0:T(8,128)(2,1)S(1)}, bf16[4,400,128]{2,1,0:T(8,128)(2,1)}, u32[]{:S(2)}) copy-start(bf16[4,400,128]{2,1,0:T(8,128)(2,1)} %constant.66.clone.place_ref) | copy-start | bytes 1228804
  32.9 21.6 %all-to-all-start.1 = ((bf16[16,48,128]{2,1,0:T(8,128)(2,1)}), bf16[16,48,128]{2,1,0:T(8,128)(2,1)S(1)}, u32[]{:S(2)}, u32[]{:S(2)}) async-start(bf16[16,48,128]{2,1,0:T(8,128)(2,1)} %shard_map.101.own_ref), calls=%async_computation.1 | async-start | bytes 393216 | tf_op jit(solution)/shard_map/all_to_all | solution.py:184
  73.9 3.8 %copy-start.8 = (f32[160]{0:T(256)S(1)}, f32[160]{0:T(256)}, u32[]{:S(2)}) copy-start(f32[160]{0:T(256)} %param.15) | copy-start | bytes 1924
  73.9 3.9 %copy-start.9 = (f32[200]{0:T(256)S(1)}, f32[200]{0:T(256)}, u32[]{:S(2)}) copy-start(f32[200]{0:T(256)} %param.16) | copy-start | bytes 2404
  73.9 19.1 %all-to-all-start.3 = ((bf16[4,10,40,384]{3,2,1,0:T(8,128)(2,1)}), bf16[4,10,40,384]{3,2,1,0:T(8,128)(2,1)S(1)}, u32[]{:S(2)}, u32[]{:S(2)}) async-start(bf16[4,10,40,384]{3,2,1,0:T(8,128)(2,1)} %shard_map.103), calls=%async_computation.3 | async-start | bytes 2457600 | tf_op jit(solution)/shard_map/all_to_all | solution.py:197
  77.7 15.3 %copy-start.4 = (bf16[160,40]{1,0:T(8,128)(2,1)S(1)}, bf16[160,40]{1,0:T(8,128)(2,1)}, u32[]{:S(2)}) copy-start(bf16[160,40]{1,0:T(8,128)(2,1)} %constant.67.clone.spread_ref) | copy-start | bytes 38404
  93.0 1.3 %copy-start = (bf16[1536,384]{1,0:T(8,128)(2,1)S(1)}, bf16[1536,384]{1,0:T(8,128)(2,1)}, u32[]{:S(2)}) copy-start(bf16[1536,384]{1,0:T(8,128)(2,1)} %all-gather.2.cloned.1.call-done.amp_ref) | copy-start | bytes 3538948
Sparse Core Ops, SparseCore 0:
  26.6 43.1 all-gather.1

commit v2 on v1

--- a/solution.py
+++ b/solution.py
@@ -1,5 +1,3 @@
-import functools
-
 import jax
 import jax.numpy as jnp
 import numpy as np
@@ -18,6 +16,8 @@
 CDS = 48
 SLOTS = 384
 LANES = 128
+STEP = 5
+CHIPS = (0, 3, 5, 1, 4, 6, 7, 2)
 F32 = jnp.float32
 BF16 = jnp.bfloat16
 VMEM = pl.BlockSpec(memory_space=pltpu.VMEM)
@@ -48,7 +48,7 @@
     masked = jnp.where(keep, amp_ref[...].astype(F32), 0.0).astype(BF16)
     rows = lax.broadcasted_iota(jnp.int32, (SLOTS, PAIRS), 0)
     place = jnp.where(rows == slot_ref[...], 1.0, 0.0).astype(BF16)
-    out_ref[...] = dot(masked, place, ((1,), (1,))).astype(BF16)
+    out_ref[0] = dot(masked, place, ((1,), (1,))).astype(BF16)
 
 
 def turn_rows(rows_ref, out_ref):
@@ -109,24 +109,39 @@
             out_ref[copy, a] = rows
 
 
-def finish(packed_ref, amp_ref, spread_ref, label_ab_ref, label_cd_ref, energy_ab_ref, label_ij_ref, energy_ij_ref,
-           slot_ref, out_ref, place_ref):
-    @pl.when(pl.program_id(0) == 0)
+def finish(packed_ref, three_ref, five_ref, core_three_ref, core_five_ref, pick_ref, vir_ref, own_label_ref, own_energy_ref, label_b_ref,
+           spread_label_b_ref, energy_b_ref, label_cd_ref, label_ij_ref, energy_ij_ref, slot_ref, out_ref,
+           amp_ref, place_ref, left_ref):
+    step = pl.program_id(0)
+
+    @pl.when(step == 0)
     def _():
         rows = lax.broadcasted_iota(jnp.int32, (SLOTS, PAIRS), 0)
         place_ref[...] = jnp.where(rows == slot_ref[...], 1.0, 0.0).astype(BF16)
-
-    label_ab = label_ab_ref[0]
-    total = jnp.zeros((NW, SLOTS), F32)
-    for part in range(4):
-        at = 384 * part
-        spread = dot(spread_ref[...], packed_ref[part, 0])
-        keep = label_ab == label_cd_ref[:, at : at + 384]
-        masked = jnp.where(keep, spread, 0.0).astype(BF16)
-        total = total + dot(masked, amp_ref[at : at + 384, :])
-    ladder = dot(total.astype(BF16), place_ref[...])
-    update = ladder / (energy_ij_ref[...] - energy_ab_ref[0])
-    out_ref[...] = jnp.where(label_ab == label_ij_ref[...], update, 0.0).astype(BF16)
+        for part, core, first in ((three_ref, 0, 0), (five_ref, 0, 3), (core_three_ref, 1, 0), (core_five_ref, 1, 3)):
+            for index in range(part.shape[0]):
+                source = ((vir_ref[0] ^ core) + 2 * CHIPS[first + index]) & 15
+                amp_ref[pl.ds(pl.multiple_of(96 * source, 96), 96), :] = part[index]
+
+    for a in range(STEP):
+        label_a = own_label_ref[step * STEP + a]
+        for part in range(4):
+            wanted = label_cd_ref[:, 384 * part : 384 * part + 384] ^ label_a
+            values = packed_ref[part, a].astype(F32)
+            values = jnp.concatenate([values, jnp.zeros((8, 384), F32)], axis=0)
+            for quarter in range(4):
+                keep = spread_label_b_ref[48 * quarter : 48 * quarter + 48, :] == wanted
+                at = 192 * a + 48 * quarter
+                left_ref[at : at + 48, 384 * part : 384 * part + 384] = jnp.where(keep, values, 0.0).astype(BF16)
+    total = dot(left_ref[...], amp_ref[...]).astype(BF16)
+    for a in range(STEP):
+        picked = dot(pick_ref[...], total[192 * a : 192 * a + 192]).astype(BF16)
+        ladder = dot(picked, place_ref[...])
+        label_a = own_label_ref[step * STEP + a]
+        energy_a = own_energy_ref[step * STEP + a]
+        update = ladder / ((energy_ij_ref[...] - energy_a) - energy_b_ref[...])
+        keep = label_b_ref[...] == (label_ij_ref[...] ^ label_a)
+        out_ref[NW * a : NW * a + NW, :] = jnp.where(keep, update, 0.0).astype(BF16)
 
 
 def swap_table():
@@ -146,11 +161,11 @@
     return table
 
 
-def spread_table():
-    table = np.zeros((NW, 40), np.float32)
+def pick_table():
+    table = np.zeros((NW, 192), np.float32)
     for b in range(NW):
         slab, within = b // SLAB, b % SLAB
-        table[b, slab * 20 + within % 20] = 1.0
+        table[b, 48 * (within // 20) + 20 * slab + within % 20] = 1.0
     return table
 
 
@@ -164,7 +179,6 @@
     own_labels = lax.dynamic_slice_in_dim(labels_vir, vir * OWN, OWN)
     own_energy = lax.dynamic_slice_in_dim(vir_energy, vir * OWN, OWN)
     label_ab = jnp.bitwise_xor(own_labels[:, None], labels_vir[None, :])
-    energy_ab = own_energy[:, None] + vir_energy[None, :]
     occ_pair = occ * PAIRS + jnp.arange(PAIRS, dtype=jnp.int32)
     first_occ = occ_pair // NOCC
     second_occ = occ_pair % NOCC
@@ -174,9 +188,10 @@
 
     label_rows = lax.dynamic_slice_in_dim(pair_irrep, vir * 96, 96)[:, None]
     packed_amp = call(
-        pack_columns, jax.ShapeDtypeStruct((96, SLOTS), BF16), (amplitudes, label_rows, label_ij, slot)
-    )
-    all_amp = lax.all_gather(packed_amp, "vir", axis=0, tiled=True)
+        pack_columns, jax.ShapeDtypeStruct((1, 96, SLOTS), BF16), (amplitudes, label_rows, label_ij, slot)
+    )
+
+    from_chip = lambda array, k: lax.ppermute(array, "vir", [(i, (i - 2 * k) % 16) for i in range(16)])
 
     turned = call(turn_rows, jax.ShapeDtypeStruct((32, CDS // 2, LANES), BF16), (pair_integrals,))
     slices = lax.all_to_all(turned, "occ", split_axis=0, concat_axis=0, tiled=True)
@@ -190,38 +205,63 @@
         jax.ShapeDtypeStruct((8, 4, CDS, LANES), BF16),
         (blocks, mirror, jnp.asarray(swap_table(), BF16), block_labels, label_cds),
     )
+    copies, packed_amp = lax.optimization_barrier((copies, packed_amp))
+    amp_three = jnp.concatenate([packed_amp, from_chip(packed_amp, 3), from_chip(packed_amp, 5)], axis=0)
     line = lax.all_to_all(copies, "occ", split_axis=0, concat_axis=0, tiled=True, axis_index_groups=z_groups)
     rows = call(
         turn_back, jax.ShapeDtypeStruct((4, OWN, 40, 384), BF16), (line, jnp.asarray(place_table(), BF16))
     )
+    rows, amp_three = lax.optimization_barrier((rows, amp_three))
+    from_core = lambda array: lax.ppermute(array, "vir", [(i, i ^ 1) for i in range(16)])
+    amp_five = jnp.concatenate([from_chip(amp_three, 1), from_chip(amp_three[:2], 7)], axis=0)
+    amp_parts = (amp_three, amp_five, from_core(amp_three), from_core(amp_five))
     packed = lax.all_to_all(rows, "occ", split_axis=0, concat_axis=0, tiled=True, axis_index_groups=x_groups)
 
+    spread_labels = jnp.pad(
+        labels_vir.reshape(2, 4, 20).transpose(1, 0, 2).reshape(4, 40), ((0, 0), (0, 8)), constant_values=-1
+    ).reshape(192, 1)
     whole = lambda *shape: pl.BlockSpec(shape, lambda i: (0,) * len(shape))
+    scalars = pl.BlockSpec(memory_space=pltpu.SMEM)
     return pl.pallas_call(
         finish,
-        grid=(OWN,),
+        grid=(OWN // STEP,),
         out_shape=jax.ShapeDtypeStruct((OWN * NW, PAIRS), BF16),
         in_specs=[
-            pl.BlockSpec((4, 1, 40, 384), lambda i: (0, i, 0, 0)),
-            whole(CD, SLOTS),
-            whole(NW, 40),
-            pl.BlockSpec((1, NW, 1), lambda i: (i, 0, 0)),
+            pl.BlockSpec((4, STEP, 40, 384), lambda i: (0, i, 0, 0)),
+            whole(3, 96, SLOTS),
+            whole(5, 96, SLOTS),
+            whole(3, 96, SLOTS),
+            whole(5, 96, SLOTS),
+            whole(NW, 192),
+            scalars,
+            scalars,
+            scalars,
+            whole(NW, 1),
+            whole(192, 1),
+            whole(NW, 1),
             whole(1, CD),
-            pl.BlockSpec((1, NW, 1), lambda i: (i, 0, 0)),
             whole(1, PAIRS),
             whole(1, PAIRS),
             whole(1, PAIRS),
         ],
-        out_specs=pl.BlockSpec((NW, PAIRS), lambda i: (i, 0)),
-        scratch_shapes=[pltpu.VMEM((SLOTS, PAIRS), BF16)],
+        out_specs=pl.BlockSpec((STEP * NW, PAIRS), lambda i: (i, 0)),
+        scratch_shapes=[
+            pltpu.VMEM((CD, SLOTS), BF16),
+            pltpu.VMEM((SLOTS, PAIRS), BF16),
+            pltpu.VMEM((STEP * 192, CD), BF16),
+        ],
         compiler_params=params(),
     )(
         packed,
-        all_amp,
-        jnp.asarray(spread_table(), BF16),
-        label_ab[:, :, None],
+        *amp_parts,
+        jnp.asarray(pick_table(), BF16),
+        vir.reshape(1),
+        own_labels,
+        own_energy,
+        labels_vir[:, None],
+        spread_labels,
+        vir_energy[:, None],
         pair_irrep[None, :],
-        energy_ab[:, :, None],
         label_ij,
         energy_ij,
         slot,

time: 116 us -> 100 us (0.86)
  starting transfers between devices: 27.6 us -> 50.3 us
  blocking collectives: 16.5 us -> 0 us
  between operations: 13.6 us -> 0.31 us
  Pallas kernels: 20.2 us -> 15.6 us
  waiting for transfers between devices: 30.3 us -> 26.2 us
    ppermute x0 -> x6, starting transfers between devices: none -> 19.5 us  [the longest x4 13.7 us: on_device(): lax.ppermute(array, 'vir', [(i, (i - 2 * k) % 16) for i in range(16)])]
    all_to_all x1 -> x0, blocking collectives: 16.5 us -> none  [on_device(): lax.all_to_all(copies, 'occ', split_axis=0, concat_axis=0, tiled=True, ax...]
    all_to_all x1, waiting for transfers between devices: 14.4 us -> 0.01 us  [on_device(): lax.all_to_all(rows, 'occ', split_axis=0, concat_axis=0, tiled=True, axis...]
    ppermute x0 -> x6, waiting for transfers between devices: none -> 9.85 us  [the longest x4 9.54 us: on_device(): lax.ppermute(array, 'vir', [(i, (i - 2 * k) % 16) for i in range(16)])]
    pallas_call x1, Pallas kernels: 14 us -> 9.26 us  [on_device(): pl.pallas_call(finish, grid=(OWN // STEP,), out_shape=jax.ShapeDtypeStruc...]
    all_to_all x0 -> x1, starting transfers between devices: none -> 3.45 us  [on_device(): lax.all_to_all(copies, 'occ', split_axis=0, concat_axis=0, tiled=True, ax...]
    unnamed x20 -> x19, local copies, waits for them, and re-layouts: 3.15 us -> 1.02 us
    all_to_all x0 -> x1, waiting for transfers between devices: none -> 2.04 us  [on_device(): lax.all_to_all(copies, 'occ', split_axis=0, concat_axis=0, tiled=True, ax...]
  transfers between devices with their start and end apart: 4 -> 10, of which waited for: 3 -> 8; matrix products, arithmetic and copies ran while one was open for 3% -> 6% of each run, Pallas kernels for 4% -> 0%
where the time goes in v2:
time: 100 us; the launch traced here: 99.4 us
  starting transfers between devices  50.3 us (50%)
  waiting for transfers between devices  26.2 us (26%)
  Pallas kernels  15.6 us (16%)
  local copies, waits for them, and re-layouts  5.37 us (5%)
  other arithmetic  1.64 us (2%)
    all_to_all x1, starting transfers between devices, on_device(): lax.all_to_all(turned, 'occ', split_axis=0, concat_axis=0, tiled=True)  13.7 us
    ppermute x4, starting transfers between devices, on_device(): lax.ppermute(array, 'vir', [(i, (i - 2 * k) % 16) for i in range(16)])  13.7 us
    all_to_all x1, starting transfers between devices, on_device(): lax.all_to_all(blocks, 'vir', split_axis=0, concat_axis=0, tiled=True)  9.96 us
    all_to_all x1, waiting for transfers between devices, on_device(): lax.all_to_all(blocks, 'vir', split_axis=0, concat_axis=0, tiled=True)  9.73 us
    ppermute x4, waiting for transfers between devices, on_device(): lax.ppermute(array, 'vir', [(i, (i - 2 * k) % 16) for i in range(16)])  9.54 us
    pallas_call x1, Pallas kernels, on_device(): pl.pallas_call(finish, grid=(OWN // STEP,), out_shape=jax.ShapeDtypeStruc...  9.26 us
    pallas_call x5, Pallas kernels, call(): pl.pallas_call(kernel, out_shape=shapes, in_specs=[VMEM] * len(args), out...  6.34 us
    ppermute x2, starting transfers between devices, on_device(): lax.ppermute(array, 'vir', [(i, i ^ 1) for i in range(16)])  5.8 us
  transfers between devices with their start and end apart: 10, of which 8 were waited for; matrix products, arithmetic and copies ran while one was open for 6% of the time, Pallas kernels for 0%

profile of v2, /device:TPU:1, one launch (start us, length us, event | category | flops | bytes accessed | tf_op | source)
XLA Modules:
  0.0 99.4 jit_solution(17274498129797933523)
XLA Ops:
  0.0 0.0 copy-start.1
  0.0 0.0 copy-start.2
  0.0 1.0 copy-done.2
  1.0 0.0 copy-start.4
  1.0 1.1 %shard_map.100 = bf16[32,24,128]{2,1,0:T(8,128)(2,1)} custom-call(bf16[50,1536]{1,0:T(8,128)(2,1)S(1)} %copy-done.2), custom_call_target="tpu_custom_call" | custom-call | tf_op jit(solution)/shard_map/pallas_call | solution.py:32
  2.0 13.7 %all-to-all-start = ((bf16[32,24,128]{2,1,0:T(8,128)(2,1)}), bf16[32,24,128]{2,1,0:T(8,128)(2,1)S(1)}, u32[]{:S(2)}, u32[]{:S(2)}) async-start(bf16[32,24,128]{2,1,0:T(8,128)(2,1)} %shard_map.100), calls=%async_computation | async-start | bytes 393216 | tf_op jit(solution)/shard_map/all_to_all | solution.py:197
  15.8 0.8 reshape.142
  16.6 0.8 xor.40
  17.3 0.1 dynamic_slice.12.own_label_ref
  17.4 0.1 xor.37
  17.5 0.1 xor.38
  17.6 0.1 copy.22
  17.6 1.1 %select_reduce_fusion.2 = (s32[1250]{0:T(1024)S(1)}, s32[1250]{0:T(1024)S(1)}) fusion(s32[1250]{0:T(1024)S(1)} %get-tuple-element.17, s32[200]{0:T(256)} %param.13, s32[1250]{0:T(1024)S(1)} %get-tuple-element.18), kind=kLoop, calls=%fused_computation.2 | loop fusion | flops 1497500 | bytes 20800 | tf_op jit(solution)/shard_map/reduce_sum | solution.py:43
  18.8 0.8 dynamic-slice_bitcast_fusion.1
  19.5 0.1 copy.24.label_cd_ref
  19.6 0.8 dynamic-slice_bitcast_fusion
  20.4 0.1 copy.25.label_cd_ref
  20.5 0.1 copy.23
  20.6 4.6 %all-to-all-done.got_ref = bf16[32,24,128]{2,1,0:T(8,128)(2,1)S(1)} async-done(((bf16[32,24,128]{2,1,0:T(8,128)(2,1)}), bf16[32,24,128]{2,1,0:T(8,128)(2,1)S(1)}, u32[]{:S(2)}, u32[]{:S(2)}) %all-to-all-start) | async-done | bytes 196640 | tf_op jit(solution)/shard_map/all_to_all | solution.py:197
  25.2 1.2 %shard_map.101.own_ref = bf16[16,48,128]{2,1,0:T(8,128)(2,1)} custom-call(bf16[32,24,128]{2,1,0:T(8,128)(2,1)S(1)} %all-to-all-done.got_ref), custom_call_target="tpu_custom_call" | custom-call | tf_op jit(solution)/shard_map/pallas_call | solution.py:32
  26.4 10.0 %all-to-all-start.1 = ((bf16[16,48,128]{2,1,0:T(8,128)(2,1)}), bf16[16,48,128]{2,1,0:T(8,128)(2,1)S(1)}, u32[]{:S(2)}, u32[]{:S(2)}) async-start(bf16[16,48,128]{2,1,0:T(8,128)(2,1)} %shard_map.101.own_ref), calls=%async_computation.1 | async-start | bytes 393216 | tf_op jit(solution)/shard_map/all_to_all | solution.py:199
  36.4 0.1 fusion.5.slot_ref
  36.5 0.0 copy-done.1
  36.5 0.0 copy-start
  36.5 0.5 shard_map.103
  37.0 9.7 %all-to-all-done.1.mirror_ref = bf16[16,48,128]{2,1,0:T(8,128)(2,1)S(1)} async-done(((bf16[16,48,128]{2,1,0:T(8,128)(2,1)}), bf16[16,48,128]{2,1,0:T(8,128)(2,1)S(1)}, u32[]{:S(2)}, u32[]{:S(2)}) %all-to-all-start.1) | async-done | bytes 196640 | tf_op jit(solution)/shard_map/all_to_all | solution.py:199
  46.7 0.0 copy-done.4
  46.7 2.0 %shard_map.102 = bf16[8,4,48,128]{3,2,1,0:T(8,128)(2,1)} custom-call(bf16[16,48,128]{2,1,0:T(8,128)(2,1)} %shard_map.101.own_ref, bf16[16,48,128]{2,1,0:T(8,128)(2,1)S(1)} %all-to-all-done.1.mirror_ref, bf16[128,128]{1,0:T(8,128)(2,1)S(1)} %copy-done.4, s32[16,128]{1,0:T(8,128)S(1)} %pad.8.label_ab_ref, s32[48,1]{1,0:T(8,128)S(1)} %copy.24.label_cd_ref), custom_call_target="tpu_custom_call" | custom-call | tf_op jit(solution)/shard_map/pallas_call | solution.py:32
  48.7 3.5 %all-to-all-start.2 = ((bf16[8,4,48,128]{3,2,1,0:T(8,128)(2,1)}), bf16[8,4,48,128]{3,2,1,0:T(8,128)(2,1)S(1)}, u32[]{:S(2)}, u32[]{:S(2)}) async-start(bf16[8,4,48,128]{3,2,1,0:T(8,128)(2,1)} %shard_map.102), calls=%async_computation.2 | async-start | bytes 786432 | tf_op jit(solution)/shard_map/all_to_all | solution.py:210
  52.1 2.7 %collective-permute-start.1 = (bf16[1,96,384]{2,1,0:T(8,128)(2,1)S(1)}, bf16[1,96,384]{2,1,0:T(8,128)(2,1)S(1)}, u32[]{:S(2)}, u32[]{:S(2)}) collective-permute-start(bf16[1,96,384]{2,1,0:T(8,128)(2,1)S(1)} %shard_map.103), channel_id=1, source_target_pairs={{0,6},{1,7},{2,8},{3,9},{4,10},{5,11},{6,12},{7,13},{8,14},{9,15},... | collective-permute-start | bytes 221192 | tf_op jit(solution)/shard_map/ppermute | solution.py:194
  54.8 5.6 %collective-permute-start = (bf16[1,96,384]{2,1,0:T(8,128)(2,1)S(1)}, bf16[1,96,384]{2,1,0:T(8,128)(2,1)S(1)}, u32[]{:S(2)}, u32[]{:S(2)}) collective-permute-start(bf16[1,96,384]{2,1,0:T(8,128)(2,1)S(1)} %shard_map.103), channel_id=1, source_target_pairs={{0,10},{1,11},{2,12},{3,13},{4,14},{5,15},{6,0},{7,1},{8,2},{9,3},... | collective-permute-start | bytes 221192 | tf_op jit(solution)/shard_map/ppermute | solution.py:194
  60.4 0.8 collective-permute-done.1
  61.2 4.0 %collective-permute-done = bf16[1,96,384]{2,1,0:T(8,128)(2,1)S(1)} collective-permute-done((bf16[1,96,384]{2,1,0:T(8,128)(2,1)S(1)}, bf16[1,96,384]{2,1,0:T(8,128)(2,1)S(1)}, u32[]{:S(2)}, u32[]{:S(2)}) %collective-permute-start) | collective-permute-done | bytes 73760 | tf_op jit(solution)/shard_map/ppermute | solution.py:194
  65.3 2.0 %all-to-all-done.2.got_ref = bf16[8,4,48,128]{3,2,1,0:T(8,128)(2,1)S(1)} async-done(((bf16[8,4,48,128]{3,2,1,0:T(8,128)(2,1)}), bf16[8,4,48,128]{3,2,1,0:T(8,128)(2,1)S(1)}, u32[]{:S(2)}, u32[]{:S(2)}) %all-to-all-start.2) | async-done | bytes 393248 | tf_op jit(solution)/shard_map/all_to_all | solution.py:210
  67.3 0.0 copy-done
  67.3 1.6 %shard_map.104 = bf16[4,10,40,384]{3,2,1,0:T(8,128)(2,1)} custom-call(bf16[8,4,48,128]{3,2,1,0:T(8,128)(2,1)S(1)} %all-to-all-done.2.got_ref, bf16[4,400,128]{2,1,0:T(8,128)(2,1)S(1)} %copy-done), custom_call_target="tpu_custom_call" | custom-call | tf_op jit(solution)/shard_map/pallas_call | solution.py:32
  68.9 0.0 copy-start.5
  68.9 0.0 copy-start.6
  68.9 0.0 copy-start.8
  68.9 0.0 copy-start.7
  68.9 3.7 %all-to-all-start.3 = ((bf16[4,10,40,384]{3,2,1,0:T(8,128)(2,1)}), bf16[4,10,40,384]{3,2,1,0:T(8,128)(2,1)S(1)}, u32[]{:S(2)}, u32[]{:S(2)}) async-start(bf16[4,10,40,384]{3,2,1,0:T(8,128)(2,1)} %shard_map.104), calls=%async_computation.3 | async-start | bytes 2457600 | tf_op jit(solution)/shard_map/all_to_all | solution.py:218
  72.6 0.0 copy-start.3
  72.6 2.8 %collective-permute-start.2 = (bf16[3,96,384]{2,1,0:T(8,128)(2,1)S(1)}, bf16[3,96,384]{2,1,0:T(8,128)(2,1)S(1)}, u32[]{:S(2)}, u32[]{:S(2)}) collective-permute-start(bf16[3,96,384]{2,1,0:T(8,128)(2,1)S(1)} %pad_maximum_fusion.three_ref), channel_id=1, source_target_pairs={{0,14},{1,15},{2,0},{3,1},{4,2},{5,3},{6,4},{7,5},{8,6},{9,7},{10,... | collective-permute-start | bytes 663560 | tf_op jit(solution)/shard_map/ppermute | solution.py:194
  75.5 2.6 %collective-permute-start.3 = (bf16[2,96,384]{2,1,0:T(8,128)(2,1)S(1)}, bf16[2,96,384]{2,1,0:T(8,128)(2,1)S(1)}, u32[]{:S(2)}, u32[]{:S(2)}) collective-permute-start(bf16[2,96,384]{2,1,0:T(8,128)(2,1)S(1)} %slice.3), channel_id=1, source_target_pairs={{0,2},{1,3},{2,4},{3,5},{4,6},{5,7},{6,8},{7,9},{8,10},{9,11},{10,... | collective-permute-start | bytes 442376 | tf_op jit(solution)/shard_map/ppermute | solution.py:194
  78.1 3.2 %collective-permute-done.2 = bf16[3,96,384]{2,1,0:T(8,128)(2,1)S(1)} collective-permute-done((bf16[3,96,384]{2,1,0:T(8,128)(2,1)S(1)}, bf16[3,96,384]{2,1,0:T(8,128)(2,1)S(1)}, u32[]{:S(2)}, u32[]{:S(2)}) %collective-permute-start.2) | collective-permute-done | bytes 221216 | tf_op jit(solution)/shard_map/ppermute | solution.py:194
  81.3 1.6 %collective-permute-done.3 = bf16[2,96,384]{2,1,0:T(8,128)(2,1)S(1)} collective-permute-done((bf16[2,96,384]{2,1,0:T(8,128)(2,1)S(1)}, bf16[2,96,384]{2,1,0:T(8,128)(2,1)S(1)}, u32[]{:S(2)}, u32[]{:S(2)}) %collective-permute-start.3) | collective-permute-done | bytes 147488 | tf_op jit(solution)/shard_map/ppermute | solution.py:194
  82.9 3.9 %collective-permute-start.5 = (bf16[5,96,384]{2,1,0:T(8,128)(2,1)S(1)}, bf16[5,96,384]{2,1,0:T(8,128)(2,1)S(1)}, u32[]{:S(2)}, u32[]{:S(2)}) collective-permute-start(bf16[5,96,384]{2,1,0:T(8,128)(2,1)S(1)} %constant_dynamic-update-slice_fusion.five_ref), channel_id=1, source_target_pairs={{0,1},{1,0},{2,3},{3,2},{4,5},{5,4},{6,7},{7,6},{8,9},{9,8},{10,11... | collective-permute-start | bytes 1105928 | tf_op jit(solution)/shard_map/ppermute | solution.py:215
  86.8 1.9 %collective-permute-start.4 = (bf16[3,96,384]{2,1,0:T(8,128)(2,1)S(1)}, bf16[3,96,384]{2,1,0:T(8,128)(2,1)S(1)}, u32[]{:S(2)}, u32[]{:S(2)}) collective-permute-start(bf16[3,96,384]{2,1,0:T(8,128)(2,1)S(1)} %pad_maximum_fusion.three_ref), channel_id=1, source_target_pairs={{0,1},{1,0},{2,3},{3,2},{4,5},{5,4},{6,7},{7,6},{8,9},{9,8},{10,11... | collective-permute-start | bytes 663560 | tf_op jit(solution)/shard_map/ppermute | solution.py:215
  88.7 0.0 copy-done.5
  88.7 0.1 reshape_reshape.3
  88.8 0.0 copy-done.6
  88.8 0.1 broadcast_in_dim_reshape.5.label_b_ref
  89.0 0.0 copy-done.8
  89.0 0.1 dynamic_slice.15.own_energy_ref
  89.0 0.1 reshape.144
  89.1 0.0 copy-done.7
  89.1 0.4 select_reduce_fusion
  89.6 0.1 copy.29.energy_b_ref
  89.7 0.1 reshape.146.spread_label_b_ref
  89.8 0.3 collective-permute-done.4.core_three_ref
  90.1 0.0 collective-permute-done.5.core_five_ref
  90.1 0.0 all-to-all-done.3.packed_ref
  90.2 0.0 copy-done.3
  90.2 9.3 %shard_map.105 = bf16[1600,1250]{1,0:T(8,128)(2,1)} custom-call(bf16[4,10,40,384]{3,2,1,0:T(8,128)(2,1)S(1)} %all-to-all-done.3.packed_ref, bf16[3,96,384]{2,1,0:T(8,128)(2,1)S(1)} %pad_maximum_fusion.three_ref, bf16[5,96,384]{2,1,0:T(8,128)(2,1)S(1)} %constant_dynamic-update-slice_fusion.five_ref, ...), custom_call_target="tpu_custom_call" | custom-call | tf_op jit(solution)/shard_map/pallas_call | solution.py:225
  (16 shorter events, 0.2 us)
Async XLA Ops:
  0.0 36.5 %copy-start.1 = (bf16[96,1250]{1,0:T(8,128)(2,1)S(1)}, bf16[96,1250]{1,0:T(8,128)(2,1)}, u32[]{:S(2)}) copy-start(bf16[96,1250]{1,0:T(8,128)(2,1)} %amp_ref.1) | copy-start | bytes 720004
  0.0 1.0 copy-start.2
  1.0 45.7 %copy-start.4 = (bf16[128,128]{1,0:T(8,128)(2,1)S(1)}, bf16[128,128]{1,0:T(8,128)(2,1)}, u32[]{:S(2)}) copy-start(bf16[128,128]{1,0:T(8,128)(2,1)} %constant.65.clone.swap_ref) | copy-start | bytes 98308
  2.0 23.1 %all-to-all-start = ((bf16[32,24,128]{2,1,0:T(8,128)(2,1)}), bf16[32,24,128]{2,1,0:T(8,128)(2,1)S(1)}, u32[]{:S(2)}, u32[]{:S(2)}) async-start(bf16[32,24,128]{2,1,0:T(8,128)(2,1)} %shard_map.100), calls=%async_computation | async-start | bytes 393216 | tf_op jit(solution)/shard_map/all_to_all | solution.py:197
  26.4 20.3 %all-to-all-start.1 = ((bf16[16,48,128]{2,1,0:T(8,128)(2,1)}), bf16[16,48,128]{2,1,0:T(8,128)(2,1)S(1)}, u32[]{:S(2)}, u32[]{:S(2)}) async-start(bf16[16,48,128]{2,1,0:T(8,128)(2,1)} %shard_map.101.own_ref), calls=%async_computation.1 | async-start | bytes 393216 | tf_op jit(solution)/shard_map/all_to_all | solution.py:199
  36.5 30.8 %copy-start = (bf16[4,400,128]{2,1,0:T(8,128)(2,1)S(1)}, bf16[4,400,128]{2,1,0:T(8,128)(2,1)}, u32[]{:S(2)}) copy-start(bf16[4,400,128]{2,1,0:T(8,128)(2,1)} %constant.66.clone.place_ref) | copy-start | bytes 1228804
  48.7 18.6 %all-to-all-start.2 = ((bf16[8,4,48,128]{3,2,1,0:T(8,128)(2,1)}), bf16[8,4,48,128]{3,2,1,0:T(8,128)(2,1)S(1)}, u32[]{:S(2)}, u32[]{:S(2)}) async-start(bf16[8,4,48,128]{3,2,1,0:T(8,128)(2,1)} %shard_map.102), calls=%async_computation.2 | async-start | bytes 786432 | tf_op jit(solution)/shard_map/all_to_all | solution.py:210
  52.1 9.1 %collective-permute-start.1 = (bf16[1,96,384]{2,1,0:T(8,128)(2,1)S(1)}, bf16[1,96,384]{2,1,0:T(8,128)(2,1)S(1)}, u32[]{:S(2)}, u32[]{:S(2)}) collective-permute-start(bf16[1,96,384]{2,1,0:T(8,128)(2,1)S(1)} %shard_map.103), channel_id=1, source_target_pairs={{0,6},{1,7},{2,8},{3,9},{4,10},{5,11},{6,12},{7,13},{8,14},{9,15},... | collective-permute-start | bytes 221192 | tf_op jit(solution)/shard_map/ppermute | solution.py:194
  54.8 10.4 %collective-permute-start = (bf16[1,96,384]{2,1,0:T(8,128)(2,1)S(1)}, bf16[1,96,384]{2,1,0:T(8,128)(2,1)S(1)}, u32[]{:S(2)}, u32[]{:S(2)}) collective-permute-start(bf16[1,96,384]{2,1,0:T(8,128)(2,1)S(1)} %shard_map.103), channel_id=1, source_target_pairs={{0,10},{1,11},{2,12},{3,13},{4,14},{5,15},{6,0},{7,1},{8,2},{9,3},... | collective-permute-start | bytes 221192 | tf_op jit(solution)/shard_map/ppermute | solution.py:194
  68.9 19.8 %copy-start.5 = (s32[2,80]{1,0:T(2,128)S(1)}, s32[2,80]{1,0:T(2,128)}, u32[]{:S(2)}) copy-start(s32[2,80]{1,0:T(2,128)} %param.12) | copy-start | bytes 1924
  68.9 19.9 %copy-start.6 = (s32[1536]{0:T(1024)S(1)}, s32[1536]{0:T(1024)}, u32[]{:S(2)}) copy-start(s32[1536]{0:T(1024)} %param.14) | copy-start | bytes 18436
  68.9 20.0 %copy-start.8 = (f32[160]{0:T(256)S(1)}, f32[160]{0:T(256)}, u32[]{:S(2)}) copy-start(f32[160]{0:T(256)} %param.15) | copy-start | bytes 1924
  68.9 20.2 %copy-start.7 = (f32[200]{0:T(256)S(1)}, f32[200]{0:T(256)}, u32[]{:S(2)}) copy-start(f32[200]{0:T(256)} %param.16) | copy-start | bytes 2404
  68.9 21.2 %all-to-all-start.3 = ((bf16[4,10,40,384]{3,2,1,0:T(8,128)(2,1)}), bf16[4,10,40,384]{3,2,1,0:T(8,128)(2,1)S(1)}, u32[]{:S(2)}, u32[]{:S(2)}) async-start(bf16[4,10,40,384]{3,2,1,0:T(8,128)(2,1)} %shard_map.104), calls=%async_computation.3 | async-start | bytes 2457600 | tf_op jit(solution)/shard_map/all_to_all | solution.py:218
  72.6 17.5 %copy-start.3 = (bf16[160,192]{1,0:T(8,128)(2,1)S(1)}, bf16[160,192]{1,0:T(8,128)(2,1)}, u32[]{:S(2)}) copy-start(bf16[160,192]{1,0:T(8,128)(2,1)} %constant.67.clone.pick_ref) | copy-start | bytes 184324
  72.6 8.6 %collective-permute-start.2 = (bf16[3,96,384]{2,1,0:T(8,128)(2,1)S(1)}, bf16[3,96,384]{2,1,0:T(8,128)(2,1)S(1)}, u32[]{:S(2)}, u32[]{:S(2)}) collective-permute-start(bf16[3,96,384]{2,1,0:T(8,128)(2,1)S(1)} %pad_maximum_fusion.three_ref), channel_id=1, source_target_pairs={{0,14},{1,15},{2,0},{3,1},{4,2},{5,3},{6,4},{7,5},{8,6},{9,7},{10,... | collective-permute-start | bytes 663560 | tf_op jit(solution)/shard_map/ppermute | solution.py:194
  75.5 7.4 %collective-permute-start.3 = (bf16[2,96,384]{2,1,0:T(8,128)(2,1)S(1)}, bf16[2,96,384]{2,1,0:T(8,128)(2,1)S(1)}, u32[]{:S(2)}, u32[]{:S(2)}) collective-permute-start(bf16[2,96,384]{2,1,0:T(8,128)(2,1)S(1)} %slice.3), channel_id=1, source_target_pairs={{0,2},{1,3},{2,4},{3,5},{4,6},{5,7},{6,8},{7,9},{8,10},{9,11},{10,... | collective-permute-start | bytes 442376 | tf_op jit(solution)/shard_map/ppermute | solution.py:194
  82.9 7.3 %collective-permute-start.5 = (bf16[5,96,384]{2,1,0:T(8,128)(2,1)S(1)}, bf16[5,96,384]{2,1,0:T(8,128)(2,1)S(1)}, u32[]{:S(2)}, u32[]{:S(2)}) collective-permute-start(bf16[5,96,384]{2,1,0:T(8,128)(2,1)S(1)} %constant_dynamic-update-slice_fusion.five_ref), channel_id=1, source_target_pairs={{0,1},{1,0},{2,3},{3,2},{4,5},{5,4},{6,7},{7,6},{8,9},{9,8},{10,11... | collective-permute-start | bytes 1105928 | tf_op jit(solution)/shard_map/ppermute | solution.py:215
  86.8 3.4 %collective-permute-start.4 = (bf16[3,96,384]{2,1,0:T(8,128)(2,1)S(1)}, bf16[3,96,384]{2,1,0:T(8,128)(2,1)S(1)}, u32[]{:S(2)}, u32[]{:S(2)}) collective-permute-start(bf16[3,96,384]{2,1,0:T(8,128)(2,1)S(1)} %pad_maximum_fusion.three_ref), channel_id=1, source_target_pairs={{0,1},{1,0},{2,3},{3,2},{4,5},{5,4},{6,7},{7,6},{8,9},{9,8},{10,11... | collective-permute-start | bytes 663560 | tf_op jit(solution)/shard_map/ppermute | solution.py:215

commit v3 on v2

--- a/solution.py
+++ b/solution.py
@@ -17,7 +17,6 @@
 SLOTS = 384
 LANES = 128
 STEP = 5
-CHIPS = (0, 3, 5, 1, 4, 6, 7, 2)
 F32 = jnp.float32
 BF16 = jnp.bfloat16
 VMEM = pl.BlockSpec(memory_space=pltpu.VMEM)
@@ -84,6 +83,8 @@
 
 def difference(own_ref, mirror_ref, swap_ref, label_ab_ref, label_cd_ref, out_ref):
     label_cd = label_cd_ref[...]
+    lane = lax.broadcasted_iota(jnp.int32, (CDS, LANES), 1)
+    blocks = [jnp.zeros((CDS, LANES), F32) for _ in range(4)]
     for slab in range(2):
         for odd in range(2):
             packed = jnp.zeros((CDS, LANES), F32)
@@ -93,53 +94,68 @@
                 diff = own_ref[partner].astype(F32) - mirrored
                 keep = label_ab_ref[partner : partner + 1, :] == label_cd
                 packed = jnp.where(keep, diff, packed)
-            packed = packed.astype(BF16)
-            for copy in range(8):
-                out_ref[copy, 2 * slab + odd] = packed
-
-
-def turn_back(got_ref, place_ref, out_ref):
-    total = jnp.zeros((400, 384), F32)
+            first = 100 * (2 * slab + odd)
+            if first:
+                packed = pltpu.roll(packed, first % LANES, axis=1)
+            for index in range(4):
+                low, high = max(first - LANES * index, 0), min(first + 100 - LANES * index, LANES)
+                if low < high:
+                    blocks[index] = jnp.where((lane >= low) & (lane < high), packed, blocks[index])
+    rest = blocks[3][0:8]
+    for group in range(1, 6):
+        rest = rest + pltpu.roll(blocks[3][8 * group : 8 * group + 8], 16 * group, axis=1)
+    whole = jnp.concatenate([*blocks[:3], rest], axis=0).astype(BF16)
+    for copy in range(32):
+        out_ref[copy] = whole
+
+
+def turn_back(got_ref, place_ref, rest_ref, out_ref):
+    for source in range(32):
+        piece = got_ref[source, 144:152, :].astype(F32)
+        groups = [piece] + [pltpu.roll(piece, LANES - 16 * group, axis=1) for group in range(1, 6)]
+        rest_ref[CDS * source : CDS * source + CDS, :] = jnp.concatenate(groups, axis=0).astype(BF16)
     for part in range(4):
-        block = got_ref[:, part].reshape(384, LANES)
-        total = total + dot(place_ref[part], block, ((1,), (1,)))
-    for a in range(OWN):
-        rows = total[40 * a : 40 * a + 40].astype(BF16)
-        for copy in range(4):
-            out_ref[copy, a] = rows
-
-
-def finish(packed_ref, three_ref, five_ref, core_three_ref, core_five_ref, pick_ref, vir_ref, own_label_ref, own_energy_ref, label_b_ref,
+        at = 384 * part
+        total = dot(place_ref[3], rest_ref[at : at + 384, :], ((1,), (1,)))
+        for index in range(3):
+            block = got_ref[8 * part : 8 * part + 8, CDS * index : CDS * index + CDS, :].reshape(384, LANES)
+            total = total + dot(place_ref[index], block, ((1,), (1,)))
+        out_ref[:, at : at + 384] = total.astype(BF16)
+
+
+def finish(got_ref, turn_ref, six_ref, core_six_ref, last_ref, core_last_ref, pick_ref, vir_ref, own_label_ref, own_energy_ref, label_b_ref,
            spread_label_b_ref, energy_b_ref, label_cd_ref, label_ij_ref, energy_ij_ref, slot_ref, out_ref,
-           amp_ref, place_ref, left_ref):
+           rest_ref, rows_ref, amp_ref, place_ref, left_ref):
     step = pl.program_id(0)
 
     @pl.when(step == 0)
     def _():
+        turn_back(got_ref, turn_ref, rest_ref, rows_ref)
         rows = lax.broadcasted_iota(jnp.int32, (SLOTS, PAIRS), 0)
         place_ref[...] = jnp.where(rows == slot_ref[...], 1.0, 0.0).astype(BF16)
-        for part, core, first in ((three_ref, 0, 0), (five_ref, 0, 3), (core_three_ref, 1, 0), (core_five_ref, 1, 3)):
-            for index in range(part.shape[0]):
-                source = ((vir_ref[0] ^ core) + 2 * CHIPS[first + index]) & 15
+        six, last = (0, 1, 2, 3, 6, 7), (4, 5)
+        for part, core, chips in ((six_ref, 0, six), (core_six_ref, 1, six), (last_ref, 0, last), (core_last_ref, 1, last)):
+            for index, chip in enumerate(chips):
+                source = ((vir_ref[0] ^ core) + 2 * chip) & 15
                 amp_ref[pl.ds(pl.multiple_of(96 * source, 96), 96), :] = part[index]
 
     for a in range(STEP):
         label_a = own_label_ref[step * STEP + a]
         for part in range(4):
             wanted = label_cd_ref[:, 384 * part : 384 * part + 384] ^ label_a
-            values = packed_ref[part, a].astype(F32)
-            values = jnp.concatenate([values, jnp.zeros((8, 384), F32)], axis=0)
+            own = pl.ds(pl.multiple_of(48 * (step * STEP + a), 48), 48)
+            values = rows_ref[own, 384 * part : 384 * part + 384].astype(F32)
             for quarter in range(4):
                 keep = spread_label_b_ref[48 * quarter : 48 * quarter + 48, :] == wanted
                 at = 192 * a + 48 * quarter
                 left_ref[at : at + 48, 384 * part : 384 * part + 384] = jnp.where(keep, values, 0.0).astype(BF16)
     total = dot(left_ref[...], amp_ref[...]).astype(BF16)
+    picked = [dot(pick_ref[...], total[192 * a : 192 * a + 192]).astype(BF16) for a in range(STEP)]
+    ladder = dot(jnp.concatenate(picked, axis=0), place_ref[...])
     for a in range(STEP):
-        picked = dot(pick_ref[...], total[192 * a : 192 * a + 192]).astype(BF16)
-        ladder = dot(picked, place_ref[...])
         label_a = own_label_ref[step * STEP + a]
         energy_a = own_energy_ref[step * STEP + a]
-        update = ladder / ((energy_ij_ref[...] - energy_a) - energy_b_ref[...])
+        update = ladder[NW * a : NW * a + NW] / ((energy_ij_ref[...] - energy_a) - energy_b_ref[...])
         keep = label_b_ref[...] == (label_ij_ref[...] ^ label_a)
         out_ref[NW * a : NW * a + NW, :] = jnp.where(keep, update, 0.0).astype(BF16)
 
@@ -153,11 +169,12 @@
 
 
 def place_table():
-    table = np.zeros((4, 400, LANES), np.float32)
+    table = np.zeros((4, 480, LANES), np.float32)
     for a in range(OWN):
         for part in range(4):
             for b in range(OWN):
-                table[part, a * 40 + part * OWN + b, a * OWN + b] = 1.0
+                column = 100 * part + OWN * a + b
+                table[column // LANES, 48 * a + OWN * part + b, column % LANES] = 1.0
     return table
 
 
@@ -172,8 +189,6 @@
 def on_device(pair_integrals, amplitudes, vir_irrep, occ_irrep, pair_irrep, vir_energy, occ_energy):
     occ = lax.axis_index("occ")
     vir = lax.axis_index("vir")
-    z_groups = [[8 * x + z for z in range(8)] for x in range(4)]
-    x_groups = [[8 * x + z for x in range(4)] for z in range(8)]
 
     labels_vir = vir_irrep.reshape(-1)
     own_labels = lax.dynamic_slice_in_dim(labels_vir, vir * OWN, OWN)
@@ -196,26 +211,24 @@
     turned = call(turn_rows, jax.ShapeDtypeStruct((32, CDS // 2, LANES), BF16), (pair_integrals,))
     slices = lax.all_to_all(turned, "occ", split_axis=0, concat_axis=0, tiled=True)
     blocks = call(by_partner, jax.ShapeDtypeStruct((16, CDS, LANES), BF16), (slices,))
+    blocks, packed_amp = lax.optimization_barrier((blocks, packed_amp))
+    amp_pair = jnp.concatenate([packed_amp, from_chip(packed_amp, 1)], axis=0)
     mirror = lax.all_to_all(blocks, "vir", split_axis=0, concat_axis=0, tiled=True)
     block_labels = label_ab.reshape(OWN, 16, OWN).transpose(1, 0, 2).reshape(16, OWN * OWN)
     block_labels = jnp.pad(block_labels, ((0, 0), (0, LANES - OWN * OWN)), constant_values=-1)
     label_cds = lax.dynamic_slice_in_dim(pair_irrep, occ * CDS, CDS)[:, None]
     copies = call(
         difference,
-        jax.ShapeDtypeStruct((8, 4, CDS, LANES), BF16),
+        jax.ShapeDtypeStruct((32, 152, LANES), BF16),
         (blocks, mirror, jnp.asarray(swap_table(), BF16), block_labels, label_cds),
     )
-    copies, packed_amp = lax.optimization_barrier((copies, packed_amp))
-    amp_three = jnp.concatenate([packed_amp, from_chip(packed_amp, 3), from_chip(packed_amp, 5)], axis=0)
-    line = lax.all_to_all(copies, "occ", split_axis=0, concat_axis=0, tiled=True, axis_index_groups=z_groups)
-    rows = call(
-        turn_back, jax.ShapeDtypeStruct((4, OWN, 40, 384), BF16), (line, jnp.asarray(place_table(), BF16))
-    )
-    rows, amp_three = lax.optimization_barrier((rows, amp_three))
+    copies, amp_pair = lax.optimization_barrier((copies, amp_pair))
+    amp_above = from_chip(amp_pair, 2)
+    amp_six = jnp.concatenate([amp_pair, amp_above, from_chip(amp_pair, 6)], axis=0)
     from_core = lambda array: lax.ppermute(array, "vir", [(i, i ^ 1) for i in range(16)])
-    amp_five = jnp.concatenate([from_chip(amp_three, 1), from_chip(amp_three[:2], 7)], axis=0)
-    amp_parts = (amp_three, amp_five, from_core(amp_three), from_core(amp_five))
-    packed = lax.all_to_all(rows, "occ", split_axis=0, concat_axis=0, tiled=True, axis_index_groups=x_groups)
+    amp_last, core_six = lax.optimization_barrier((from_chip(amp_above, 2), from_core(amp_six)))
+    amp_parts = (amp_six, core_six, amp_last, from_core(amp_last))
+    gathered = lax.all_to_all(copies, "occ", split_axis=0, concat_axis=0, tiled=True)
 
     spread_labels = jnp.pad(
         labels_vir.reshape(2, 4, 20).transpose(1, 0, 2).reshape(4, 40), ((0, 0), (0, 8)), constant_values=-1
@@ -227,11 +240,12 @@
         grid=(OWN // STEP,),
         out_shape=jax.ShapeDtypeStruct((OWN * NW, PAIRS), BF16),
         in_specs=[
-            pl.BlockSpec((4, STEP, 40, 384), lambda i: (0, i, 0, 0)),
-            whole(3, 96, SLOTS),
-            whole(5, 96, SLOTS),
-            whole(3, 96, SLOTS),
-            whole(5, 96, SLOTS),
+            whole(32, 152, LANES),
+            whole(4, 480, LANES),
+            whole(6, 96, SLOTS),
+            whole(6, 96, SLOTS),
+            whole(2, 96, SLOTS),
+            whole(2, 96, SLOTS),
             whole(NW, 192),
             scalars,
             scalars,
@@ -246,13 +260,16 @@
         ],
         out_specs=pl.BlockSpec((STEP * NW, PAIRS), lambda i: (i, 0)),
         scratch_shapes=[
+            pltpu.VMEM((CD, LANES), BF16),
+            pltpu.VMEM((480, CD), BF16),
             pltpu.VMEM((CD, SLOTS), BF16),
             pltpu.VMEM((SLOTS, PAIRS), BF16),
             pltpu.VMEM((STEP * 192, CD), BF16),
         ],
         compiler_params=params(),
     )(
-        packed,
+        gathered,
+        jnp.asarray(place_table(), BF16),
         *amp_parts,
         jnp.asarray(pick_table(), BF16),
         vir.reshape(1),

time: 100 us -> 96.7 us (0.967)
  starting transfers between devices: 50.3 us -> 47.6 us
    all_to_all x1, waiting for transfers between devices: 9.73 us -> 2.15 us  [on_device(): lax.all_to_all(blocks, 'vir', split_axis=0, concat_axis=0, tiled=True)]
    ppermute x4, waiting for transfers between devices: 9.54 us -> 13.6 us  [on_device(): lax.ppermute(array, 'vir', [(i, (i - 2 * k) % 16) for i in range(16)])]
    all_to_all x2 -> x1, waiting for transfers between devices: 2.04 us -> 5.19 us  [on_device(): lax.all_to_all(copies, 'occ', split_axis=0, concat_axis=0, tiled=True)]
    all_to_all x2 -> x1, starting transfers between devices: 7.13 us -> 4.08 us  [on_device(): lax.all_to_all(copies, 'occ', split_axis=0, concat_axis=0, tiled=True)]
    pallas_call x1, Pallas kernels: 9.26 us -> 10.5 us  [on_device(): pl.pallas_call(finish, grid=(OWN // STEP,), out_shape=jax.ShapeDtypeStruc...]
    pallas_call x5 -> x4, Pallas kernels: 6.34 us -> 5.17 us  [call(): pl.pallas_call(kernel, out_shape=shapes, in_specs=[VMEM] * len(args), out...]
  transfers between devices with their start and end apart: 10 -> 9, of which waited for: 8 -> 7; matrix products, arithmetic and copies ran while one was open for 6% -> 6% of each run, Pallas kernels for 0% -> 0%
where the time goes in v3:
time: 96.7 us; the launch traced here: 96 us
  starting transfers between devices  47.6 us (49%)
  waiting for transfers between devices  26.1 us (27%)
  Pallas kernels  15.7 us (16%)
  local copies, waits for them, and re-layouts  4.69 us (5%)
  other arithmetic  1.63 us (2%)
    ppermute x4, starting transfers between devices, on_device(): lax.ppermute(array, 'vir', [(i, (i - 2 * k) % 16) for i in range(16)])  13.9 us
    all_to_all x1, starting transfers between devices, on_device(): lax.all_to_all(turned, 'occ', split_axis=0, concat_axis=0, tiled=True)  13.8 us
    ppermute x4, waiting for transfers between devices, on_device(): lax.ppermute(array, 'vir', [(i, (i - 2 * k) % 16) for i in range(16)])  13.6 us
    pallas_call x1, Pallas kernels, on_device(): pl.pallas_call(finish, grid=(OWN // STEP,), out_shape=jax.ShapeDtypeStruc...  10.5 us
    all_to_all x1, starting transfers between devices, on_device(): lax.all_to_all(blocks, 'vir', split_axis=0, concat_axis=0, tiled=True)  9.96 us
    ppermute x2, starting transfers between devices, on_device(): lax.ppermute(array, 'vir', [(i, i ^ 1) for i in range(16)])  5.81 us
    all_to_all x1, waiting for transfers between devices, on_device(): lax.all_to_all(copies, 'occ', split_axis=0, concat_axis=0, tiled=True)  5.19 us
    pallas_call x4, Pallas kernels, call(): pl.pallas_call(kernel, out_shape=shapes, in_specs=[VMEM] * len(args), out...  5.17 us
  transfers between devices with their start and end apart: 9, of which 7 were waited for; matrix products, arithmetic and copies ran while one was open for 6% of the time, Pallas kernels for 0%

profile of v3, /device:TPU:1, one launch (start us, length us, event | category | flops | bytes accessed | tf_op | source)
XLA Modules:
  0.0 96.0 jit_solution(11327414486514343606)
XLA Ops:
  0.0 0.0 copy-start.1
  0.0 0.0 copy-start.2
  0.0 1.0 copy-done.2
  1.0 0.0 copy-start.6
  1.0 1.1 %shard_map.100 = bf16[32,24,128]{2,1,0:T(8,128)(2,1)} custom-call(bf16[50,1536]{1,0:T(8,128)(2,1)S(1)} %copy-done.2), custom_call_target="tpu_custom_call" | custom-call | tf_op jit(solution)/shard_map/pallas_call | solution.py:31
  2.0 0.0 copy-start.4
  2.0 13.8 %all-to-all-start = ((bf16[32,24,128]{2,1,0:T(8,128)(2,1)}), bf16[32,24,128]{2,1,0:T(8,128)(2,1)S(1)}, u32[]{:S(2)}, u32[]{:S(2)}) async-start(bf16[32,24,128]{2,1,0:T(8,128)(2,1)} %shard_map.100), calls=%async_computation | async-start | bytes 393216 | tf_op jit(solution)/shard_map/all_to_all | solution.py:212
  15.9 1.1 %select_reduce_fusion.2 = (s32[1250]{0:T(1024)S(1)}, s32[1250]{0:T(1024)S(1)}) fusion(s32[1250]{0:T(1024)S(1)} %get-tuple-element.21, s32[200]{0:T(256)} %param.13, s32[1250]{0:T(1024)S(1)} %get-tuple-element.22), kind=kLoop, calls=%fused_computation.2 | loop fusion | flops 1497500 | bytes 20800 | tf_op jit(solution)/shard_map/reduce_sum | solution.py:42
  17.0 0.8 reshape.142
  17.8 0.8 xor.42
  18.6 0.1 dynamic_slice.13.own_label_ref
  18.6 0.1 xor.39
  18.7 0.1 xor.40
  18.8 0.1 copy.23
  18.9 0.8 dynamic-slice_bitcast_fusion.1
  19.7 0.1 copy.22.label_cd_ref
  19.8 0.1 copy.24
  19.9 0.1 fusion.5.slot_ref
  20.0 0.0 copy-done.1
  20.0 0.5 shard_map.102
  20.4 4.9 %all-to-all-done.got_ref = bf16[32,24,128]{2,1,0:T(8,128)(2,1)S(1)} async-done(((bf16[32,24,128]{2,1,0:T(8,128)(2,1)}), bf16[32,24,128]{2,1,0:T(8,128)(2,1)S(1)}, u32[]{:S(2)}, u32[]{:S(2)}) %all-to-all-start) | async-done | bytes 196640 | tf_op jit(solution)/shard_map/all_to_all | solution.py:212
  25.3 1.2 %shard_map.101.own_ref = bf16[16,48,128]{2,1,0:T(8,128)(2,1)} custom-call(bf16[32,24,128]{2,1,0:T(8,128)(2,1)S(1)} %all-to-all-done.got_ref), custom_call_target="tpu_custom_call" | custom-call | tf_op jit(solution)/shard_map/pallas_call | solution.py:31
  26.5 10.0 %all-to-all-start.1 = ((bf16[16,48,128]{2,1,0:T(8,128)(2,1)}), bf16[16,48,128]{2,1,0:T(8,128)(2,1)S(1)}, u32[]{:S(2)}, u32[]{:S(2)}) async-start(bf16[16,48,128]{2,1,0:T(8,128)(2,1)} %shard_map.101.own_ref), calls=%async_computation.1 | async-start | bytes 393216 | tf_op jit(solution)/shard_map/all_to_all | solution.py:216
  36.5 4.5 %collective-permute-start = (bf16[1,96,384]{2,1,0:T(8,128)(2,1)S(1)}, bf16[1,96,384]{2,1,0:T(8,128)(2,1)S(1)}, u32[]{:S(2)}, u32[]{:S(2)}) collective-permute-start(bf16[1,96,384]{2,1,0:T(8,128)(2,1)S(1)} %shard_map.102), channel_id=1, source_target_pairs={{0,14},{1,15},{2,0},{3,1},{4,2},{5,3},{6,4},{7,5},{8,6},{9,7},{10,... | collective-permute-start | bytes 221192 | tf_op jit(solution)/shard_map/ppermute | solution.py:209
  41.0 0.0 copy-done.6
  41.0 0.1 dynamic-slice_bitcast_fusion
  41.1 0.1 copy.25.label_cd_ref
  41.2 3.4 %collective-permute-done = bf16[1,96,384]{2,1,0:T(8,128)(2,1)S(1)} collective-permute-done((bf16[1,96,384]{2,1,0:T(8,128)(2,1)S(1)}, bf16[1,96,384]{2,1,0:T(8,128)(2,1)S(1)}, u32[]{:S(2)}, u32[]{:S(2)}) %collective-permute-start) | collective-permute-done | bytes 73760 | tf_op jit(solution)/shard_map/ppermute | solution.py:209
  44.7 2.2 %all-to-all-done.1.mirror_ref = bf16[16,48,128]{2,1,0:T(8,128)(2,1)S(1)} async-done(((bf16[16,48,128]{2,1,0:T(8,128)(2,1)}), bf16[16,48,128]{2,1,0:T(8,128)(2,1)S(1)}, u32[]{:S(2)}, u32[]{:S(2)}) %all-to-all-start.1) | async-done | bytes 196640 | tf_op jit(solution)/shard_map/all_to_all | solution.py:216
  46.8 0.0 copy-done.4
  46.8 2.4 %shard_map.103 = bf16[32,152,128]{2,1,0:T(8,128)(2,1)} custom-call(bf16[16,48,128]{2,1,0:T(8,128)(2,1)} %shard_map.101.own_ref, bf16[16,48,128]{2,1,0:T(8,128)(2,1)S(1)} %all-to-all-done.1.mirror_ref, bf16[128,128]{1,0:T(8,128)(2,1)S(1)} %copy-done.4, s32[16,128]{1,0:T(8,128)S(1)} %pad.8.label_ab_ref, s32[48,1]{1,0:T(8,128)S(1)} %copy.25.label_cd_ref), custom_call_target="tpu_custom_call" | custom-call | tf_op jit(solution)/shard_map/pallas_call | solution.py:31
  49.2 0.0 copy-start.5
  49.2 0.0 copy-start.8
  49.2 0.0 copy-start.7
  49.2 4.1 %all-to-all-start.2 = ((bf16[32,152,128]{2,1,0:T(8,128)(2,1)}), bf16[32,152,128]{2,1,0:T(8,128)(2,1)S(1)}, u32[]{:S(2)}, u32[]{:S(2)}) async-start(bf16[32,152,128]{2,1,0:T(8,128)(2,1)} %shard_map.103), calls=%async_computation.2 | async-start | bytes 2490368 | tf_op jit(solution)/shard_map/all_to_all | solution.py:231
  53.3 0.0 copy-start
  53.3 0.0 copy-start.3
  53.4 2.5 %collective-permute-start.1 = (bf16[2,96,384]{2,1,0:T(8,128)(2,1)S(1)}, bf16[2,96,384]{2,1,0:T(8,128)(2,1)S(1)}, u32[]{:S(2)}, u32[]{:S(2)}) collective-permute-start(bf16[2,96,384]{2,1,0:T(8,128)(2,1)S(1)} %pad_maximum_fusion), channel_id=1, source_target_pairs={{0,12},{1,13},{2,14},{3,15},{4,0},{5,1},{6,2},{7,3},{8,4},{9,5},{1... | collective-permute-start | bytes 442376 | tf_op jit(solution)/shard_map/ppermute | solution.py:209
  55.9 3.8 %collective-permute-start.2 = (bf16[2,96,384]{2,1,0:T(8,128)(2,1)S(1)}, bf16[2,96,384]{2,1,0:T(8,128)(2,1)S(1)}, u32[]{:S(2)}, u32[]{:S(2)}) collective-permute-start(bf16[2,96,384]{2,1,0:T(8,128)(2,1)S(1)} %pad_maximum_fusion), channel_id=1, source_target_pairs={{0,4},{1,5},{2,6},{3,7},{4,8},{5,9},{6,10},{7,11},{8,12},{9,13},{1... | collective-permute-start | bytes 442376 | tf_op jit(solution)/shard_map/ppermute | solution.py:209
  59.7 5.4 %collective-permute-done.1 = bf16[2,96,384]{2,1,0:T(8,128)(2,1)S(1)} collective-permute-done((bf16[2,96,384]{2,1,0:T(8,128)(2,1)S(1)}, bf16[2,96,384]{2,1,0:T(8,128)(2,1)S(1)}, u32[]{:S(2)}, u32[]{:S(2)}) %collective-permute-start.1) | collective-permute-done | bytes 147488 | tf_op jit(solution)/shard_map/ppermute | solution.py:209
  65.1 0.0 collective-permute-done.2
  65.2 3.1 %collective-permute-start.4 = (bf16[6,96,384]{2,1,0:T(8,128)(2,1)S(1)}, bf16[6,96,384]{2,1,0:T(8,128)(2,1)S(1)}, u32[]{:S(2)}, u32[]{:S(2)}) collective-permute-start(bf16[6,96,384]{2,1,0:T(8,128)(2,1)S(1)} %constant_dynamic-update-slice_fusion.six_ref), channel_id=1, source_target_pairs={{0,1},{1,0},{2,3},{3,2},{4,5},{5,4},{6,7},{7,6},{8,9},{9,8},{10,11... | collective-permute-start | bytes 1327112 | tf_op jit(solution)/shard_map/ppermute | solution.py:228
  68.2 3.1 %collective-permute-start.3 = (bf16[2,96,384]{2,1,0:T(8,128)(2,1)S(1)}, bf16[2,96,384]{2,1,0:T(8,128)(2,1)S(1)}, u32[]{:S(2)}, u32[]{:S(2)}) collective-permute-start(bf16[2,96,384]{2,1,0:T(8,128)(2,1)S(1)} %collective-permute-done.1), channel_id=1, source_target_pairs={{0,12},{1,13},{2,14},{3,15},{4,0},{5,1},{6,2},{7,3},{8,4},{9,5},{1... | collective-permute-start | bytes 442376 | tf_op jit(solution)/shard_map/ppermute | solution.py:209
  71.3 0.0 copy-done.5
  71.3 0.1 reshape_reshape.3
  71.4 0.1 broadcast_in_dim_reshape.5.label_b_ref
  71.6 0.0 copy-done.8
  71.6 0.1 dynamic_slice.15.own_energy_ref
  71.7 0.1 reshape.144
  71.8 4.7 %collective-permute-done.3.last_ref = bf16[2,96,384]{2,1,0:T(8,128)(2,1)S(1)} collective-permute-done((bf16[2,96,384]{2,1,0:T(8,128)(2,1)S(1)}, bf16[2,96,384]{2,1,0:T(8,128)(2,1)S(1)}, u32[]{:S(2)}, u32[]{:S(2)}) %collective-permute-start.3) | collective-permute-done | bytes 147488 | tf_op jit(solution)/shard_map/ppermute | solution.py:209
  76.5 0.0 collective-permute-done.4.core_six_ref
  76.5 2.7 %collective-permute-start.5 = (bf16[2,96,384]{2,1,0:T(8,128)(2,1)S(1)}, bf16[2,96,384]{2,1,0:T(8,128)(2,1)S(1)}, u32[]{:S(2)}, u32[]{:S(2)}) collective-permute-start(bf16[2,96,384]{2,1,0:T(8,128)(2,1)S(1)} %collective-permute-done.3.last_ref), channel_id=1, source_target_pairs={{0,1},{1,0},{2,3},{3,2},{4,5},{5,4},{6,7},{7,6},{8,9},{9,8},{10,11... | collective-permute-start | bytes 442376 | tf_op jit(solution)/shard_map/ppermute | solution.py:228
  79.3 0.0 copy-done.7
  79.3 0.4 select_reduce_fusion
  79.7 0.1 copy.29.energy_b_ref
  79.8 0.1 reshape.146.spread_label_b_ref
  80.0 0.3 collective-permute-done.5.core_last_ref
  80.2 5.2 %all-to-all-done.2.got_ref = bf16[32,152,128]{2,1,0:T(8,128)(2,1)S(1)} async-done(((bf16[32,152,128]{2,1,0:T(8,128)(2,1)}), bf16[32,152,128]{2,1,0:T(8,128)(2,1)S(1)}, u32[]{:S(2)}, u32[]{:S(2)}) %all-to-all-start.2) | async-done | bytes 1245216 | tf_op jit(solution)/shard_map/all_to_all | solution.py:231
  85.4 0.0 copy-done
  85.4 0.0 copy-done.3
  85.4 10.5 %shard_map.104 = bf16[1600,1250]{1,0:T(8,128)(2,1)} custom-call(bf16[32,152,128]{2,1,0:T(8,128)(2,1)S(1)} %all-to-all-done.2.got_ref, bf16[4,480,128]{2,1,0:T(8,128)(2,1)S(1)} %copy-done, bf16[6,96,384]{2,1,0:T(8,128)(2,1)S(1)} %constant_dynamic-update-slice_fusion.six_ref, bf16[6,96,384]{2,1,0:T(8,128)(2,1)S(1)} %collective-permute-done.4.core_six_ref, ...), custom_call_target="tpu_custom_call" | custom-call | tf_op jit(solution)/shard_map/pallas_call | solution.py:238
  (16 shorter events, 0.2 us)
Async XLA Ops:
  0.0 20.0 %copy-start.1 = (bf16[96,1250]{1,0:T(8,128)(2,1)S(1)}, bf16[96,1250]{1,0:T(8,128)(2,1)}, u32[]{:S(2)}) copy-start(bf16[96,1250]{1,0:T(8,128)(2,1)} %amp_ref.1) | copy-start | bytes 720004
  0.0 1.0 %copy-start.2 = (bf16[50,1536]{1,0:T(8,128)(2,1)S(1)}, bf16[50,1536]{1,0:T(8,128)(2,1)}, u32[]{:S(2)}) copy-start(bf16[50,1536]{1,0:T(8,128)(2,1)} %rows_ref.1) | copy-start | bytes 460804
  1.0 40.1 %copy-start.6 = (s32[1536]{0:T(1024)S(1)}, s32[1536]{0:T(1024)}, u32[]{:S(2)}) copy-start(s32[1536]{0:T(1024)} %param.14) | copy-start | bytes 18436
  2.0 44.8 %copy-start.4 = (bf16[128,128]{1,0:T(8,128)(2,1)S(1)}, bf16[128,128]{1,0:T(8,128)(2,1)}, u32[]{:S(2)}) copy-start(bf16[128,128]{1,0:T(8,128)(2,1)} %constant.65.clone.swap_ref) | copy-start | bytes 98308
  2.0 23.3 %all-to-all-start = ((bf16[32,24,128]{2,1,0:T(8,128)(2,1)}), bf16[32,24,128]{2,1,0:T(8,128)(2,1)S(1)}, u32[]{:S(2)}, u32[]{:S(2)}) async-start(bf16[32,24,128]{2,1,0:T(8,128)(2,1)} %shard_map.100), calls=%async_computation | async-start | bytes 393216 | tf_op jit(solution)/shard_map/all_to_all | solution.py:212
  26.5 20.3 %all-to-all-start.1 = ((bf16[16,48,128]{2,1,0:T(8,128)(2,1)}), bf16[16,48,128]{2,1,0:T(8,128)(2,1)S(1)}, u32[]{:S(2)}, u32[]{:S(2)}) async-start(bf16[16,48,128]{2,1,0:T(8,128)(2,1)} %shard_map.101.own_ref), calls=%async_computation.1 | async-start | bytes 393216 | tf_op jit(solution)/shard_map/all_to_all | solution.py:216
  36.5 8.1 %collective-permute-start = (bf16[1,96,384]{2,1,0:T(8,128)(2,1)S(1)}, bf16[1,96,384]{2,1,0:T(8,128)(2,1)S(1)}, u32[]{:S(2)}, u32[]{:S(2)}) collective-permute-start(bf16[1,96,384]{2,1,0:T(8,128)(2,1)S(1)} %shard_map.102), channel_id=1, source_target_pairs={{0,14},{1,15},{2,0},{3,1},{4,2},{5,3},{6,4},{7,5},{8,6},{9,7},{10,... | collective-permute-start | bytes 221192 | tf_op jit(solution)/shard_map/ppermute | solution.py:209
  49.2 22.1 %copy-start.5 = (s32[2,80]{1,0:T(2,128)S(1)}, s32[2,80]{1,0:T(2,128)}, u32[]{:S(2)}) copy-start(s32[2,80]{1,0:T(2,128)} %param.12) | copy-start | bytes 1924
  49.2 22.3 %copy-start.8 = (f32[160]{0:T(256)S(1)}, f32[160]{0:T(256)}, u32[]{:S(2)}) copy-start(f32[160]{0:T(256)} %param.15) | copy-start | bytes 1924
  49.2 30.0 %copy-start.7 = (f32[200]{0:T(256)S(1)}, f32[200]{0:T(256)}, u32[]{:S(2)}) copy-start(f32[200]{0:T(256)} %param.16) | copy-start | bytes 2404
  49.2 36.2 %all-to-all-start.2 = ((bf16[32,152,128]{2,1,0:T(8,128)(2,1)}), bf16[32,152,128]{2,1,0:T(8,128)(2,1)S(1)}, u32[]{:S(2)}, u32[]{:S(2)}) async-start(bf16[32,152,128]{2,1,0:T(8,128)(2,1)} %shard_map.103), calls=%async_computation.2 | async-start | bytes 2490368 | tf_op jit(solution)/shard_map/all_to_all | solution.py:231
  53.3 32.1 %copy-start = (bf16[4,480,128]{2,1,0:T(8,128)(2,1)S(1)}, bf16[4,480,128]{2,1,0:T(8,128)(2,1)}, u32[]{:S(2)}) copy-start(bf16[4,480,128]{2,1,0:T(8,128)(2,1)} %constant.66.clone.turn_ref) | copy-start | bytes 1474564
  53.3 32.1 %copy-start.3 = (bf16[160,192]{1,0:T(8,128)(2,1)S(1)}, bf16[160,192]{1,0:T(8,128)(2,1)}, u32[]{:S(2)}) copy-start(bf16[160,192]{1,0:T(8,128)(2,1)} %constant.67.clone.pick_ref) | copy-start | bytes 184324
  53.4 11.7 %collective-permute-start.1 = (bf16[2,96,384]{2,1,0:T(8,128)(2,1)S(1)}, bf16[2,96,384]{2,1,0:T(8,128)(2,1)S(1)}, u32[]{:S(2)}, u32[]{:S(2)}) collective-permute-start(bf16[2,96,384]{2,1,0:T(8,128)(2,1)S(1)} %pad_maximum_fusion), channel_id=1, source_target_pairs={{0,12},{1,13},{2,14},{3,15},{4,0},{5,1},{6,2},{7,3},{8,4},{9,5},{1... | collective-permute-start | bytes 442376 | tf_op jit(solution)/shard_map/ppermute | solution.py:209
  55.9 9.2 %collective-permute-start.2 = (bf16[2,96,384]{2,1,0:T(8,128)(2,1)S(1)}, bf16[2,96,384]{2,1,0:T(8,128)(2,1)S(1)}, u32[]{:S(2)}, u32[]{:S(2)}) collective-permute-start(bf16[2,96,384]{2,1,0:T(8,128)(2,1)S(1)} %pad_maximum_fusion), channel_id=1, source_target_pairs={{0,4},{1,5},{2,6},{3,7},{4,8},{5,9},{6,10},{7,11},{8,12},{9,13},{1... | collective-permute-start | bytes 442376 | tf_op jit(solution)/shard_map/ppermute | solution.py:209
  65.2 11.3 %collective-permute-start.4 = (bf16[6,96,384]{2,1,0:T(8,128)(2,1)S(1)}, bf16[6,96,384]{2,1,0:T(8,128)(2,1)S(1)}, u32[]{:S(2)}, u32[]{:S(2)}) collective-permute-start(bf16[6,96,384]{2,1,0:T(8,128)(2,1)S(1)} %constant_dynamic-update-slice_fusion.six_ref), channel_id=1, source_target_pairs={{0,1},{1,0},{2,3},{3,2},{4,5},{5,4},{6,7},{7,6},{8,9},{9,8},{10,11... | collective-permute-start | bytes 1327112 | tf_op jit(solution)/shard_map/ppermute | solution.py:228
  68.2 8.3 %collective-permute-start.3 = (bf16[2,96,384]{2,1,0:T(8,128)(2,1)S(1)}, bf16[2,96,384]{2,1,0:T(8,128)(2,1)S(1)}, u32[]{:S(2)}, u32[]{:S(2)}) collective-permute-start(bf16[2,96,384]{2,1,0:T(8,128)(2,1)S(1)} %collective-permute-done.1), channel_id=1, source_target_pairs={{0,12},{1,13},{2,14},{3,15},{4,0},{5,1},{6,2},{7,3},{8,4},{9,5},{1... | collective-permute-start | bytes 442376 | tf_op jit(solution)/shard_map/ppermute | solution.py:209
  76.5 3.7 %collective-permute-start.5 = (bf16[2,96,384]{2,1,0:T(8,128)(2,1)S(1)}, bf16[2,96,384]{2,1,0:T(8,128)(2,1)S(1)}, u32[]{:S(2)}, u32[]{:S(2)}) collective-permute-start(bf16[2,96,384]{2,1,0:T(8,128)(2,1)S(1)} %collective-permute-done.3.last_ref), channel_id=1, source_target_pairs={{0,1},{1,0},{2,3},{3,2},{4,5},{5,4},{6,7},{7,6},{8,9},{9,8},{10,11... | collective-permute-start | bytes 442376 | tf_op jit(solution)/shard_map/ppermute | solution.py:228

commit v4 on v3

--- a/solution.py
+++ b/solution.py
@@ -16,7 +16,7 @@
 CDS = 48
 SLOTS = 384
 LANES = 128
-STEP = 5
+STEP = 2
 F32 = jnp.float32
 BF16 = jnp.bfloat16
 VMEM = pl.BlockSpec(memory_space=pltpu.VMEM)
@@ -42,11 +42,12 @@
     return jnp.sum(jnp.where(chosen, table[None, :], jnp.zeros((), table.dtype)), axis=1)
 
 
-def pack_columns(amp_ref, label_cd_ref, label_ij_ref, slot_ref, out_ref):
+def pack_columns(amp_ref, label_cd_ref, label_ij_ref, slot_ref, out_ref, place_ref):
     keep = label_cd_ref[...] == label_ij_ref[...]
     masked = jnp.where(keep, amp_ref[...].astype(F32), 0.0).astype(BF16)
     rows = lax.broadcasted_iota(jnp.int32, (SLOTS, PAIRS), 0)
     place = jnp.where(rows == slot_ref[...], 1.0, 0.0).astype(BF16)
+    place_ref[...] = place
     out_ref[0] = dot(masked, place, ((1,), (1,))).astype(BF16)
 
 
@@ -85,13 +86,13 @@
     label_cd = label_cd_ref[...]
     lane = lax.broadcasted_iota(jnp.int32, (CDS, LANES), 1)
     blocks = [jnp.zeros((CDS, LANES), F32) for _ in range(4)]
+    mirrored = dot(mirror_ref[...].reshape(16 * CDS, LANES), swap_ref[...])
     for slab in range(2):
         for odd in range(2):
             packed = jnp.zeros((CDS, LANES), F32)
             for quarter in range(4):
                 partner = 8 * slab + 2 * quarter + odd
-                mirrored = dot(mirror_ref[partner], swap_ref[...])
-                diff = own_ref[partner].astype(F32) - mirrored
+                diff = own_ref[partner].astype(F32) - mirrored[CDS * partner : CDS * partner + CDS]
                 keep = label_ab_ref[partner : partner + 1, :] == label_cd
                 packed = jnp.where(keep, diff, packed)
             first = 100 * (2 * slab + odd)
@@ -123,35 +124,36 @@
         out_ref[:, at : at + 384] = total.astype(BF16)
 
 
-def finish(got_ref, turn_ref, six_ref, core_six_ref, last_ref, core_last_ref, pick_ref, vir_ref, own_label_ref, own_energy_ref, label_b_ref,
-           spread_label_b_ref, energy_b_ref, label_cd_ref, label_ij_ref, energy_ij_ref, slot_ref, out_ref,
-           rest_ref, rows_ref, amp_ref, place_ref, left_ref):
+def finish(got_ref, turn_ref, six_ref, core_six_ref, last_ref, core_last_ref, place_ref, pick_ref, vir_ref,
+           own_label_ref, own_energy_ref, label_b_ref, spread_label_b_ref, energy_b_ref, label_cd_ref, label_ij_ref,
+           energy_ij_ref, out_ref, rest_ref, rows_ref, amp_ref, left_ref, picked_ref):
     step = pl.program_id(0)
 
     @pl.when(step == 0)
     def _():
-        turn_back(got_ref, turn_ref, rest_ref, rows_ref)
-        rows = lax.broadcasted_iota(jnp.int32, (SLOTS, PAIRS), 0)
-        place_ref[...] = jnp.where(rows == slot_ref[...], 1.0, 0.0).astype(BF16)
         six, last = (0, 1, 2, 3, 6, 7), (4, 5)
         for part, core, chips in ((six_ref, 0, six), (core_six_ref, 1, six), (last_ref, 0, last), (core_last_ref, 1, last)):
             for index, chip in enumerate(chips):
                 source = ((vir_ref[0] ^ core) + 2 * chip) & 15
                 amp_ref[pl.ds(pl.multiple_of(96 * source, 96), 96), :] = part[index]
-
-    for a in range(STEP):
-        label_a = own_label_ref[step * STEP + a]
-        for part in range(4):
-            wanted = label_cd_ref[:, 384 * part : 384 * part + 384] ^ label_a
-            own = pl.ds(pl.multiple_of(48 * (step * STEP + a), 48), 48)
-            values = rows_ref[own, 384 * part : 384 * part + 384].astype(F32)
-            for quarter in range(4):
-                keep = spread_label_b_ref[48 * quarter : 48 * quarter + 48, :] == wanted
-                at = 192 * a + 48 * quarter
-                left_ref[at : at + 48, 384 * part : 384 * part + 384] = jnp.where(keep, values, 0.0).astype(BF16)
-    total = dot(left_ref[...], amp_ref[...]).astype(BF16)
-    picked = [dot(pick_ref[...], total[192 * a : 192 * a + 192]).astype(BF16) for a in range(STEP)]
-    ladder = dot(jnp.concatenate(picked, axis=0), place_ref[...])
+        turn_back(got_ref, turn_ref, rest_ref, rows_ref)
+        for a in range(OWN):
+            label_a = own_label_ref[a]
+            for part in range(4):
+                lanes = slice(384 * part, 384 * part + 384)
+                wanted = label_cd_ref[:, lanes] ^ label_a
+                values = rows_ref[48 * a : 48 * a + 48, lanes].astype(F32)
+                for quarter in range(4):
+                    keep = spread_label_b_ref[48 * quarter : 48 * quarter + 48, :] == wanted
+                    at = 192 * a + 48 * quarter
+                    left_ref[at : at + 48, lanes] = jnp.where(keep, values, 0.0).astype(BF16)
+        total = dot(left_ref[...], amp_ref[...]).astype(BF16)
+        for a in range(OWN):
+            rows = dot(pick_ref[...], total[192 * a : 192 * a + 192]).astype(BF16)
+            picked_ref[NW * a : NW * a + NW, :] = rows
+
+    own = pl.ds(pl.multiple_of(STEP * NW * step, STEP * NW), STEP * NW)
+    ladder = dot(picked_ref[own, :], place_ref[...])
     for a in range(STEP):
         label_a = own_label_ref[step * STEP + a]
         energy_a = own_energy_ref[step * STEP + a]
@@ -202,8 +204,10 @@
     slot = ((first_occ - (occ * PAIRS) // NOCC) * 50 + second_occ % 50)[None, :]
 
     label_rows = lax.dynamic_slice_in_dim(pair_irrep, vir * 96, 96)[:, None]
-    packed_amp = call(
-        pack_columns, jax.ShapeDtypeStruct((1, 96, SLOTS), BF16), (amplitudes, label_rows, label_ij, slot)
+    packed_amp, place_columns = call(
+        pack_columns,
+        (jax.ShapeDtypeStruct((1, 96, SLOTS), BF16), jax.ShapeDtypeStruct((SLOTS, PAIRS), BF16)),
+        (amplitudes, label_rows, label_ij, slot),
     )
 
     from_chip = lambda array, k: lax.ppermute(array, "vir", [(i, (i - 2 * k) % 16) for i in range(16)])
@@ -246,6 +250,7 @@
             whole(6, 96, SLOTS),
             whole(2, 96, SLOTS),
             whole(2, 96, SLOTS),
+            whole(SLOTS, PAIRS),
             whole(NW, 192),
             scalars,
             scalars,
@@ -256,21 +261,21 @@
             whole(1, CD),
             whole(1, PAIRS),
             whole(1, PAIRS),
-            whole(1, PAIRS),
         ],
         out_specs=pl.BlockSpec((STEP * NW, PAIRS), lambda i: (i, 0)),
         scratch_shapes=[
             pltpu.VMEM((CD, LANES), BF16),
             pltpu.VMEM((480, CD), BF16),
             pltpu.VMEM((CD, SLOTS), BF16),
-            pltpu.VMEM((SLOTS, PAIRS), BF16),
-            pltpu.VMEM((STEP * 192, CD), BF16),
+            pltpu.VMEM((OWN * 192, CD), BF16),
+            pltpu.VMEM((OWN * NW, SLOTS), BF16),
         ],
         compiler_params=params(),
     )(
         gathered,
         jnp.asarray(place_table(), BF16),
         *amp_parts,
+        place_columns,
         jnp.asarray(pick_table(), BF16),
         vir.reshape(1),
         own_labels,
@@ -281,7 +286,6 @@
         pair_irrep[None, :],
         label_ij,
         energy_ij,
-        slot,
     )
 
 

time: 96.7 us -> 97.5 us (level)
  waiting for transfers between devices: 26.1 us -> 24.9 us
    all_to_all x1, waiting for transfers between devices: 5.19 us -> 4.07 us  [on_device(): lax.all_to_all(copies, 'occ', split_axis=0, concat_axis=0, tiled=True)]
  transfers between devices with their start and end apart: 9 -> 9, of which waited for: 7 -> 7; matrix products, arithmetic and copies ran while one was open for 6% -> 6% of each run, Pallas kernels for 0% -> 1%
where the time goes in v4:
time: 97.5 us; the launch traced here: 96.7 us
  starting transfers between devices  47.7 us (49%)
  waiting for transfers between devices  24.9 us (26%)
  Pallas kernels  16.6 us (17%)
  local copies, waits for them, and re-layouts  5.6 us (6%)
  other arithmetic  1.63 us (2%)
    ppermute x4, starting transfers between devices, on_device(): lax.ppermute(array, 'vir', [(i, (i - 2 * k) % 16) for i in range(16)])  14.5 us
    all_to_all x1, starting transfers between devices, on_device(): lax.all_to_all(turned, 'occ', split_axis=0, concat_axis=0, tiled=True)  13.8 us
    ppermute x4, waiting for transfers between devices, on_device(): lax.ppermute(array, 'vir', [(i, (i - 2 * k) % 16) for i in range(16)])  13.3 us
    pallas_call x1, Pallas kernels, on_device(): pl.pallas_call(finish, grid=(OWN // STEP,), out_shape=jax.ShapeDtypeStruc...  11.3 us
    all_to_all x1, starting transfers between devices, on_device(): lax.all_to_all(blocks, 'vir', split_axis=0, concat_axis=0, tiled=True)  9.96 us
    ppermute x2, starting transfers between devices, on_device(): lax.ppermute(array, 'vir', [(i, i ^ 1) for i in range(16)])  5.27 us
    pallas_call x4, Pallas kernels, call(): pl.pallas_call(kernel, out_shape=shapes, in_specs=[VMEM] * len(args), out...  5.27 us
    all_to_all x1, waiting for transfers between devices, on_device(): lax.all_to_all(turned, 'occ', split_axis=0, concat_axis=0, tiled=True)  4.72 us
  transfers between devices with their start and end apart: 9, of which 7 were waited for; matrix products, arithmetic and copies ran while one was open for 6% of the time, Pallas kernels for 1%

profile of v4, /device:TPU:1, one launch (start us, length us, event | category | flops | bytes accessed | tf_op | source)
XLA Modules:
  0.0 96.7 jit_solution(9487082383943307672)
XLA Ops:
  0.0 0.0 copy-start.1
  0.0 0.0 copy-start.2
  0.0 1.0 copy-done.2
  1.0 0.0 copy-start.6
  1.0 1.1 %shard_map.100 = bf16[32,24,128]{2,1,0:T(8,128)(2,1)} custom-call(bf16[50,1536]{1,0:T(8,128)(2,1)S(1)} %copy-done.2), custom_call_target="tpu_custom_call" | custom-call | tf_op jit(solution)/shard_map/pallas_call | solution.py:31
  2.0 0.0 copy-start.4
  2.0 13.8 %all-to-all-start = ((bf16[32,24,128]{2,1,0:T(8,128)(2,1)}), bf16[32,24,128]{2,1,0:T(8,128)(2,1)S(1)}, u32[]{:S(2)}, u32[]{:S(2)}) async-start(bf16[32,24,128]{2,1,0:T(8,128)(2,1)} %shard_map.100), calls=%async_computation | async-start | bytes 393216 | tf_op jit(solution)/shard_map/all_to_all | solution.py:216
  15.9 1.1 %select_reduce_fusion.2 = (s32[1250]{0:T(1024)S(1)}, s32[1250]{0:T(1024)S(1)}) fusion(s32[1250]{0:T(1024)S(1)} %get-tuple-element.25, s32[200]{0:T(256)} %param.13, s32[1250]{0:T(1024)S(1)} %get-tuple-element.26), kind=kLoop, calls=%fused_computation.2 | loop fusion | flops 1497500 | bytes 20800 | tf_op jit(solution)/shard_map/reduce_sum | solution.py:42
  17.0 0.8 reshape.142
  17.8 0.8 xor.42
  18.6 0.1 dynamic_slice.13.own_label_ref
  18.6 0.1 xor.39
  18.7 0.1 xor.40
  18.8 0.1 copy.23
  18.9 0.8 dynamic-slice_bitcast_fusion.1
  19.7 0.1 copy.22.label_cd_ref
  19.8 0.1 copy.24
  19.9 0.1 fusion.5.slot_ref
  20.0 0.0 copy-done.1
  20.0 0.6 shard_map.102
  20.6 4.7 %all-to-all-done.got_ref = bf16[32,24,128]{2,1,0:T(8,128)(2,1)S(1)} async-done(((bf16[32,24,128]{2,1,0:T(8,128)(2,1)}), bf16[32,24,128]{2,1,0:T(8,128)(2,1)S(1)}, u32[]{:S(2)}, u32[]{:S(2)}) %all-to-all-start) | async-done | bytes 196640 | tf_op jit(solution)/shard_map/all_to_all | solution.py:216
  25.3 1.2 %shard_map.101.own_ref = bf16[16,48,128]{2,1,0:T(8,128)(2,1)} custom-call(bf16[32,24,128]{2,1,0:T(8,128)(2,1)S(1)} %all-to-all-done.got_ref), custom_call_target="tpu_custom_call" | custom-call | tf_op jit(solution)/shard_map/pallas_call | solution.py:31
  26.5 10.0 %all-to-all-start.1 = ((bf16[16,48,128]{2,1,0:T(8,128)(2,1)}), bf16[16,48,128]{2,1,0:T(8,128)(2,1)S(1)}, u32[]{:S(2)}, u32[]{:S(2)}) async-start(bf16[16,48,128]{2,1,0:T(8,128)(2,1)} %shard_map.101.own_ref), calls=%async_computation.1 | async-start | bytes 393216 | tf_op jit(solution)/shard_map/all_to_all | solution.py:220
  36.5 4.5 %collective-permute-start = (bf16[1,96,384]{2,1,0:T(8,128)(2,1)S(1)}, bf16[1,96,384]{2,1,0:T(8,128)(2,1)S(1)}, u32[]{:S(2)}, u32[]{:S(2)}) collective-permute-start(bf16[1,96,384]{2,1,0:T(8,128)(2,1)S(1)} %get-tuple-element.15), channel_id=1, source_target_pairs={{0,14},{1,15},{2,0},{3,1},{4,2},{5,3},{6,4},{7,5},{8,6},{9,7},{10,... | collective-permute-start | bytes 221192 | tf_op jit(solution)/shard_map/ppermute | solution.py:213
  41.0 0.0 copy-done.6
  41.0 0.1 dynamic-slice_bitcast_fusion
  41.1 0.1 copy.25.label_cd_ref
  41.2 3.4 %collective-permute-done = bf16[1,96,384]{2,1,0:T(8,128)(2,1)S(1)} collective-permute-done((bf16[1,96,384]{2,1,0:T(8,128)(2,1)S(1)}, bf16[1,96,384]{2,1,0:T(8,128)(2,1)S(1)}, u32[]{:S(2)}, u32[]{:S(2)}) %collective-permute-start) | collective-permute-done | bytes 73760 | tf_op jit(solution)/shard_map/ppermute | solution.py:213
  44.7 2.2 %all-to-all-done.1.mirror_ref = bf16[16,48,128]{2,1,0:T(8,128)(2,1)S(1)} async-done(((bf16[16,48,128]{2,1,0:T(8,128)(2,1)}), bf16[16,48,128]{2,1,0:T(8,128)(2,1)S(1)}, u32[]{:S(2)}, u32[]{:S(2)}) %all-to-all-start.1) | async-done | bytes 196640 | tf_op jit(solution)/shard_map/all_to_all | solution.py:220
  46.8 0.0 copy-done.4
  46.8 2.4 %shard_map.103 = bf16[32,152,128]{2,1,0:T(8,128)(2,1)} custom-call(bf16[16,48,128]{2,1,0:T(8,128)(2,1)} %shard_map.101.own_ref, bf16[16,48,128]{2,1,0:T(8,128)(2,1)S(1)} %all-to-all-done.1.mirror_ref, bf16[128,128]{1,0:T(8,128)(2,1)S(1)} %copy-done.4, s32[16,128]{1,0:T(8,128)S(1)} %pad.8.label_ab_ref, s32[48,1]{1,0:T(8,128)S(1)} %copy.25.label_cd_ref), custom_call_target="tpu_custom_call" | custom-call | tf_op jit(solution)/shard_map/pallas_call | solution.py:31
  49.2 0.0 copy-start.5
  49.2 0.0 copy-start.8
  49.2 0.0 copy-start.7
  49.2 4.1 %all-to-all-start.2 = ((bf16[32,152,128]{2,1,0:T(8,128)(2,1)}), bf16[32,152,128]{2,1,0:T(8,128)(2,1)S(1)}, u32[]{:S(2)}, u32[]{:S(2)}) async-start(bf16[32,152,128]{2,1,0:T(8,128)(2,1)} %shard_map.103), calls=%async_computation.2 | async-start | bytes 2490368 | tf_op jit(solution)/shard_map/all_to_all | solution.py:235
  53.3 0.0 copy-start
  53.3 0.0 copy-start.3
  53.3 2.5 %collective-permute-start.1 = (bf16[2,96,384]{2,1,0:T(8,128)(2,1)S(1)}, bf16[2,96,384]{2,1,0:T(8,128)(2,1)}, u32[]{:S(2)}, u32[]{:S(2)}) collective-permute-start(bf16[2,96,384]{2,1,0:T(8,128)(2,1)S(1)} %pad_maximum_fusion), channel_id=1, source_target_pairs={{0,12},{1,13},{2,14},{3,15},{4,0},{5,1},{6,2},{7,3},{8,4},{9,5},{1... | collective-permute-start | bytes 442376 | tf_op jit(solution)/shard_map/ppermute | solution.py:213
  55.9 3.8 %collective-permute-start.2 = (bf16[2,96,384]{2,1,0:T(8,128)(2,1)S(1)}, bf16[2,96,384]{2,1,0:T(8,128)(2,1)S(1)}, u32[]{:S(2)}, u32[]{:S(2)}) collective-permute-start(bf16[2,96,384]{2,1,0:T(8,128)(2,1)S(1)} %pad_maximum_fusion), channel_id=1, source_target_pairs={{0,4},{1,5},{2,6},{3,7},{4,8},{5,9},{6,10},{7,11},{8,12},{9,13},{1... | collective-permute-start | bytes 442376 | tf_op jit(solution)/shard_map/ppermute | solution.py:213
  59.7 5.5 %collective-permute-done.1 = bf16[2,96,384]{2,1,0:T(8,128)(2,1)} collective-permute-done((bf16[2,96,384]{2,1,0:T(8,128)(2,1)S(1)}, bf16[2,96,384]{2,1,0:T(8,128)(2,1)}, u32[]{:S(2)}, u32[]{:S(2)}) %collective-permute-start.1) | collective-permute-done | bytes 147488 | tf_op jit(solution)/shard_map/ppermute | solution.py:213
  65.1 0.9 constant_dynamic-update-slice_fusion.1
  66.1 0.0 collective-permute-done.2
  66.1 2.5 %collective-permute-start.4 = (bf16[6,96,384]{2,1,0:T(8,128)(2,1)S(1)}, bf16[6,96,384]{2,1,0:T(8,128)(2,1)}, u32[]{:S(2)}, u32[]{:S(2)}) collective-permute-start(bf16[6,96,384]{2,1,0:T(8,128)(2,1)S(1)} %constant_dynamic-update-slice_fusion.six_ref), channel_id=1, source_target_pairs={{0,1},{1,0},{2,3},{3,2},{4,5},{5,4},{6,7},{7,6},{8,9},{9,8},{10,11... | collective-permute-start | bytes 1327112 | tf_op jit(solution)/shard_map/ppermute | solution.py:232
  68.6 3.7 %collective-permute-start.3 = (bf16[2,96,384]{2,1,0:T(8,128)(2,1)}, bf16[2,96,384]{2,1,0:T(8,128)(2,1)}, u32[]{:S(2)}, u32[]{:S(2)}) collective-permute-start(bf16[2,96,384]{2,1,0:T(8,128)(2,1)} %collective-permute-done.1), channel_id=1, source_target_pairs={{0,12},{1,13},{2,14},{3,15},{4,0},{5,1},{6,2},{7,3},{8,4},{9,5},{1... | collective-permute-start | bytes 442376 | tf_op jit(solution)/shard_map/ppermute | solution.py:213
  72.3 0.0 copy-done.5
  72.3 0.1 reshape_reshape.3
  72.4 0.1 broadcast_in_dim_reshape.5.label_b_ref
  72.5 0.0 copy-done.8
  72.5 0.1 dynamic_slice.15.own_energy_ref
  72.6 0.1 reshape.144
  72.7 4.4 %collective-permute-done.3.last_ref = bf16[2,96,384]{2,1,0:T(8,128)(2,1)} collective-permute-done((bf16[2,96,384]{2,1,0:T(8,128)(2,1)}, bf16[2,96,384]{2,1,0:T(8,128)(2,1)}, u32[]{:S(2)}, u32[]{:S(2)}) %collective-permute-start.3) | collective-permute-done | bytes 147488 | tf_op jit(solution)/shard_map/ppermute | solution.py:213
  77.2 0.0 collective-permute-done.4.core_six_ref
  77.2 2.8 %collective-permute-start.5 = (bf16[2,96,384]{2,1,0:T(8,128)(2,1)}, bf16[2,96,384]{2,1,0:T(8,128)(2,1)}, u32[]{:S(2)}, u32[]{:S(2)}) collective-permute-start(bf16[2,96,384]{2,1,0:T(8,128)(2,1)} %collective-permute-done.3.last_ref), channel_id=1, source_target_pairs={{0,1},{1,0},{2,3},{3,2},{4,5},{5,4},{6,7},{7,6},{8,9},{9,8},{10,11... | collective-permute-start | bytes 442376 | tf_op jit(solution)/shard_map/ppermute | solution.py:232
  80.0 0.0 copy-done.7
  80.0 0.4 select_reduce_fusion
  80.4 0.1 copy.29.energy_b_ref
  80.5 0.1 reshape.146.spread_label_b_ref
  80.7 0.6 collective-permute-done.5.core_last_ref
  81.3 4.1 %all-to-all-done.2.got_ref = bf16[32,152,128]{2,1,0:T(8,128)(2,1)S(1)} async-done(((bf16[32,152,128]{2,1,0:T(8,128)(2,1)}), bf16[32,152,128]{2,1,0:T(8,128)(2,1)S(1)}, u32[]{:S(2)}, u32[]{:S(2)}) %all-to-all-start.2) | async-done | bytes 1245216 | tf_op jit(solution)/shard_map/all_to_all | solution.py:235
  85.4 0.0 copy-done
  85.4 0.0 copy-done.3
  85.4 11.3 %shard_map.104 = bf16[1600,1250]{1,0:T(8,128)(2,1)} custom-call(bf16[32,152,128]{2,1,0:T(8,128)(2,1)S(1)} %all-to-all-done.2.got_ref, bf16[4,480,128]{2,1,0:T(8,128)(2,1)S(1)} %copy-done, bf16[6,96,384]{2,1,0:T(8,128)(2,1)S(1)} %constant_dynamic-update-slice_fusion.six_ref, bf16[6,96,384]{2,1,0:T(8,128)(2,1)} %collective-permute-done.4.core_six_ref, ...), custom_call_target="tpu_custom_call" | custom-call | tf_op jit(solution)/shard_map/pallas_call | solution.py:242
  (15 shorter events, 0.1 us)
Async XLA Ops:
  0.0 20.0 %copy-start.1 = (bf16[96,1250]{1,0:T(8,128)(2,1)S(1)}, bf16[96,1250]{1,0:T(8,128)(2,1)}, u32[]{:S(2)}) copy-start(bf16[96,1250]{1,0:T(8,128)(2,1)} %amp_ref.1) | copy-start | bytes 720004
  0.0 1.0 copy-start.2
  1.0 40.1 %copy-start.6 = (s32[1536]{0:T(1024)S(1)}, s32[1536]{0:T(1024)}, u32[]{:S(2)}) copy-start(s32[1536]{0:T(1024)} %param.14) | copy-start | bytes 18436
  2.0 44.8 %copy-start.4 = (bf16[128,128]{1,0:T(8,128)(2,1)S(1)}, bf16[128,128]{1,0:T(8,128)(2,1)}, u32[]{:S(2)}) copy-start(bf16[128,128]{1,0:T(8,128)(2,1)} %constant.65.clone.swap_ref) | copy-start | bytes 98308
  2.0 23.3 %all-to-all-start = ((bf16[32,24,128]{2,1,0:T(8,128)(2,1)}), bf16[32,24,128]{2,1,0:T(8,128)(2,1)S(1)}, u32[]{:S(2)}, u32[]{:S(2)}) async-start(bf16[32,24,128]{2,1,0:T(8,128)(2,1)} %shard_map.100), calls=%async_computation | async-start | bytes 393216 | tf_op jit(solution)/shard_map/all_to_all | solution.py:216
  26.5 20.3 %all-to-all-start.1 = ((bf16[16,48,128]{2,1,0:T(8,128)(2,1)}), bf16[16,48,128]{2,1,0:T(8,128)(2,1)S(1)}, u32[]{:S(2)}, u32[]{:S(2)}) async-start(bf16[16,48,128]{2,1,0:T(8,128)(2,1)} %shard_map.101.own_ref), calls=%async_computation.1 | async-start | bytes 393216 | tf_op jit(solution)/shard_map/all_to_all | solution.py:220
  36.5 8.1 %collective-permute-start = (bf16[1,96,384]{2,1,0:T(8,128)(2,1)S(1)}, bf16[1,96,384]{2,1,0:T(8,128)(2,1)S(1)}, u32[]{:S(2)}, u32[]{:S(2)}) collective-permute-start(bf16[1,96,384]{2,1,0:T(8,128)(2,1)S(1)} %get-tuple-element.15), channel_id=1, source_target_pairs={{0,14},{1,15},{2,0},{3,1},{4,2},{5,3},{6,4},{7,5},{8,6},{9,7},{10,... | collective-permute-start | bytes 221192 | tf_op jit(solution)/shard_map/ppermute | solution.py:213
  49.2 23.1 %copy-start.5 = (s32[2,80]{1,0:T(2,128)S(1)}, s32[2,80]{1,0:T(2,128)}, u32[]{:S(2)}) copy-start(s32[2,80]{1,0:T(2,128)} %param.12) | copy-start | bytes 1924
  49.2 23.4 %copy-start.8 = (f32[160]{0:T(256)S(1)}, f32[160]{0:T(256)}, u32[]{:S(2)}) copy-start(f32[160]{0:T(256)} %param.15) | copy-start | bytes 1924
  49.2 30.8 %copy-start.7 = (f32[200]{0:T(256)S(1)}, f32[200]{0:T(256)}, u32[]{:S(2)}) copy-start(f32[200]{0:T(256)} %param.16) | copy-start | bytes 2404
  49.2 36.2 %all-to-all-start.2 = ((bf16[32,152,128]{2,1,0:T(8,128)(2,1)}), bf16[32,152,128]{2,1,0:T(8,128)(2,1)S(1)}, u32[]{:S(2)}, u32[]{:S(2)}) async-start(bf16[32,152,128]{2,1,0:T(8,128)(2,1)} %shard_map.103), calls=%async_computation.2 | async-start | bytes 2490368 | tf_op jit(solution)/shard_map/all_to_all | solution.py:235
  53.3 32.1 %copy-start = (bf16[4,480,128]{2,1,0:T(8,128)(2,1)S(1)}, bf16[4,480,128]{2,1,0:T(8,128)(2,1)}, u32[]{:S(2)}) copy-start(bf16[4,480,128]{2,1,0:T(8,128)(2,1)} %constant.66.clone.turn_ref) | copy-start | bytes 1474564
  53.3 32.1 %copy-start.3 = (bf16[160,192]{1,0:T(8,128)(2,1)S(1)}, bf16[160,192]{1,0:T(8,128)(2,1)}, u32[]{:S(2)}) copy-start(bf16[160,192]{1,0:T(8,128)(2,1)} %constant.67.clone.pick_ref) | copy-start | bytes 184324
  53.3 11.8 %collective-permute-start.1 = (bf16[2,96,384]{2,1,0:T(8,128)(2,1)S(1)}, bf16[2,96,384]{2,1,0:T(8,128)(2,1)}, u32[]{:S(2)}, u32[]{:S(2)}) collective-permute-start(bf16[2,96,384]{2,1,0:T(8,128)(2,1)S(1)} %pad_maximum_fusion), channel_id=1, source_target_pairs={{0,12},{1,13},{2,14},{3,15},{4,0},{5,1},{6,2},{7,3},{8,4},{9,5},{1... | collective-permute-start | bytes 442376 | tf_op jit(solution)/shard_map/ppermute | solution.py:213
  55.9 10.2 %collective-permute-start.2 = (bf16[2,96,384]{2,1,0:T(8,128)(2,1)S(1)}, bf16[2,96,384]{2,1,0:T(8,128)(2,1)S(1)}, u32[]{:S(2)}, u32[]{:S(2)}) collective-permute-start(bf16[2,96,384]{2,1,0:T(8,128)(2,1)S(1)} %pad_maximum_fusion), channel_id=1, source_target_pairs={{0,4},{1,5},{2,6},{3,7},{4,8},{5,9},{6,10},{7,11},{8,12},{9,13},{1... | collective-permute-start | bytes 442376 | tf_op jit(solution)/shard_map/ppermute | solution.py:213
  66.1 11.1 %collective-permute-start.4 = (bf16[6,96,384]{2,1,0:T(8,128)(2,1)S(1)}, bf16[6,96,384]{2,1,0:T(8,128)(2,1)}, u32[]{:S(2)}, u32[]{:S(2)}) collective-permute-start(bf16[6,96,384]{2,1,0:T(8,128)(2,1)S(1)} %constant_dynamic-update-slice_fusion.six_ref), channel_id=1, source_target_pairs={{0,1},{1,0},{2,3},{3,2},{4,5},{5,4},{6,7},{7,6},{8,9},{9,8},{10,11... | collective-permute-start | bytes 1327112 | tf_op jit(solution)/shard_map/ppermute | solution.py:232
  68.6 8.6 %collective-permute-start.3 = (bf16[2,96,384]{2,1,0:T(8,128)(2,1)}, bf16[2,96,384]{2,1,0:T(8,128)(2,1)}, u32[]{:S(2)}, u32[]{:S(2)}) collective-permute-start(bf16[2,96,384]{2,1,0:T(8,128)(2,1)} %collective-permute-done.1), channel_id=1, source_target_pairs={{0,12},{1,13},{2,14},{3,15},{4,0},{5,1},{6,2},{7,3},{8,4},{9,5},{1... | collective-permute-start | bytes 442376 | tf_op jit(solution)/shard_map/ppermute | solution.py:213
  77.2 4.1 %collective-permute-start.5 = (bf16[2,96,384]{2,1,0:T(8,128)(2,1)}, bf16[2,96,384]{2,1,0:T(8,128)(2,1)}, u32[]{:S(2)}, u32[]{:S(2)}) collective-permute-start(bf16[2,96,384]{2,1,0:T(8,128)(2,1)} %collective-permute-done.3.last_ref), channel_id=1, source_target_pairs={{0,1},{1,0},{2,3},{3,2},{4,5},{5,4},{6,7},{7,6},{8,9},{9,8},{10,11... | collective-permute-start | bytes 442376 | tf_op jit(solution)/shard_map/ppermute | solution.py:232

commit v5 on v3

--- a/solution.py
+++ b/solution.py
@@ -42,11 +42,12 @@
     return jnp.sum(jnp.where(chosen, table[None, :], jnp.zeros((), table.dtype)), axis=1)
 
 
-def pack_columns(amp_ref, label_cd_ref, label_ij_ref, slot_ref, out_ref):
+def pack_columns(amp_ref, label_cd_ref, label_ij_ref, slot_ref, out_ref, place_ref):
     keep = label_cd_ref[...] == label_ij_ref[...]
     masked = jnp.where(keep, amp_ref[...].astype(F32), 0.0).astype(BF16)
     rows = lax.broadcasted_iota(jnp.int32, (SLOTS, PAIRS), 0)
     place = jnp.where(rows == slot_ref[...], 1.0, 0.0).astype(BF16)
+    place_ref[...] = place
     out_ref[0] = dot(masked, place, ((1,), (1,))).astype(BF16)
 
 
@@ -85,13 +86,13 @@
     label_cd = label_cd_ref[...]
     lane = lax.broadcasted_iota(jnp.int32, (CDS, LANES), 1)
     blocks = [jnp.zeros((CDS, LANES), F32) for _ in range(4)]
+    mirrored = dot(mirror_ref[...].reshape(16 * CDS, LANES), swap_ref[...])
     for slab in range(2):
         for odd in range(2):
             packed = jnp.zeros((CDS, LANES), F32)
             for quarter in range(4):
                 partner = 8 * slab + 2 * quarter + odd
-                mirrored = dot(mirror_ref[partner], swap_ref[...])
-                diff = own_ref[partner].astype(F32) - mirrored
+                diff = own_ref[partner].astype(F32) - mirrored[CDS * partner : CDS * partner + CDS]
                 keep = label_ab_ref[partner : partner + 1, :] == label_cd
                 packed = jnp.where(keep, diff, packed)
             first = 100 * (2 * slab + odd)
@@ -123,18 +124,16 @@
         out_ref[:, at : at + 384] = total.astype(BF16)
 
 
-def finish(got_ref, turn_ref, six_ref, core_six_ref, last_ref, core_last_ref, pick_ref, vir_ref, own_label_ref, own_energy_ref, label_b_ref,
-           spread_label_b_ref, energy_b_ref, label_cd_ref, label_ij_ref, energy_ij_ref, slot_ref, out_ref,
-           rest_ref, rows_ref, amp_ref, place_ref, left_ref):
+def finish(got_ref, turn_ref, pair_ref, core_pair_ref, most_ref, core_most_ref, place_ref, pick_ref, vir_ref, own_label_ref, own_energy_ref, label_b_ref,
+           spread_label_b_ref, energy_b_ref, label_cd_ref, label_ij_ref, energy_ij_ref, out_ref,
+           rest_ref, rows_ref, amp_ref, left_ref):
     step = pl.program_id(0)
 
     @pl.when(step == 0)
     def _():
         turn_back(got_ref, turn_ref, rest_ref, rows_ref)
-        rows = lax.broadcasted_iota(jnp.int32, (SLOTS, PAIRS), 0)
-        place_ref[...] = jnp.where(rows == slot_ref[...], 1.0, 0.0).astype(BF16)
-        six, last = (0, 1, 2, 3, 6, 7), (4, 5)
-        for part, core, chips in ((six_ref, 0, six), (core_six_ref, 1, six), (last_ref, 0, last), (core_last_ref, 1, last)):
+        pair, most = (0, 1), (2, 3, 6, 7, 4, 5)
+        for part, core, chips in ((pair_ref, 0, pair), (core_pair_ref, 1, pair), (most_ref, 0, most), (core_most_ref, 1, most)):
             for index, chip in enumerate(chips):
                 source = ((vir_ref[0] ^ core) + 2 * chip) & 15
                 amp_ref[pl.ds(pl.multiple_of(96 * source, 96), 96), :] = part[index]
@@ -202,8 +201,10 @@
     slot = ((first_occ - (occ * PAIRS) // NOCC) * 50 + second_occ % 50)[None, :]
 
     label_rows = lax.dynamic_slice_in_dim(pair_irrep, vir * 96, 96)[:, None]
-    packed_amp = call(
-        pack_columns, jax.ShapeDtypeStruct((1, 96, SLOTS), BF16), (amplitudes, label_rows, label_ij, slot)
+    packed_amp, place_columns = call(
+        pack_columns,
+        (jax.ShapeDtypeStruct((1, 96, SLOTS), BF16), jax.ShapeDtypeStruct((SLOTS, PAIRS), BF16)),
+        (amplitudes, label_rows, label_ij, slot),
     )
 
     from_chip = lambda array, k: lax.ppermute(array, "vir", [(i, (i - 2 * k) % 16) for i in range(16)])
@@ -223,11 +224,12 @@
         (blocks, mirror, jnp.asarray(swap_table(), BF16), block_labels, label_cds),
     )
     copies, amp_pair = lax.optimization_barrier((copies, amp_pair))
-    amp_above = from_chip(amp_pair, 2)
-    amp_six = jnp.concatenate([amp_pair, amp_above, from_chip(amp_pair, 6)], axis=0)
     from_core = lambda array: lax.ppermute(array, "vir", [(i, i ^ 1) for i in range(16)])
-    amp_last, core_six = lax.optimization_barrier((from_chip(amp_above, 2), from_core(amp_six)))
-    amp_parts = (amp_six, core_six, amp_last, from_core(amp_last))
+    amp_above, amp_below, core_pair = lax.optimization_barrier(
+        (from_chip(amp_pair, 2), from_chip(amp_pair, 6), from_core(amp_pair))
+    )
+    amp_rest = jnp.concatenate([amp_above, amp_below, from_chip(amp_above, 2)], axis=0)
+    amp_parts = (amp_pair, core_pair, amp_rest, from_core(amp_rest))
     gathered = lax.all_to_all(copies, "occ", split_axis=0, concat_axis=0, tiled=True)
 
     spread_labels = jnp.pad(
@@ -242,10 +244,11 @@
         in_specs=[
             whole(32, 152, LANES),
             whole(4, 480, LANES),
+            whole(2, 96, SLOTS),
+            whole(2, 96, SLOTS),
             whole(6, 96, SLOTS),
             whole(6, 96, SLOTS),
-            whole(2, 96, SLOTS),
-            whole(2, 96, SLOTS),
+            whole(SLOTS, PAIRS),
             whole(NW, 192),
             scalars,
             scalars,
@@ -256,14 +259,12 @@
             whole(1, CD),
             whole(1, PAIRS),
             whole(1, PAIRS),
-            whole(1, PAIRS),
         ],
         out_specs=pl.BlockSpec((STEP * NW, PAIRS), lambda i: (i, 0)),
         scratch_shapes=[
             pltpu.VMEM((CD, LANES), BF16),
             pltpu.VMEM((480, CD), BF16),
             pltpu.VMEM((CD, SLOTS), BF16),
-            pltpu.VMEM((SLOTS, PAIRS), BF16),
             pltpu.VMEM((STEP * 192, CD), BF16),
         ],
         compiler_params=params(),
@@ -271,6 +272,7 @@
         gathered,
         jnp.asarray(place_table(), BF16),
         *amp_parts,
+        place_columns,
         jnp.asarray(pick_table(), BF16),
         vir.reshape(1),
         own_labels,
@@ -281,7 +283,6 @@
         pair_irrep[None, :],
         label_ij,
         energy_ij,
-        slot,
     )
 
 

time: 96.7 us -> 99.7 us (1.031)
  local copies, waits for them, and re-layouts: 4.69 us -> 8.63 us
  waiting for transfers between devices: 26.1 us -> 23.2 us
  starting transfers between devices: 47.6 us -> 49.2 us
    all_to_all x1, waiting for transfers between devices: 5.19 us -> 0.01 us  [on_device(): lax.all_to_all(copies, 'occ', split_axis=0, concat_axis=0, tiled=True)]
    unnamed x20 -> x26, local copies, waits for them, and re-layouts: 1.04 us -> 4.35 us
    ppermute x4, starting transfers between devices: 13.9 us -> 16.9 us  [on_device(): lax.ppermute(array, 'vir', [(i, (i - 2 * k) % 16) for i in range(16)])]
    ppermute x4, waiting for transfers between devices: 13.6 us -> 16.3 us  [on_device(): lax.ppermute(array, 'vir', [(i, (i - 2 * k) % 16) for i in range(16)])]
    ppermute x2, starting transfers between devices: 5.81 us -> 4.47 us  [on_device(): lax.ppermute(array, 'vir', [(i, i ^ 1) for i in range(16)])]
  transfers between devices with their start and end apart: 9 -> 9, of which waited for: 7 -> 6; matrix products, arithmetic and copies ran while one was open for 6% -> 6% of each run, Pallas kernels for 0% -> 1%
where the time goes in v5:
time: 99.7 us; the launch traced here: 98.9 us
  starting transfers between devices  49.2 us (49%)
  waiting for transfers between devices  23.2 us (23%)
  Pallas kernels  15.9 us (16%)
  local copies, waits for them, and re-layouts  8.63 us (9%)
  other arithmetic  1.63 us (2%)
    ppermute x4, starting transfers between devices, on_device(): lax.ppermute(array, 'vir', [(i, (i - 2 * k) % 16) for i in range(16)])  16.9 us
    ppermute x4, waiting for transfers between devices, on_device(): lax.ppermute(array, 'vir', [(i, (i - 2 * k) % 16) for i in range(16)])  16.3 us
    all_to_all x1, starting transfers between devices, on_device(): lax.all_to_all(turned, 'occ', split_axis=0, concat_axis=0, tiled=True)  13.8 us
    pallas_call x1, Pallas kernels, on_device(): pl.pallas_call(finish, grid=(OWN // STEP,), out_shape=jax.ShapeDtypeStruc...  10.6 us
    all_to_all x1, starting transfers between devices, on_device(): lax.all_to_all(blocks, 'vir', split_axis=0, concat_axis=0, tiled=True)  9.96 us
    pallas_call x4, Pallas kernels, call(): pl.pallas_call(kernel, out_shape=shapes, in_specs=[VMEM] * len(args), out...  5.26 us
    all_to_all x1, waiting for transfers between devices, on_device(): lax.all_to_all(turned, 'occ', split_axis=0, concat_axis=0, tiled=True)  4.72 us
    ppermute x2, starting transfers between devices, on_device(): lax.ppermute(array, 'vir', [(i, i ^ 1) for i in range(16)])  4.47 us
  transfers between devices with their start and end apart: 9, of which 6 were waited for; matrix products, arithmetic and copies ran while one was open for 6% of the time, Pallas kernels for 1%

profile of v5, /device:TPU:1, one launch (start us, length us, event | category | flops | bytes accessed | tf_op | source)
XLA Modules:
  0.0 98.9 jit_solution(4261469789502681045)
XLA Ops:
  0.0 0.0 copy-start.2
  0.0 0.0 copy-start.3
  0.0 1.0 copy-done.3
  1.0 0.0 copy-start.9
  1.0 1.1 %shard_map.100 = bf16[32,24,128]{2,1,0:T(8,128)(2,1)} custom-call(bf16[50,1536]{1,0:T(8,128)(2,1)S(1)} %copy-done.3), custom_call_target="tpu_custom_call" | custom-call | tf_op jit(solution)/shard_map/pallas_call | solution.py:31
  2.0 0.0 copy-start.7
  2.0 13.8 %all-to-all-start = ((bf16[32,24,128]{2,1,0:T(8,128)(2,1)}), bf16[32,24,128]{2,1,0:T(8,128)(2,1)S(1)}, u32[]{:S(2)}, u32[]{:S(2)}) async-start(bf16[32,24,128]{2,1,0:T(8,128)(2,1)} %shard_map.100), calls=%async_computation | async-start | bytes 393216 | tf_op jit(solution)/shard_map/all_to_all | solution.py:213
  15.9 1.1 %select_reduce_fusion.2 = (s32[1250]{0:T(1024)S(1)}, s32[1250]{0:T(1024)S(1)}) fusion(s32[1250]{0:T(1024)S(1)} %get-tuple-element.27, s32[200]{0:T(256)} %param.13, s32[1250]{0:T(1024)S(1)} %get-tuple-element.28), kind=kLoop, calls=%fused_computation.2 | loop fusion | flops 1497500 | bytes 20800 | tf_op jit(solution)/shard_map/reduce_sum | solution.py:42
  17.0 0.8 reshape.142
  17.8 0.8 xor.42
  18.6 0.1 dynamic_slice.13.own_label_ref
  18.6 0.1 xor.39
  18.7 0.1 xor.40
  18.8 0.1 copy.23
  18.9 0.8 dynamic-slice_bitcast_fusion.1
  19.7 0.1 copy.22.label_cd_ref
  19.8 0.1 copy.24
  19.9 0.1 fusion.5.slot_ref
  20.0 0.0 copy-done.2
  20.0 0.6 shard_map.102
  20.6 4.7 %all-to-all-done.got_ref = bf16[32,24,128]{2,1,0:T(8,128)(2,1)S(1)} async-done(((bf16[32,24,128]{2,1,0:T(8,128)(2,1)}), bf16[32,24,128]{2,1,0:T(8,128)(2,1)S(1)}, u32[]{:S(2)}, u32[]{:S(2)}) %all-to-all-start) | async-done | bytes 196640 | tf_op jit(solution)/shard_map/all_to_all | solution.py:213
  25.3 1.2 %shard_map.101.own_ref = bf16[16,48,128]{2,1,0:T(8,128)(2,1)} custom-call(bf16[32,24,128]{2,1,0:T(8,128)(2,1)S(1)} %all-to-all-done.got_ref), custom_call_target="tpu_custom_call" | custom-call | tf_op jit(solution)/shard_map/pallas_call | solution.py:31
  26.5 10.0 %all-to-all-start.1 = ((bf16[16,48,128]{2,1,0:T(8,128)(2,1)}), bf16[16,48,128]{2,1,0:T(8,128)(2,1)S(1)}, u32[]{:S(2)}, u32[]{:S(2)}) async-start(bf16[16,48,128]{2,1,0:T(8,128)(2,1)} %shard_map.101.own_ref), calls=%async_computation.1 | async-start | bytes 393216 | tf_op jit(solution)/shard_map/all_to_all | solution.py:217
  36.5 4.5 %collective-permute-start = (bf16[1,96,384]{2,1,0:T(8,128)(2,1)S(1)}, bf16[1,96,384]{2,1,0:T(8,128)(2,1)S(1)}, u32[]{:S(2)}, u32[]{:S(2)}) collective-permute-start(bf16[1,96,384]{2,1,0:T(8,128)(2,1)S(1)} %get-tuple-element.16), channel_id=1, source_target_pairs={{0,14},{1,15},{2,0},{3,1},{4,2},{5,3},{6,4},{7,5},{8,6},{9,7},{10,... | collective-permute-start | bytes 221192 | tf_op jit(solution)/shard_map/ppermute | solution.py:210
  41.0 0.0 copy-done.9
  41.0 0.1 dynamic-slice_bitcast_fusion
  41.1 0.1 copy.25.label_cd_ref
  41.2 3.4 %collective-permute-done = bf16[1,96,384]{2,1,0:T(8,128)(2,1)S(1)} collective-permute-done((bf16[1,96,384]{2,1,0:T(8,128)(2,1)S(1)}, bf16[1,96,384]{2,1,0:T(8,128)(2,1)S(1)}, u32[]{:S(2)}, u32[]{:S(2)}) %collective-permute-start) | collective-permute-done | bytes 73760 | tf_op jit(solution)/shard_map/ppermute | solution.py:210
  44.7 2.2 %all-to-all-done.1.mirror_ref = bf16[16,48,128]{2,1,0:T(8,128)(2,1)S(1)} async-done(((bf16[16,48,128]{2,1,0:T(8,128)(2,1)}), bf16[16,48,128]{2,1,0:T(8,128)(2,1)S(1)}, u32[]{:S(2)}, u32[]{:S(2)}) %all-to-all-start.1) | async-done | bytes 196640 | tf_op jit(solution)/shard_map/all_to_all | solution.py:217
  46.8 0.0 copy-done.7
  46.8 2.3 %shard_map.103 = bf16[32,152,128]{2,1,0:T(8,128)(2,1)} custom-call(bf16[16,48,128]{2,1,0:T(8,128)(2,1)} %shard_map.101.own_ref, bf16[16,48,128]{2,1,0:T(8,128)(2,1)S(1)} %all-to-all-done.1.mirror_ref, bf16[128,128]{1,0:T(8,128)(2,1)S(1)} %copy-done.7, s32[16,128]{1,0:T(8,128)S(1)} %pad.8.label_ab_ref, s32[48,1]{1,0:T(8,128)S(1)} %copy.25.label_cd_ref), custom_call_target="tpu_custom_call" | custom-call | tf_op jit(solution)/shard_map/pallas_call | solution.py:31
  49.2 0.0 copy-start.8
  49.2 0.0 copy-start.11
  49.2 4.1 %all-to-all-start.2 = ((bf16[32,152,128]{2,1,0:T(8,128)(2,1)}), bf16[32,152,128]{2,1,0:T(8,128)(2,1)S(1)}, u32[]{:S(2)}, u32[]{:S(2)}) async-start(bf16[32,152,128]{2,1,0:T(8,128)(2,1)} %shard_map.103), calls=%async_computation.2 | async-start | bytes 2490368 | tf_op jit(solution)/shard_map/all_to_all | solution.py:233
  53.3 0.0 copy-start
  53.3 2.1 %collective-permute-start.3 = (bf16[2,96,384]{2,1,0:T(8,128)(2,1)S(1)}, bf16[2,96,384]{2,1,0:T(8,128)(2,1)S(1)}, u32[]{:S(2)}, u32[]{:S(2)}) collective-permute-start(bf16[2,96,384]{2,1,0:T(8,128)(2,1)S(1)} %pad_maximum_fusion.pair_ref), channel_id=1, source_target_pairs={{0,1},{1,0},{2,3},{3,2},{4,5},{5,4},{6,7},{7,6},{8,9},{9,8},{10,11... | collective-permute-start | bytes 442376 | tf_op jit(solution)/shard_map/ppermute | solution.py:227
  55.3 2.9 %collective-permute-start.2 = (bf16[2,96,384]{2,1,0:T(8,128)(2,1)S(1)}, bf16[2,96,384]{2,1,0:T(8,128)(2,1)S(1)}, u32[]{:S(2)}, u32[]{:S(2)}) collective-permute-start(bf16[2,96,384]{2,1,0:T(8,128)(2,1)S(1)} %pad_maximum_fusion.pair_ref), channel_id=1, source_target_pairs={{0,4},{1,5},{2,6},{3,7},{4,8},{5,9},{6,10},{7,11},{8,12},{9,13},{1... | collective-permute-start | bytes 442376 | tf_op jit(solution)/shard_map/ppermute | solution.py:210
  58.2 4.5 %collective-permute-start.1 = (bf16[2,96,384]{2,1,0:T(8,128)(2,1)S(1)}, bf16[2,96,384]{2,1,0:T(8,128)(2,1)S(1)}, u32[]{:S(2)}, u32[]{:S(2)}) collective-permute-start(bf16[2,96,384]{2,1,0:T(8,128)(2,1)S(1)} %pad_maximum_fusion.pair_ref), channel_id=1, source_target_pairs={{0,12},{1,13},{2,14},{3,15},{4,0},{5,1},{6,2},{7,3},{8,4},{9,5},{1... | collective-permute-start | bytes 442376 | tf_op jit(solution)/shard_map/ppermute | solution.py:210
  62.7 0.0 collective-permute-done.3.core_pair_ref
  62.8 0.0 copy-start.4
  62.8 0.6 copy-done.4
  63.4 2.0 %collective-permute-done.2 = bf16[2,96,384]{2,1,0:T(8,128)(2,1)S(1)} collective-permute-done((bf16[2,96,384]{2,1,0:T(8,128)(2,1)S(1)}, bf16[2,96,384]{2,1,0:T(8,128)(2,1)S(1)}, u32[]{:S(2)}, u32[]{:S(2)}) %collective-permute-start.2) | collective-permute-done | bytes 147488 | tf_op jit(solution)/shard_map/ppermute | solution.py:210
  65.4 4.1 %collective-permute-done.1 = bf16[2,96,384]{2,1,0:T(8,128)(2,1)S(1)} collective-permute-done((bf16[2,96,384]{2,1,0:T(8,128)(2,1)S(1)}, bf16[2,96,384]{2,1,0:T(8,128)(2,1)S(1)}, u32[]{:S(2)}, u32[]{:S(2)}) %collective-permute-start.1) | collective-permute-done | bytes 147488 | tf_op jit(solution)/shard_map/ppermute | solution.py:210
  69.6 5.0 %collective-permute-start.4 = (bf16[2,96,384]{2,1,0:T(8,128)(2,1)S(1)}, bf16[2,96,384]{2,1,0:T(8,128)(2,1)S(1)}, u32[]{:S(2)}, u32[]{:S(2)}) collective-permute-start(bf16[2,96,384]{2,1,0:T(8,128)(2,1)S(1)} %collective-permute-done.1), channel_id=1, source_target_pairs={{0,12},{1,13},{2,14},{3,15},{4,0},{5,1},{6,2},{7,3},{8,4},{9,5},{1... | collective-permute-start | bytes 442376 | tf_op jit(solution)/shard_map/ppermute | solution.py:210
  74.6 6.7 %collective-permute-done.4 = bf16[2,96,384]{2,1,0:T(8,128)(2,1)S(1)} collective-permute-done((bf16[2,96,384]{2,1,0:T(8,128)(2,1)S(1)}, bf16[2,96,384]{2,1,0:T(8,128)(2,1)S(1)}, u32[]{:S(2)}, u32[]{:S(2)}) %collective-permute-start.4) | collective-permute-done | bytes 147488 | tf_op jit(solution)/shard_map/ppermute | solution.py:210
  81.4 2.4 %collective-permute-start.5 = (bf16[6,96,384]{2,1,0:T(8,128)(2,1)S(1)}, bf16[6,96,384]{2,1,0:T(8,128)(2,1)}, u32[]{:S(2)}, u32[]{:S(2)}) collective-permute-start(bf16[6,96,384]{2,1,0:T(8,128)(2,1)S(1)} %constant_dynamic-update-slice_fusion.most_ref), channel_id=1, source_target_pairs={{0,1},{1,0},{2,3},{3,2},{4,5},{5,4},{6,7},{7,6},{8,9},{9,8},{10,11... | collective-permute-start | bytes 1327112 | tf_op jit(solution)/shard_map/ppermute | solution.py:227
  83.8 0.0 copy-done.8
  83.8 0.1 reshape_reshape.3
  83.9 0.1 broadcast_in_dim_reshape.5.label_b_ref
  84.0 0.0 copy-done.11
  84.0 0.1 dynamic_slice.15.own_energy_ref
  84.1 0.1 reshape.144
  84.2 0.0 copy-done.10
  84.2 0.4 select_reduce_fusion
  84.7 0.7 copy.29.energy_b_ref
  85.4 0.1 reshape.146.spread_label_b_ref
  85.6 0.0 collective-permute-done.5.core_most_ref
  85.6 0.0 all-to-all-done.2.got_ref
  85.6 0.0 copy-done
  85.6 0.0 copy-start.1
  85.6 0.9 copy-done.1
  86.5 0.9 copy-done.5
  87.4 0.9 copy-done.6
  88.3 10.6 %shard_map.104 = bf16[1600,1250]{1,0:T(8,128)(2,1)} custom-call(bf16[32,152,128]{2,1,0:T(8,128)(2,1)S(1)} %all-to-all-done.2.got_ref, bf16[4,480,128]{2,1,0:T(8,128)(2,1)S(1)} %copy-done, bf16[2,96,384]{2,1,0:T(8,128)(2,1)S(1)} %pad_maximum_fusion.pair_ref, bf16[2,96,384]{2,1,0:T(8,128)(2,1)S(1)} %copy-done.5, ...), custom_call_target="tpu_custom_call" | custom-call | tf_op jit(solution)/shard_map/pallas_call | solution.py:240
  (19 shorter events, 0.2 us)
Async XLA Ops:
  0.0 20.0 %copy-start.2 = (bf16[96,1250]{1,0:T(8,128)(2,1)S(1)}, bf16[96,1250]{1,0:T(8,128)(2,1)}, u32[]{:S(2)}) copy-start(bf16[96,1250]{1,0:T(8,128)(2,1)} %amp_ref.1) | copy-start | bytes 720004
  0.0 1.0 copy-start.3
  1.0 40.1 %copy-start.9 = (s32[1536]{0:T(1024)S(1)}, s32[1536]{0:T(1024)}, u32[]{:S(2)}) copy-start(s32[1536]{0:T(1024)} %param.14) | copy-start | bytes 18436
  2.0 44.8 %copy-start.7 = (bf16[128,128]{1,0:T(8,128)(2,1)S(1)}, bf16[128,128]{1,0:T(8,128)(2,1)}, u32[]{:S(2)}) copy-start(bf16[128,128]{1,0:T(8,128)(2,1)} %constant.65.clone.swap_ref) | copy-start | bytes 98308
  2.0 23.3 %all-to-all-start = ((bf16[32,24,128]{2,1,0:T(8,128)(2,1)}), bf16[32,24,128]{2,1,0:T(8,128)(2,1)S(1)}, u32[]{:S(2)}, u32[]{:S(2)}) async-start(bf16[32,24,128]{2,1,0:T(8,128)(2,1)} %shard_map.100), calls=%async_computation | async-start | bytes 393216 | tf_op jit(solution)/shard_map/all_to_all | solution.py:213
  26.5 20.3 %all-to-all-start.1 = ((bf16[16,48,128]{2,1,0:T(8,128)(2,1)}), bf16[16,48,128]{2,1,0:T(8,128)(2,1)S(1)}, u32[]{:S(2)}, u32[]{:S(2)}) async-start(bf16[16,48,128]{2,1,0:T(8,128)(2,1)} %shard_map.101.own_ref), calls=%async_computation.1 | async-start | bytes 393216 | tf_op jit(solution)/shard_map/all_to_all | solution.py:217
  36.5 8.1 %collective-permute-start = (bf16[1,96,384]{2,1,0:T(8,128)(2,1)S(1)}, bf16[1,96,384]{2,1,0:T(8,128)(2,1)S(1)}, u32[]{:S(2)}, u32[]{:S(2)}) collective-permute-start(bf16[1,96,384]{2,1,0:T(8,128)(2,1)S(1)} %get-tuple-element.16), channel_id=1, source_target_pairs={{0,14},{1,15},{2,0},{3,1},{4,2},{5,3},{6,4},{7,5},{8,6},{9,7},{10,... | collective-permute-start | bytes 221192 | tf_op jit(solution)/shard_map/ppermute | solution.py:210
  49.2 34.6 %copy-start.8 = (s32[2,80]{1,0:T(2,128)S(1)}, s32[2,80]{1,0:T(2,128)}, u32[]{:S(2)}) copy-start(s32[2,80]{1,0:T(2,128)} %param.12) | copy-start | bytes 1924
  49.2 34.9 %copy-start.11 = (f32[160]{0:T(256)S(1)}, f32[160]{0:T(256)}, u32[]{:S(2)}) copy-start(f32[160]{0:T(256)} %param.15) | copy-start | bytes 1924
  49.2 35.1 %copy-start.10 = (f32[200]{0:T(256)S(1)}, f32[200]{0:T(256)}, u32[]{:S(2)}) copy-start(f32[200]{0:T(256)} %param.16) | copy-start | bytes 2404
  49.2 36.4 %all-to-all-start.2 = ((bf16[32,152,128]{2,1,0:T(8,128)(2,1)}), bf16[32,152,128]{2,1,0:T(8,128)(2,1)S(1)}, u32[]{:S(2)}, u32[]{:S(2)}) async-start(bf16[32,152,128]{2,1,0:T(8,128)(2,1)} %shard_map.103), calls=%async_computation.2 | async-start | bytes 2490368 | tf_op jit(solution)/shard_map/all_to_all | solution.py:233
  53.3 32.3 %copy-start = (bf16[4,480,128]{2,1,0:T(8,128)(2,1)S(1)}, bf16[4,480,128]{2,1,0:T(8,128)(2,1)}, u32[]{:S(2)}) copy-start(bf16[4,480,128]{2,1,0:T(8,128)(2,1)} %constant.66.clone.turn_ref) | copy-start | bytes 1474564
  53.3 9.5 %collective-permute-start.3 = (bf16[2,96,384]{2,1,0:T(8,128)(2,1)S(1)}, bf16[2,96,384]{2,1,0:T(8,128)(2,1)S(1)}, u32[]{:S(2)}, u32[]{:S(2)}) collective-permute-start(bf16[2,96,384]{2,1,0:T(8,128)(2,1)S(1)} %pad_maximum_fusion.pair_ref), channel_id=1, source_target_pairs={{0,1},{1,0},{2,3},{3,2},{4,5},{5,4},{6,7},{7,6},{8,9},{9,8},{10,11... | collective-permute-start | bytes 442376 | tf_op jit(solution)/shard_map/ppermute | solution.py:227
  55.3 10.1 %collective-permute-start.2 = (bf16[2,96,384]{2,1,0:T(8,128)(2,1)S(1)}, bf16[2,96,384]{2,1,0:T(8,128)(2,1)S(1)}, u32[]{:S(2)}, u32[]{:S(2)}) collective-permute-start(bf16[2,96,384]{2,1,0:T(8,128)(2,1)S(1)} %pad_maximum_fusion.pair_ref), channel_id=1, source_target_pairs={{0,4},{1,5},{2,6},{3,7},{4,8},{5,9},{6,10},{7,11},{8,12},{9,13},{1... | collective-permute-start | bytes 442376 | tf_op jit(solution)/shard_map/ppermute | solution.py:210
  58.2 11.4 %collective-permute-start.1 = (bf16[2,96,384]{2,1,0:T(8,128)(2,1)S(1)}, bf16[2,96,384]{2,1,0:T(8,128)(2,1)S(1)}, u32[]{:S(2)}, u32[]{:S(2)}) collective-permute-start(bf16[2,96,384]{2,1,0:T(8,128)(2,1)S(1)} %pad_maximum_fusion.pair_ref), channel_id=1, source_target_pairs={{0,12},{1,13},{2,14},{3,15},{4,0},{5,1},{6,2},{7,3},{8,4},{9,5},{1... | collective-permute-start | bytes 442376 | tf_op jit(solution)/shard_map/ppermute | solution.py:210
  62.8 0.7 copy-start.4
  69.6 11.8 %collective-permute-start.4 = (bf16[2,96,384]{2,1,0:T(8,128)(2,1)S(1)}, bf16[2,96,384]{2,1,0:T(8,128)(2,1)S(1)}, u32[]{:S(2)}, u32[]{:S(2)}) collective-permute-start(bf16[2,96,384]{2,1,0:T(8,128)(2,1)S(1)} %collective-permute-done.1), channel_id=1, source_target_pairs={{0,12},{1,13},{2,14},{3,15},{4,0},{5,1},{6,2},{7,3},{8,4},{9,5},{1... | collective-permute-start | bytes 442376 | tf_op jit(solution)/shard_map/ppermute | solution.py:210
  81.4 4.2 %collective-permute-start.5 = (bf16[6,96,384]{2,1,0:T(8,128)(2,1)S(1)}, bf16[6,96,384]{2,1,0:T(8,128)(2,1)}, u32[]{:S(2)}, u32[]{:S(2)}) collective-permute-start(bf16[6,96,384]{2,1,0:T(8,128)(2,1)S(1)} %constant_dynamic-update-slice_fusion.most_ref), channel_id=1, source_target_pairs={{0,1},{1,0},{2,3},{3,2},{4,5},{5,4},{6,7},{7,6},{8,9},{9,8},{10,11... | collective-permute-start | bytes 1327112 | tf_op jit(solution)/shard_map/ppermute | solution.py:227
  85.6 0.9 copy-start.1
  86.5 0.9 copy-start.5
  87.4 0.9 copy-start.6

commit v6 on v3

--- a/solution.py
+++ b/solution.py
@@ -139,17 +139,19 @@
                 source = ((vir_ref[0] ^ core) + 2 * chip) & 15
                 amp_ref[pl.ds(pl.multiple_of(96 * source, 96), 96), :] = part[index]
 
-    for a in range(STEP):
-        label_a = own_label_ref[step * STEP + a]
-        for part in range(4):
-            wanted = label_cd_ref[:, 384 * part : 384 * part + 384] ^ label_a
+    total = jnp.zeros((STEP * 192, SLOTS), F32)
+    for part in range(4):
+        lanes = slice(384 * part, 384 * part + 384)
+        for a in range(STEP):
+            wanted = label_cd_ref[:, lanes] ^ own_label_ref[step * STEP + a]
             own = pl.ds(pl.multiple_of(48 * (step * STEP + a), 48), 48)
-            values = rows_ref[own, 384 * part : 384 * part + 384].astype(F32)
+            values = rows_ref[own, lanes].astype(F32)
             for quarter in range(4):
                 keep = spread_label_b_ref[48 * quarter : 48 * quarter + 48, :] == wanted
                 at = 192 * a + 48 * quarter
-                left_ref[at : at + 48, 384 * part : 384 * part + 384] = jnp.where(keep, values, 0.0).astype(BF16)
-    total = dot(left_ref[...], amp_ref[...]).astype(BF16)
+                left_ref[part, at : at + 48, :] = jnp.where(keep, values, 0.0).astype(BF16)
+        total = total + dot(left_ref[part], amp_ref[lanes, :])
+    total = total.astype(BF16)
     picked = [dot(pick_ref[...], total[192 * a : 192 * a + 192]).astype(BF16) for a in range(STEP)]
     ladder = dot(jnp.concatenate(picked, axis=0), place_ref[...])
     for a in range(STEP):
@@ -264,7 +266,7 @@
             pltpu.VMEM((480, CD), BF16),
             pltpu.VMEM((CD, SLOTS), BF16),
             pltpu.VMEM((SLOTS, PAIRS), BF16),
-            pltpu.VMEM((STEP * 192, CD), BF16),
+            pltpu.VMEM((4, STEP * 192, 384), BF16),
         ],
         compiler_params=params(),
     )(

time: 96.7 us -> 98.5 us (1.019)
  Pallas kernels: 15.7 us -> 17.5 us
    pallas_call x1, Pallas kernels: 10.5 us -> 12.3 us  [on_device(): pl.pallas_call(finish, grid=(OWN // STEP,), out_shape=jax.ShapeDtypeStruc...]
  transfers between devices with their start and end apart: 9 -> 9, of which waited for: 7 -> 7; matrix products, arithmetic and copies ran while one was open for 6% -> 5% of each run, Pallas kernels for 0% -> 0%
where the time goes in v6:
time: 98.5 us; the launch traced here: 97.7 us
  starting transfers between devices  47.6 us (48%)
  waiting for transfers between devices  26.1 us (26%)
  Pallas kernels  17.5 us (18%)
  local copies, waits for them, and re-layouts  4.69 us (5%)
  other arithmetic  1.63 us (2%)
    ppermute x4, starting transfers between devices, on_device(): lax.ppermute(array, 'vir', [(i, (i - 2 * k) % 16) for i in range(16)])  13.9 us
    all_to_all x1, starting transfers between devices, on_device(): lax.all_to_all(turned, 'occ', split_axis=0, concat_axis=0, tiled=True)  13.8 us
    ppermute x4, waiting for transfers between devices, on_device(): lax.ppermute(array, 'vir', [(i, (i - 2 * k) % 16) for i in range(16)])  13.6 us
    pallas_call x1, Pallas kernels, on_device(): pl.pallas_call(finish, grid=(OWN // STEP,), out_shape=jax.ShapeDtypeStruc...  12.3 us
    all_to_all x1, starting transfers between devices, on_device(): lax.all_to_all(blocks, 'vir', split_axis=0, concat_axis=0, tiled=True)  9.96 us
    ppermute x2, starting transfers between devices, on_device(): lax.ppermute(array, 'vir', [(i, i ^ 1) for i in range(16)])  5.81 us
    all_to_all x1, waiting for transfers between devices, on_device(): lax.all_to_all(copies, 'occ', split_axis=0, concat_axis=0, tiled=True)  5.19 us
    pallas_call x4, Pallas kernels, call(): pl.pallas_call(kernel, out_shape=shapes, in_specs=[VMEM] * len(args), out...  5.17 us
  transfers between devices with their start and end apart: 9, of which 7 were waited for; matrix products, arithmetic and copies ran while one was open for 5% of the time, Pallas kernels for 0%

profile of v6, /device:TPU:1, one launch (start us, length us, event | category | flops | bytes accessed | tf_op | source)
XLA Modules:
  0.0 97.7 jit_solution(16501624879754874345)
XLA Ops:
  0.0 0.0 copy-start.1
  0.0 0.0 copy-start.2
  0.0 1.0 copy-done.2
  1.0 0.0 copy-start.6
  1.0 1.1 %shard_map.100 = bf16[32,24,128]{2,1,0:T(8,128)(2,1)} custom-call(bf16[50,1536]{1,0:T(8,128)(2,1)S(1)} %copy-done.2), custom_call_target="tpu_custom_call" | custom-call | tf_op jit(solution)/shard_map/pallas_call | solution.py:31
  2.0 0.0 copy-start.4
  2.0 13.8 %all-to-all-start = ((bf16[32,24,128]{2,1,0:T(8,128)(2,1)}), bf16[32,24,128]{2,1,0:T(8,128)(2,1)S(1)}, u32[]{:S(2)}, u32[]{:S(2)}) async-start(bf16[32,24,128]{2,1,0:T(8,128)(2,1)} %shard_map.100), calls=%async_computation | async-start | bytes 393216 | tf_op jit(solution)/shard_map/all_to_all | solution.py:214
  15.9 1.1 %select_reduce_fusion.2 = (s32[1250]{0:T(1024)S(1)}, s32[1250]{0:T(1024)S(1)}) fusion(s32[1250]{0:T(1024)S(1)} %get-tuple-element.21, s32[200]{0:T(256)} %param.13, s32[1250]{0:T(1024)S(1)} %get-tuple-element.22), kind=kLoop, calls=%fused_computation.2 | loop fusion | flops 1497500 | bytes 20800 | tf_op jit(solution)/shard_map/reduce_sum | solution.py:42
  17.0 0.8 reshape.142
  17.8 0.8 xor.42
  18.6 0.1 dynamic_slice.13.own_label_ref
  18.6 0.1 xor.39
  18.7 0.1 xor.40
  18.8 0.1 copy.23
  18.9 0.8 dynamic-slice_bitcast_fusion.1
  19.7 0.1 copy.22.label_cd_ref
  19.8 0.1 copy.24
  19.9 0.1 fusion.5.slot_ref
  20.0 0.0 copy-done.1
  20.0 0.5 shard_map.102
  20.4 4.9 %all-to-all-done.got_ref = bf16[32,24,128]{2,1,0:T(8,128)(2,1)S(1)} async-done(((bf16[32,24,128]{2,1,0:T(8,128)(2,1)}), bf16[32,24,128]{2,1,0:T(8,128)(2,1)S(1)}, u32[]{:S(2)}, u32[]{:S(2)}) %all-to-all-start) | async-done | bytes 196640 | tf_op jit(solution)/shard_map/all_to_all | solution.py:214
  25.3 1.2 %shard_map.101.own_ref = bf16[16,48,128]{2,1,0:T(8,128)(2,1)} custom-call(bf16[32,24,128]{2,1,0:T(8,128)(2,1)S(1)} %all-to-all-done.got_ref), custom_call_target="tpu_custom_call" | custom-call | tf_op jit(solution)/shard_map/pallas_call | solution.py:31
  26.5 10.0 %all-to-all-start.1 = ((bf16[16,48,128]{2,1,0:T(8,128)(2,1)}), bf16[16,48,128]{2,1,0:T(8,128)(2,1)S(1)}, u32[]{:S(2)}, u32[]{:S(2)}) async-start(bf16[16,48,128]{2,1,0:T(8,128)(2,1)} %shard_map.101.own_ref), calls=%async_computation.1 | async-start | bytes 393216 | tf_op jit(solution)/shard_map/all_to_all | solution.py:218
  36.5 4.5 %collective-permute-start = (bf16[1,96,384]{2,1,0:T(8,128)(2,1)S(1)}, bf16[1,96,384]{2,1,0:T(8,128)(2,1)S(1)}, u32[]{:S(2)}, u32[]{:S(2)}) collective-permute-start(bf16[1,96,384]{2,1,0:T(8,128)(2,1)S(1)} %shard_map.102), channel_id=1, source_target_pairs={{0,14},{1,15},{2,0},{3,1},{4,2},{5,3},{6,4},{7,5},{8,6},{9,7},{10,... | collective-permute-start | bytes 221192 | tf_op jit(solution)/shard_map/ppermute | solution.py:211
  41.0 0.0 copy-done.6
  41.0 0.1 dynamic-slice_bitcast_fusion
  41.1 0.1 copy.25.label_cd_ref
  41.2 3.4 %collective-permute-done = bf16[1,96,384]{2,1,0:T(8,128)(2,1)S(1)} collective-permute-done((bf16[1,96,384]{2,1,0:T(8,128)(2,1)S(1)}, bf16[1,96,384]{2,1,0:T(8,128)(2,1)S(1)}, u32[]{:S(2)}, u32[]{:S(2)}) %collective-permute-start) | collective-permute-done | bytes 73760 | tf_op jit(solution)/shard_map/ppermute | solution.py:211
  44.7 2.2 %all-to-all-done.1.mirror_ref = bf16[16,48,128]{2,1,0:T(8,128)(2,1)S(1)} async-done(((bf16[16,48,128]{2,1,0:T(8,128)(2,1)}), bf16[16,48,128]{2,1,0:T(8,128)(2,1)S(1)}, u32[]{:S(2)}, u32[]{:S(2)}) %all-to-all-start.1) | async-done | bytes 196640 | tf_op jit(solution)/shard_map/all_to_all | solution.py:218
  46.8 0.0 copy-done.4
  46.8 2.4 %shard_map.103 = bf16[32,152,128]{2,1,0:T(8,128)(2,1)} custom-call(bf16[16,48,128]{2,1,0:T(8,128)(2,1)} %shard_map.101.own_ref, bf16[16,48,128]{2,1,0:T(8,128)(2,1)S(1)} %all-to-all-done.1.mirror_ref, bf16[128,128]{1,0:T(8,128)(2,1)S(1)} %copy-done.4, s32[16,128]{1,0:T(8,128)S(1)} %pad.8.label_ab_ref, s32[48,1]{1,0:T(8,128)S(1)} %copy.25.label_cd_ref), custom_call_target="tpu_custom_call" | custom-call | tf_op jit(solution)/shard_map/pallas_call | solution.py:31
  49.2 0.0 copy-start.5
  49.2 0.0 copy-start.8
  49.2 0.0 copy-start.7
  49.2 4.1 %all-to-all-start.2 = ((bf16[32,152,128]{2,1,0:T(8,128)(2,1)}), bf16[32,152,128]{2,1,0:T(8,128)(2,1)S(1)}, u32[]{:S(2)}, u32[]{:S(2)}) async-start(bf16[32,152,128]{2,1,0:T(8,128)(2,1)} %shard_map.103), calls=%async_computation.2 | async-start | bytes 2490368 | tf_op jit(solution)/shard_map/all_to_all | solution.py:233
  53.3 0.0 copy-start
  53.3 0.0 copy-start.3
  53.4 2.5 %collective-permute-start.1 = (bf16[2,96,384]{2,1,0:T(8,128)(2,1)S(1)}, bf16[2,96,384]{2,1,0:T(8,128)(2,1)S(1)}, u32[]{:S(2)}, u32[]{:S(2)}) collective-permute-start(bf16[2,96,384]{2,1,0:T(8,128)(2,1)S(1)} %pad_maximum_fusion), channel_id=1, source_target_pairs={{0,12},{1,13},{2,14},{3,15},{4,0},{5,1},{6,2},{7,3},{8,4},{9,5},{1... | collective-permute-start | bytes 442376 | tf_op jit(solution)/shard_map/ppermute | solution.py:211
  55.9 3.8 %collective-permute-start.2 = (bf16[2,96,384]{2,1,0:T(8,128)(2,1)S(1)}, bf16[2,96,384]{2,1,0:T(8,128)(2,1)S(1)}, u32[]{:S(2)}, u32[]{:S(2)}) collective-permute-start(bf16[2,96,384]{2,1,0:T(8,128)(2,1)S(1)} %pad_maximum_fusion), channel_id=1, source_target_pairs={{0,4},{1,5},{2,6},{3,7},{4,8},{5,9},{6,10},{7,11},{8,12},{9,13},{1... | collective-permute-start | bytes 442376 | tf_op jit(solution)/shard_map/ppermute | solution.py:211
  59.7 5.4 %collective-permute-done.1 = bf16[2,96,384]{2,1,0:T(8,128)(2,1)S(1)} collective-permute-done((bf16[2,96,384]{2,1,0:T(8,128)(2,1)S(1)}, bf16[2,96,384]{2,1,0:T(8,128)(2,1)S(1)}, u32[]{:S(2)}, u32[]{:S(2)}) %collective-permute-start.1) | collective-permute-done | bytes 147488 | tf_op jit(solution)/shard_map/ppermute | solution.py:211
  65.1 0.0 collective-permute-done.2
  65.2 3.1 %collective-permute-start.4 = (bf16[6,96,384]{2,1,0:T(8,128)(2,1)S(1)}, bf16[6,96,384]{2,1,0:T(8,128)(2,1)S(1)}, u32[]{:S(2)}, u32[]{:S(2)}) collective-permute-start(bf16[6,96,384]{2,1,0:T(8,128)(2,1)S(1)} %constant_dynamic-update-slice_fusion.six_ref), channel_id=1, source_target_pairs={{0,1},{1,0},{2,3},{3,2},{4,5},{5,4},{6,7},{7,6},{8,9},{9,8},{10,11... | collective-permute-start | bytes 1327112 | tf_op jit(solution)/shard_map/ppermute | solution.py:230
  68.2 3.1 %collective-permute-start.3 = (bf16[2,96,384]{2,1,0:T(8,128)(2,1)S(1)}, bf16[2,96,384]{2,1,0:T(8,128)(2,1)S(1)}, u32[]{:S(2)}, u32[]{:S(2)}) collective-permute-start(bf16[2,96,384]{2,1,0:T(8,128)(2,1)S(1)} %collective-permute-done.1), channel_id=1, source_target_pairs={{0,12},{1,13},{2,14},{3,15},{4,0},{5,1},{6,2},{7,3},{8,4},{9,5},{1... | collective-permute-start | bytes 442376 | tf_op jit(solution)/shard_map/ppermute | solution.py:211
  71.3 0.0 copy-done.5
  71.3 0.1 reshape_reshape.3
  71.4 0.1 broadcast_in_dim_reshape.5.label_b_ref
  71.6 0.0 copy-done.8
  71.6 0.1 dynamic_slice.15.own_energy_ref
  71.7 0.1 reshape.144
  71.8 4.7 %collective-permute-done.3.last_ref = bf16[2,96,384]{2,1,0:T(8,128)(2,1)S(1)} collective-permute-done((bf16[2,96,384]{2,1,0:T(8,128)(2,1)S(1)}, bf16[2,96,384]{2,1,0:T(8,128)(2,1)S(1)}, u32[]{:S(2)}, u32[]{:S(2)}) %collective-permute-start.3) | collective-permute-done | bytes 147488 | tf_op jit(solution)/shard_map/ppermute | solution.py:211
  76.5 0.0 collective-permute-done.4.core_six_ref
  76.5 2.7 %collective-permute-start.5 = (bf16[2,96,384]{2,1,0:T(8,128)(2,1)S(1)}, bf16[2,96,384]{2,1,0:T(8,128)(2,1)S(1)}, u32[]{:S(2)}, u32[]{:S(2)}) collective-permute-start(bf16[2,96,384]{2,1,0:T(8,128)(2,1)S(1)} %collective-permute-done.3.last_ref), channel_id=1, source_target_pairs={{0,1},{1,0},{2,3},{3,2},{4,5},{5,4},{6,7},{7,6},{8,9},{9,8},{10,11... | collective-permute-start | bytes 442376 | tf_op jit(solution)/shard_map/ppermute | solution.py:230
  79.3 0.0 copy-done.7
  79.3 0.4 select_reduce_fusion
  79.7 0.1 copy.29.energy_b_ref
  79.8 0.1 reshape.146.spread_label_b_ref
  80.0 0.3 collective-permute-done.5.core_last_ref
  80.2 5.2 %all-to-all-done.2.got_ref = bf16[32,152,128]{2,1,0:T(8,128)(2,1)S(1)} async-done(((bf16[32,152,128]{2,1,0:T(8,128)(2,1)}), bf16[32,152,128]{2,1,0:T(8,128)(2,1)S(1)}, u32[]{:S(2)}, u32[]{:S(2)}) %all-to-all-start.2) | async-done | bytes 1245216 | tf_op jit(solution)/shard_map/all_to_all | solution.py:233
  85.4 0.0 copy-done
  85.4 0.0 copy-done.3
  85.4 12.3 %shard_map.104 = bf16[1600,1250]{1,0:T(8,128)(2,1)} custom-call(bf16[32,152,128]{2,1,0:T(8,128)(2,1)S(1)} %all-to-all-done.2.got_ref, bf16[4,480,128]{2,1,0:T(8,128)(2,1)S(1)} %copy-done, bf16[6,96,384]{2,1,0:T(8,128)(2,1)S(1)} %constant_dynamic-update-slice_fusion.six_ref, bf16[6,96,384]{2,1,0:T(8,128)(2,1)S(1)} %collective-permute-done.4.core_six_ref, ...), custom_call_target="tpu_custom_call" | custom-call | tf_op jit(solution)/shard_map/pallas_call | solution.py:240
  (16 shorter events, 0.2 us)
Async XLA Ops:
  0.0 20.0 %copy-start.1 = (bf16[96,1250]{1,0:T(8,128)(2,1)S(1)}, bf16[96,1250]{1,0:T(8,128)(2,1)}, u32[]{:S(2)}) copy-start(bf16[96,1250]{1,0:T(8,128)(2,1)} %amp_ref.1) | copy-start | bytes 720004
  0.0 1.0 copy-start.2
  1.0 40.1 %copy-start.6 = (s32[1536]{0:T(1024)S(1)}, s32[1536]{0:T(1024)}, u32[]{:S(2)}) copy-start(s32[1536]{0:T(1024)} %param.14) | copy-start | bytes 18436
  2.0 44.8 %copy-start.4 = (bf16[128,128]{1,0:T(8,128)(2,1)S(1)}, bf16[128,128]{1,0:T(8,128)(2,1)}, u32[]{:S(2)}) copy-start(bf16[128,128]{1,0:T(8,128)(2,1)} %constant.65.clone.swap_ref) | copy-start | bytes 98308
  2.0 23.3 %all-to-all-start = ((bf16[32,24,128]{2,1,0:T(8,128)(2,1)}), bf16[32,24,128]{2,1,0:T(8,128)(2,1)S(1)}, u32[]{:S(2)}, u32[]{:S(2)}) async-start(bf16[32,24,128]{2,1,0:T(8,128)(2,1)} %shard_map.100), calls=%async_computation | async-start | bytes 393216 | tf_op jit(solution)/shard_map/all_to_all | solution.py:214
  26.5 20.3 %all-to-all-start.1 = ((bf16[16,48,128]{2,1,0:T(8,128)(2,1)}), bf16[16,48,128]{2,1,0:T(8,128)(2,1)S(1)}, u32[]{:S(2)}, u32[]{:S(2)}) async-start(bf16[16,48,128]{2,1,0:T(8,128)(2,1)} %shard_map.101.own_ref), calls=%async_computation.1 | async-start | bytes 393216 | tf_op jit(solution)/shard_map/all_to_all | solution.py:218
  36.5 8.1 %collective-permute-start = (bf16[1,96,384]{2,1,0:T(8,128)(2,1)S(1)}, bf16[1,96,384]{2,1,0:T(8,128)(2,1)S(1)}, u32[]{:S(2)}, u32[]{:S(2)}) collective-permute-start(bf16[1,96,384]{2,1,0:T(8,128)(2,1)S(1)} %shard_map.102), channel_id=1, source_target_pairs={{0,14},{1,15},{2,0},{3,1},{4,2},{5,3},{6,4},{7,5},{8,6},{9,7},{10,... | collective-permute-start | bytes 221192 | tf_op jit(solution)/shard_map/ppermute | solution.py:211
  49.2 22.1 %copy-start.5 = (s32[2,80]{1,0:T(2,128)S(1)}, s32[2,80]{1,0:T(2,128)}, u32[]{:S(2)}) copy-start(s32[2,80]{1,0:T(2,128)} %param.12) | copy-start | bytes 1924
  49.2 22.3 %copy-start.8 = (f32[160]{0:T(256)S(1)}, f32[160]{0:T(256)}, u32[]{:S(2)}) copy-start(f32[160]{0:T(256)} %param.15) | copy-start | bytes 1924
  49.2 30.0 %copy-start.7 = (f32[200]{0:T(256)S(1)}, f32[200]{0:T(256)}, u32[]{:S(2)}) copy-start(f32[200]{0:T(256)} %param.16) | copy-start | bytes 2404
  49.2 36.2 %all-to-all-start.2 = ((bf16[32,152,128]{2,1,0:T(8,128)(2,1)}), bf16[32,152,128]{2,1,0:T(8,128)(2,1)S(1)}, u32[]{:S(2)}, u32[]{:S(2)}) async-start(bf16[32,152,128]{2,1,0:T(8,128)(2,1)} %shard_map.103), calls=%async_computation.2 | async-start | bytes 2490368 | tf_op jit(solution)/shard_map/all_to_all | solution.py:233
  53.3 32.1 %copy-start = (bf16[4,480,128]{2,1,0:T(8,128)(2,1)S(1)}, bf16[4,480,128]{2,1,0:T(8,128)(2,1)}, u32[]{:S(2)}) copy-start(bf16[4,480,128]{2,1,0:T(8,128)(2,1)} %constant.66.clone.turn_ref) | copy-start | bytes 1474564
  53.3 32.1 %copy-start.3 = (bf16[160,192]{1,0:T(8,128)(2,1)S(1)}, bf16[160,192]{1,0:T(8,128)(2,1)}, u32[]{:S(2)}) copy-start(bf16[160,192]{1,0:T(8,128)(2,1)} %constant.67.clone.pick_ref) | copy-start | bytes 184324
  53.4 11.7 %collective-permute-start.1 = (bf16[2,96,384]{2,1,0:T(8,128)(2,1)S(1)}, bf16[2,96,384]{2,1,0:T(8,128)(2,1)S(1)}, u32[]{:S(2)}, u32[]{:S(2)}) collective-permute-start(bf16[2,96,384]{2,1,0:T(8,128)(2,1)S(1)} %pad_maximum_fusion), channel_id=1, source_target_pairs={{0,12},{1,13},{2,14},{3,15},{4,0},{5,1},{6,2},{7,3},{8,4},{9,5},{1... | collective-permute-start | bytes 442376 | tf_op jit(solution)/shard_map/ppermute | solution.py:211
  55.9 9.2 %collective-permute-start.2 = (bf16[2,96,384]{2,1,0:T(8,128)(2,1)S(1)}, bf16[2,96,384]{2,1,0:T(8,128)(2,1)S(1)}, u32[]{:S(2)}, u32[]{:S(2)}) collective-permute-start(bf16[2,96,384]{2,1,0:T(8,128)(2,1)S(1)} %pad_maximum_fusion), channel_id=1, source_target_pairs={{0,4},{1,5},{2,6},{3,7},{4,8},{5,9},{6,10},{7,11},{8,12},{9,13},{1... | collective-permute-start | bytes 442376 | tf_op jit(solution)/shard_map/ppermute | solution.py:211
  65.2 11.3 %collective-permute-start.4 = (bf16[6,96,384]{2,1,0:T(8,128)(2,1)S(1)}, bf16[6,96,384]{2,1,0:T(8,128)(2,1)S(1)}, u32[]{:S(2)}, u32[]{:S(2)}) collective-permute-start(bf16[6,96,384]{2,1,0:T(8,128)(2,1)S(1)} %constant_dynamic-update-slice_fusion.six_ref), channel_id=1, source_target_pairs={{0,1},{1,0},{2,3},{3,2},{4,5},{5,4},{6,7},{7,6},{8,9},{9,8},{10,11... | collective-permute-start | bytes 1327112 | tf_op jit(solution)/shard_map/ppermute | solution.py:230
  68.2 8.3 %collective-permute-start.3 = (bf16[2,96,384]{2,1,0:T(8,128)(2,1)S(1)}, bf16[2,96,384]{2,1,0:T(8,128)(2,1)S(1)}, u32[]{:S(2)}, u32[]{:S(2)}) collective-permute-start(bf16[2,96,384]{2,1,0:T(8,128)(2,1)S(1)} %collective-permute-done.1), channel_id=1, source_target_pairs={{0,12},{1,13},{2,14},{3,15},{4,0},{5,1},{6,2},{7,3},{8,4},{9,5},{1... | collective-permute-start | bytes 442376 | tf_op jit(solution)/shard_map/ppermute | solution.py:211
  76.5 3.7 %collective-permute-start.5 = (bf16[2,96,384]{2,1,0:T(8,128)(2,1)S(1)}, bf16[2,96,384]{2,1,0:T(8,128)(2,1)S(1)}, u32[]{:S(2)}, u32[]{:S(2)}) collective-permute-start(bf16[2,96,384]{2,1,0:T(8,128)(2,1)S(1)} %collective-permute-done.3.last_ref), channel_id=1, source_target_pairs={{0,1},{1,0},{2,3},{3,2},{4,5},{5,4},{6,7},{7,6},{8,9},{9,8},{10,11... | collective-permute-start | bytes 442376 | tf_op jit(solution)/shard_map/ppermute | solution.py:230
